TPU v7x, 512 devices: a whole 4x4x16 slice. The times are simulated.
512 devices in a mesh: site: 64 (over y_hi, z, core), probe: 8 (over y_lo, x).
Axes of the slice: x: 4, y: 4 (y_hi: 2, y_lo: 2; y = y_hi * 2 + y_lo), z: 16, core: 2. Of those that a mesh axis runs over, the one named last changes fastest.
Arguments:
- angles: float32 [128, 4, 256], P('site'), may hold values from -3.140625 to 3.140625
- coupling: float32 [128, 4, 256], P('site'), may hold values from 0.03 to 0.46, as said below
- thermal_noise: float32 [128, 4, 256], P('site'), may hold values from -6 to 6
- coefficients: float32 [5], replicated, may hold values from 0.3 to 1.5
- probes: bfloat16 [128, 4, 2, 512, 256], P('site', None, None, 'probe'), may hold values from -6 to 6
- hopping: bfloat16 [128, 4, 4, 256, 256], P('site'), as said below
- offsets: int32 [128, 4, 4], P('site'), may hold values from 1 to 7, as said below
Outputs:
- angle_next: float32 [128, 4, 256], P('site')
- spin_force: float32 [128, 4, 256], P('site')
Inputs may be any that keep to these rules, and one draw needn't show every extreme that they name: `offsets`: each tile names the four codes 1, 3, 5, 7 in some order; code o points to the tile o // 3 - 1 tile rows and o % 3 - 1 tile columns away. `hopping`: reciprocal tiles: the tile of code c at a tile is the transpose of the tile of code 8 - c at the tile it points to. `coupling`: positive couplings.
All inputs are finite; a program needn't handle non-finite values. Where the computation divides by a largest or mean magnitude, that divisor is 1e-20 or more.
Results may differ from a plain program's by a relative error of at most 0.0037.
Values may be sent and summed in bfloat16 or wider, within the bound.
No kernel may reach another device: no remote copies, remote signals or barrier semaphores. Data moves between devices by JAX's collectives and lax.ppermute only.
A program may use at most 64 MiB of HBM per device.

v0:
```python
import jax
import jax.numpy as jnp
from jax import lax
from jax.sharding import PartitionSpec as P

BAND = 8.0
STEP_MAX = 0.3
TWO_TEMP = 0.1


def extended(block, sides, width):
    for axis, dim in sides:
        count = lax.axis_size(axis)
        forward = [(i, i + 1) for i in range(count - 1)]
        forward.append((count - 1, 0))
        backward = [(target, source) for source, target in forward]
        low = lax.ppermute(
            lax.slice_in_dim(block, block.shape[dim] - width, None, axis=dim), axis, forward
        )
        high = lax.ppermute(lax.slice_in_dim(block, 0, width, axis=dim), axis, backward)
        block = jnp.concatenate([low, block, high], axis=dim)
    return block


def tile_sources(offsets):
    tile_rows = jnp.arange(offsets.shape[0], dtype=jnp.int32)[:, None, None]
    tile_cols = jnp.arange(offsets.shape[1], dtype=jnp.int32)[None, :, None]
    row_move = offsets // 3 - 1
    col_move = offsets % 3 - 1
    return (tile_rows + 1 + row_move) * offsets.shape[1] + jnp.mod(
        tile_cols + col_move, offsets.shape[1]
    )


def apply_hop(padded, hopping, sources):
    flattened = padded.reshape((-1,) + padded.shape[2:])
    picked = jnp.take(flattened, sources, axis=0)
    return jnp.einsum("abkopj,abkij->abopi", picked, hopping, preferred_element_type=jnp.float32)


def kondo_term(vectors, coupled_cos, coupled_sin):
    upper = vectors[:, :, 0]
    lower = vectors[:, :, 1]
    first_orb = coupled_cos[:, :, None, :] * upper + coupled_sin[:, :, None, :] * lower
    second_orb = coupled_sin[:, :, None, :] * upper - coupled_cos[:, :, None, :] * lower
    return jnp.stack([first_orb, second_orb], axis=2)


def chebyshev(probe_part, hopping, sources, coupled_cos, coupled_sin, coefficients, exchanger):
    start_vec = probe_part.astype(jnp.float32)
    previous = start_vec
    current = start_vec
    current_low = probe_part
    weighted = coefficients[0] * start_vec
    for level in range(coefficients.shape[0] - 1):
        padded = exchanger(current_low)
        product = apply_hop(padded, hopping, sources) + kondo_term(
            current, coupled_cos, coupled_sin
        )
        if level == 0:
            following = 2.0 * product
        else:
            following = 2.0 * product - previous
        weighted = weighted + (level + 2) * coefficients[level + 1] * following
        previous = current
        current = following
        current_low = following.astype(jnp.bfloat16)
    return weighted


def probe_contract(probe_part, weighted, cosines, sine_values):
    start_vec = probe_part.astype(jnp.float32)
    upper_r = start_vec[:, :, 0]
    lower_r = start_vec[:, :, 1]
    upper_w = weighted[:, :, 0]
    lower_w = weighted[:, :, 1]
    terms = -sine_values[:, :, None, :] * (upper_r * upper_w - lower_r * lower_w) + cosines[
        :, :, None, :
    ] * (upper_r * lower_w + lower_r * upper_w)
    return jnp.sum(terms, axis=2)


def local(angles, coupling, thermal_noise, coefficients, probes, hopping, offsets):
    cosines = jnp.cos(angles)
    sine_values = jnp.sin(angles)
    coupled_cos = coupling * cosines
    coupled_sin = coupling * sine_values
    sources = tile_sources(offsets)
    probe_total = lax.axis_size("probe") * probes.shape[3]

    def vector_rims(vectors_low):
        return extended(vectors_low, (("site", 0),), 1)

    weighted = chebyshev(
        probes, hopping, sources, coupled_cos, coupled_sin, coefficients, vector_rims
    )
    partial_value = probe_contract(probes, weighted, cosines, sine_values)
    summed = lax.psum(partial_value, "probe")
    spin_force = -BAND * coupling * summed / probe_total
    largest = lax.pmax(jnp.max(jnp.abs(spin_force)), "site")
    step_size = STEP_MAX / (largest + 1e-06)
    angle_next = angles + step_size * spin_force + jnp.sqrt(TWO_TEMP * step_size) * thermal_noise
    return (angle_next, spin_force)


def solution(mesh):
    in_specs = (
        P("site", None, None),
        P("site", None, None),
        P("site", None, None),
        P(),
        P("site", None, None, "probe", None),
        P("site", None, None, None, None),
        P("site", None, None),
    )
    out_specs = (P("site", None, None), P("site", None, None))
    return jax.shard_map(local, mesh=mesh, in_specs=in_specs, out_specs=out_specs, check_vma=False)
```

profile of v0, /device:TPU:1, one launch (start us, length us, event | category | flops | bytes accessed | tf_op | source)
XLA Modules:
  0.0 247.0 jit_solution(12286324772203556738)
XLA Ops:
  0.7 1.1 fusion.112
  1.8 0.0 copy-start.2
  1.8 5.1 %collective-permute-start = (bf16[1,4,2,64,256]{4,3,2,1,0:T(8,128)(2,1)S(1)}, bf16[1,4,2,64,256]{4,3,2,1,0:T(8,128)(2,1)S(1)}, u32[]{:S(2)}, u32[]{:S(2)}) collective-permute-start(bf16[1,4,2,64,256]{4,3,2,1,0:T(8,128)(2,1)S(1)} %get-tuple-element.25), channel_id=1, source_target_pairs={{0,8},{8,16},{16,24},{24,32},{32,40},{40,48},{48,56},{56,64},{64,7... | collective-permute-start | bytes 786440 | tf_op jit(solution)/shard_map/ppermute | solution.py:17
  6.8 5.8 %collective-permute-start.1 = (bf16[1,4,2,64,256]{4,3,2,1,0:T(8,128)(2,1)S(1)}, bf16[1,4,2,64,256]{4,3,2,1,0:T(8,128)(2,1)}, u32[]{:S(2)}, u32[]{:S(2)}) collective-permute-start(bf16[1,4,2,64,256]{4,3,2,1,0:T(8,128)(2,1)S(1)} %get-tuple-element.26), channel_id=1, source_target_pairs={{8,0},{16,8},{24,16},{32,24},{40,32},{48,40},{56,48},{64,56},{72,6... | collective-permute-start | bytes 786440 | tf_op jit(solution)/shard_map/ppermute | solution.py:20
  12.6 1.1 copy_convert_fusion
  13.9 0.1 compare_and_fusion
  13.9 0.1 reshape.89
  14.1 0.6 fusion.115
  17.2 0.9 multiply_add_fusion.2
  18.1 0.0 collective-permute-done
  18.1 0.0 collective-permute-done.1
  18.1 1.1 pad_maximum_fusion
  19.2 2.0 gather_fusion
  21.2 4.4 %broadcast_multiply_fusion = (f32[2,4,2,64,256]{4,3,2,1,0:T(8,128)S(1)}, bf16[2,4,2,64,256]{4,3,2,1,0:T(8,128)(2,1)S(1)}, f32[2,4,2,64,256]{4,3,2,1,0:T(8,128)S(1)}) fusion(bf16[2,4,4,256,256]{4,3,2,1,0:T(8,128)(2,1)} %param.14, bf16[2,4,4,2,64,256]{5,4,3,2,1,0:T(8,128)(2,1)} %bitcast.164, pred[2,4,4]{2,1,0:T(4,128)(4,1)S(1)} %get-tuple-element.7, ...), kind=kOutput, calls=%fused_computation.50 | convolution fusion | flops 538968064 | bytes 9961504 | tf_op jit(solution)/shard_map/abkopj,abkij->abopi/dot_general | solution.py:38
  25.6 1.9 collective-permute-start.2
  27.5 8.1 %collective-permute-start.3 = (bf16[1,4,2,64,256]{4,3,2,1,0:T(8,128)(2,1)S(1)}, bf16[1,4,2,64,256]{4,3,2,1,0:T(8,128)(2,1)S(1)}, u32[]{:S(2)}, u32[]{:S(2)}) collective-permute-start(bf16[1,4,2,64,256]{4,3,2,1,0:T(8,128)(2,1)S(1)} %get-tuple-element.24), channel_id=1, source_target_pairs={{8,0},{16,8},{24,16},{32,24},{40,32},{48,40},{56,48},{64,56},{72,6... | collective-permute-start | bytes 786440 | tf_op jit(solution)/shard_map/ppermute | solution.py:20
  35.6 1.1 multiply_add_fusion.1
  36.8 0.0 collective-permute-done.2
  36.8 0.0 collective-permute-done.3
  36.8 0.1 pad_maximum_fusion.2
  36.9 2.0 gather_fusion.1
  38.9 4.7 %fusion.116 = (bf16[2,4,2,64,256]{4,3,1,0,2:T(8,128)(2,1)S(1)}, f32[2,4,2,64,256]{4,3,1,0,2:T(8,128)S(1)}) fusion(bf16[2,4,2,64,256]{4,3,2,1,0:T(8,128)(2,1)} %param.13, f32[2,4,1,64,256]{4,3,1,0,2:T(8,128)} %get-tuple-element.12, f32[2,4,1,64,256]{4,3,1,0,2:T(8,128)} %get-tuple-element.11, bf16[2,4,4,256,256]{4,3,2,1,0:T(8,128)(2,1)} %param.14, ...), kind=kOutput, calls=%fused_computation.102 | convolution fusion | flops 539492352 | bytes 9437216 | tf_op jit(solution)/shard_map/abkopj,abkij->abopi/dot_general | solution.py:38
  43.7 1.9 collective-permute-start.4
  45.6 10.0 %collective-permute-start.5 = (bf16[1,4,2,64,256]{4,3,1,0,2:T(8,128)(2,1)S(1)}, bf16[1,4,2,64,256]{4,3,1,0,2:T(8,128)(2,1)S(1)}, u32[]{:S(2)}, u32[]{:S(2)}) collective-permute-start(bf16[1,4,2,64,256]{4,3,1,0,2:T(8,128)(2,1)S(1)} %get-tuple-element.22), channel_id=1, source_target_pairs={{8,0},{16,8},{24,16},{32,24},{40,32},{48,40},{56,48},{64,56},{72,6... | collective-permute-start | bytes 786440 | tf_op jit(solution)/shard_map/ppermute | solution.py:20
  55.6 1.1 multiply_add_fusion
  56.8 0.0 collective-permute-done.5
  56.8 0.1 pad_maximum_fusion.3
  56.9 2.0 gather_fusion.2
  58.9 4.6 %fusion.79 = f32[2,4,2,64,256]{4,3,1,0,2:T(8,128)S(1)} fusion(bf16[2,4,4,256,256]{4,3,2,1,0:T(8,128)(2,1)} %param.14, f32[2,4,1,64,256]{4,3,1,0,2:T(8,128)} %get-tuple-element.10, f32[2,4,1,64,256]{4,3,1,0,2:T(8,128)} %get-tuple-element.9, bf16[2,4,4,2,64,256]{5,4,3,2,1,0:T(8,128)(2,1)} %bitcast.167, pred[2,4,4]{2,1,0:T(4,128)(4,1)S(1)} %get-tuple-element.7), kind=kOutput, calls=%fused_computation.33 | convolution fusion | flops 538705920 | bytes 8388640 | tf_op jit(solution)/shard_map/abkopj,abkij->abopi/dot_general | solution.py:38
  63.5 0.0 copy-start.3
  63.5 0.2 fusion.108
  63.7 1.0 copy-done.1
  64.7 0.1 copy-done.3
  64.8 2.1 fusion.91
  67.0 0.9 fusion.99
  67.9 1.9 collective-permute-start.6
  69.8 10.2 %collective-permute-start.7 = (bf16[1,4,2,64,256]{4,3,2,1,0:T(8,128)(2,1)S(1)}, bf16[1,4,2,64,256]{4,3,2,1,0:T(8,128)(2,1)S(1)}, u32[]{:S(2)}, u32[]{:S(2)}) collective-permute-start(bf16[1,4,2,64,256]{4,3,2,1,0:T(8,128)(2,1)S(1)} %get-tuple-element.20), channel_id=1, source_target_pairs={{8,0},{16,8},{24,16},{32,24},{40,32},{48,40},{56,48},{64,56},{72,6... | collective-permute-start | bytes 786440 | tf_op jit(solution)/shard_map/ppermute | solution.py:20
  80.0 0.9 fusion.97
  80.9 0.3 collective-permute-done.7
  81.1 0.1 pad_maximum_fusion.4
  81.3 2.0 gather_fusion.3
  83.3 4.9 %fusion.84 = f32[2,4,2,64,256]{4,3,2,1,0:T(8,128)S(1)} fusion(bf16[2,4,4,256,256]{4,3,2,1,0:T(8,128)(2,1)} %param.14, bf16[2,4,4,2,64,256]{5,4,3,2,1,0:T(8,128)(2,1)} %bitcast.165, pred[2,4,4]{2,1,0:T(4,128)(4,1)S(1)} %get-tuple-element.7, f32[2,4,1,64,256]{4,3,2,1,0:T(8,128)} %fusion.97, f32[2,4,1,64,256]{4,3,2,1,0:T(8,128)} %fusion.99, ...), kind=kOutput, calls=%fused_computation.34 | convolution fusion | flops 539492352 | bytes 10485796 | tf_op jit(solution)/shard_map/abkopj,abkij->abopi/dot_general | solution.py:38
  88.2 0.0 copy-start.8
  88.2 0.3 fusion.95
  88.4 15.3 %psum.7 = f32[2,4,256]{2,1,0:T(4,128)S(1)} all-reduce(f32[2,4,256]{2,1,0:T(4,128)S(1)} %fusion.95), channel_id=1, replica_groups=mesh['site'=64,'probe'=8] {'probe'}, use_global_device_ids=true, to_apply=%region_1.3 | all-reduce | flops 2048 | bytes 16384 | tf_op jit(solution)/shard_map/psum | solution.py:98
  103.8 1.2 abs_reduce_fusion
  105.0 140.7 %pmax.7 = f32[]{:T(128)} all-reduce(f32[]{:T(128)} %get-tuple-element.3), channel_id=1, replica_groups=mesh['site'=64,'probe'=8] {'site'}, use_global_device_ids=true, to_apply=%region_3.5 | all-reduce | flops 1 | bytes 8 | tf_op jit(solution)/shard_map/pmax | solution.py:100
  246.4 0.6 multiply_add_fusion.3
  (24 shorter events, 0.2 us)
Async XLA Ops:
  0.6 13.2 %copy-start.6 = (f32[2,4,256]{2,1,0:T(4,128)S(1)}, f32[2,4,256]{2,1,0:T(4,128)}, u32[]{:S(2)}) copy-start(f32[2,4,256]{2,1,0:T(4,128)} %param.9) | copy-start | bytes 24580
  0.6 13.2 %copy-start.9 = (s32[2,4,4]{2,1,0:T(4,128)S(1)}, s32[2,4,4]{2,1,0:T(4,128)}, u32[]{:S(2)}) copy-start(s32[2,4,4]{2,1,0:T(4,128)} %param.15) | copy-start | bytes 388
  0.7 13.4 %copy-start.7 = (f32[5]{0:T(128)S(1)}, f32[5]{0:T(128)}, u32[]{:S(2)}) copy-start(f32[5]{0:T(128)} %param.12) | copy-start | bytes 64
  0.7 16.5 %copy-start.5 = (f32[2,4,256]{2,1,0:T(4,128)S(1)}, f32[2,4,256]{2,1,0:T(4,128)}, u32[]{:S(2)}) copy-start(f32[2,4,256]{2,1,0:T(4,128)} %param.10) | copy-start | bytes 24580
  1.8 16.4 %copy-start.2 = (bf16[2,4,2,64,256]{4,3,2,1,0:T(8,128)(2,1)S(1)}, bf16[2,4,2,64,256]{4,3,2,1,0:T(8,128)(2,1)}, u32[]{:S(2)}) copy-start(bf16[2,4,2,64,256]{4,3,2,1,0:T(8,128)(2,1)} %param.13) | copy-start | bytes 1572868
  1.8 16.3 %collective-permute-start = (bf16[1,4,2,64,256]{4,3,2,1,0:T(8,128)(2,1)S(1)}, bf16[1,4,2,64,256]{4,3,2,1,0:T(8,128)(2,1)S(1)}, u32[]{:S(2)}, u32[]{:S(2)}) collective-permute-start(bf16[1,4,2,64,256]{4,3,2,1,0:T(8,128)(2,1)S(1)} %get-tuple-element.25), channel_id=1, source_target_pairs={{0,8},{8,16},{16,24},{24,32},{32,40},{40,48},{48,56},{56,64},{64,7... | collective-permute-start | bytes 786440 | tf_op jit(solution)/shard_map/ppermute | solution.py:17
  6.8 11.3 %collective-permute-start.1 = (bf16[1,4,2,64,256]{4,3,2,1,0:T(8,128)(2,1)S(1)}, bf16[1,4,2,64,256]{4,3,2,1,0:T(8,128)(2,1)}, u32[]{:S(2)}, u32[]{:S(2)}) collective-permute-start(bf16[1,4,2,64,256]{4,3,2,1,0:T(8,128)(2,1)S(1)} %get-tuple-element.26), channel_id=1, source_target_pairs={{8,0},{16,8},{24,16},{32,24},{40,32},{48,40},{56,48},{64,56},{72,6... | collective-permute-start | bytes 786440 | tf_op jit(solution)/shard_map/ppermute | solution.py:20
  19.2 2.0 copy-start.4
  25.6 11.2 %collective-permute-start.2 = (bf16[1,4,2,64,256]{4,3,2,1,0:T(8,128)(2,1)S(1)}, bf16[1,4,2,64,256]{4,3,2,1,0:T(8,128)(2,1)S(1)}, u32[]{:S(2)}, u32[]{:S(2)}) collective-permute-start(bf16[1,4,2,64,256]{4,3,2,1,0:T(8,128)(2,1)S(1)} %get-tuple-element.23), channel_id=1, source_target_pairs={{0,8},{8,16},{16,24},{24,32},{32,40},{40,48},{48,56},{56,64},{64,7... | collective-permute-start | bytes 786440 | tf_op jit(solution)/shard_map/ppermute | solution.py:17
  27.5 9.2 %collective-permute-start.3 = (bf16[1,4,2,64,256]{4,3,2,1,0:T(8,128)(2,1)S(1)}, bf16[1,4,2,64,256]{4,3,2,1,0:T(8,128)(2,1)S(1)}, u32[]{:S(2)}, u32[]{:S(2)}) collective-permute-start(bf16[1,4,2,64,256]{4,3,2,1,0:T(8,128)(2,1)S(1)} %get-tuple-element.24), channel_id=1, source_target_pairs={{8,0},{16,8},{24,16},{32,24},{40,32},{48,40},{56,48},{64,56},{72,6... | collective-permute-start | bytes 786440 | tf_op jit(solution)/shard_map/ppermute | solution.py:20
  43.7 13.1 %copy-start = (f32[2,4,2,64,256]{4,3,1,0,2:T(8,128)}, f32[2,4,2,64,256]{4,3,1,0,2:T(8,128)S(1)}, u32[]{:S(2)}) copy-start(f32[2,4,2,64,256]{4,3,1,0,2:T(8,128)S(1)} %get-tuple-element.39) | copy-start | bytes 3145732
  43.7 13.0 %collective-permute-start.4 = (bf16[1,4,2,64,256]{4,3,1,0,2:T(8,128)(2,1)S(1)}, bf16[1,4,2,64,256]{4,3,1,0,2:T(8,128)(2,1)S(1)}, u32[]{:S(2)}, u32[]{:S(2)}) collective-permute-start(bf16[1,4,2,64,256]{4,3,1,0,2:T(8,128)(2,1)S(1)} %get-tuple-element.21), channel_id=1, source_target_pairs={{0,8},{8,16},{16,24},{24,32},{32,40},{40,48},{48,56},{56,64},{64,7... | collective-permute-start | bytes 786440 | tf_op jit(solution)/shard_map/ppermute | solution.py:17
  45.6 11.1 %collective-permute-start.5 = (bf16[1,4,2,64,256]{4,3,1,0,2:T(8,128)(2,1)S(1)}, bf16[1,4,2,64,256]{4,3,1,0,2:T(8,128)(2,1)S(1)}, u32[]{:S(2)}, u32[]{:S(2)}) collective-permute-start(bf16[1,4,2,64,256]{4,3,1,0,2:T(8,128)(2,1)S(1)} %get-tuple-element.22), channel_id=1, source_target_pairs={{8,0},{16,8},{24,16},{32,24},{40,32},{48,40},{56,48},{64,56},{72,6... | collective-permute-start | bytes 786440 | tf_op jit(solution)/shard_map/ppermute | solution.py:20
  63.5 1.2 copy-start.1
  63.5 1.3 copy-start.3
  67.9 13.0 %collective-permute-start.6 = (bf16[1,4,2,64,256]{4,3,2,1,0:T(8,128)(2,1)S(1)}, bf16[1,4,2,64,256]{4,3,2,1,0:T(8,128)(2,1)S(1)}, u32[]{:S(2)}, u32[]{:S(2)}) collective-permute-start(bf16[1,4,2,64,256]{4,3,2,1,0:T(8,128)(2,1)S(1)} %get-tuple-element.19), channel_id=1, source_target_pairs={{0,8},{8,16},{16,24},{24,32},{32,40},{40,48},{48,56},{56,64},{64,7... | collective-permute-start | bytes 786440 | tf_op jit(solution)/shard_map/ppermute | solution.py:17
  69.8 11.3 %collective-permute-start.7 = (bf16[1,4,2,64,256]{4,3,2,1,0:T(8,128)(2,1)S(1)}, bf16[1,4,2,64,256]{4,3,2,1,0:T(8,128)(2,1)S(1)}, u32[]{:S(2)}, u32[]{:S(2)}) collective-permute-start(bf16[1,4,2,64,256]{4,3,2,1,0:T(8,128)(2,1)S(1)} %get-tuple-element.20), channel_id=1, source_target_pairs={{8,0},{16,8},{24,16},{32,24},{40,32},{48,40},{56,48},{64,56},{72,6... | collective-permute-start | bytes 786440 | tf_op jit(solution)/shard_map/ppermute | solution.py:20
  88.2 158.3 %copy-start.8 = (f32[2,4,256]{2,1,0:T(4,128)S(1)}, f32[2,4,256]{2,1,0:T(4,128)}, u32[]{:S(2)}) copy-start(f32[2,4,256]{2,1,0:T(4,128)} %param.11) | copy-start | bytes 24580
where the time goes:
time: 248 us; the launch traced here: 247 us
  blocking collectives  156 us (63%)
  starting transfers between devices  44.8 us (18%)
  matrix products  18.5 us (7%)
  other arithmetic  12 us (5%)
  local copies, waits for them, and re-layouts  11.2 us (5%)
  between operations  4.17 us (2%)
    pmax x1, blocking collectives, local(): largest = lax.pmax(jnp.max(jnp.abs(spin_force)), 'site')  141 us
    ppermute x4, starting transfers between devices, extended(): lax.ppermute(lax.slice_in_dim(block, 0, width, axis=dim), axis, backward)  34 us
    dot_general x4, matrix products, apply_hop(): jnp.einsum('abkopj,abkij->abopi', picked, hopping, preferred_element_type...  18.5 us
    psum x1, blocking collectives, local(): summed = lax.psum(partial_value, 'probe')  15.3 us
    ppermute x4, starting transfers between devices, extended(): lax.ppermute(lax.slice_in_dim(block, block.shape[dim] - width, None, axis...  10.8 us
    gather x4, local copies, waits for them, and re-layouts, apply_hop(): picked = jnp.take(flattened, sources, axis=0)  8.03 us
  transfers between devices with their start and end apart: 8, of which 1 were waited for; matrix products, arithmetic and copies ran while one was open for 2% of the time, Pallas kernels for 0%

commit v1 on v0

v1 whole, which is shorter than its diff:
```python
import functools
import jax
import jax.numpy as jnp
from jax import lax
from jax.experimental import pallas as pl
from jax.experimental.pallas import tpu as pltpu
from jax.sharding import PartitionSpec as P

BAND = 8.0
STEP_MAX = 0.3
TWO_TEMP = 0.1

VERT, LEFT, RIGHT, RIM = range(4)
IN_VMEM = pl.BlockSpec(memory_space=pltpu.VMEM)
IN_SMEM = pl.BlockSpec(memory_space=pltpu.SMEM)
IN_HBM = pl.BlockSpec(memory_space=pltpu.HBM)


def held(array, space=pltpu.VMEM):
    return pltpu.with_memory_space_constraint(array, space)


def call(body, outs, in_specs, args, scratch=(), flops=0, moved=0):
    return pl.pallas_call(
        body,
        out_shape=[pltpu.VMEM(shape, dtype) for shape, dtype in outs],
        in_specs=in_specs,
        out_specs=[IN_VMEM] * len(outs),
        scratch_shapes=list(scratch),
        compiler_params=pltpu.CompilerParams(vmem_limit_bytes=16 * 1024 * 1024),
        cost_estimate=pl.CostEstimate(flops=flops, bytes_accessed=moved, transcendentals=0),
    )(*args)


def product(vectors, matrix):
    return jnp.dot(vectors, matrix, preferred_element_type=jnp.float32)


def folded(values):
    return jnp.sum(values.reshape(-1, 8, values.shape[-1]), axis=0)


def overlap_terms(probe, vectors):
    half = probe.shape[0] // 2
    upper_r = probe[:half].astype(jnp.float32)
    lower_r = probe[half:].astype(jnp.float32)
    upper_w, lower_w = vectors[:half], vectors[half:]
    same = folded(upper_r * upper_w - lower_r * lower_w)
    cross = folded(upper_r * lower_w + lower_r * upper_w)
    return same, cross


def split_body(parity_ref, probes_ref, outer_ref, inner_ref, sems):
    parity = parity_ref[0]
    copies = [
        pltpu.make_async_copy(probes_ref.at[parity], outer_ref, sems.at[0]),
        pltpu.make_async_copy(probes_ref.at[1 - parity], inner_ref, sems.at[1]),
    ]
    for copy in copies:
        copy.start()
    for copy in copies:
        copy.wait()


def local_hop(cols, rows, outer_ref, inner_ref, tile, matrix):
    refs = (outer_ref, inner_ref)
    row, col = divmod(tile, cols)

    def vectors(r, c):
        return refs[r][pl.ds(c * rows, rows), :]

    right, left = (col + 1) % cols, (col - 1) % cols
    total = product(vectors(1 - row, col), matrix(VERT, (1 - row) * cols + col))
    total += product(vectors(row, right), matrix(LEFT, row * cols + right))
    total += product(vectors(row, left), matrix(RIGHT, row * cols + left))
    return total


def kondo(vectors, twice_cos, twice_sin):
    half = vectors.shape[0] // 2
    upper, lower = vectors[:half], vectors[half:]
    return jnp.concatenate(
        [twice_cos * upper + twice_sin * lower, twice_sin * upper - twice_cos * lower], axis=0
    )


def first_body(cols, rows, parity_ref, offsets_ref, coef_ref, hopping_ref, outer_ref, inner_ref,
               cos_ref, sin_ref, sorted_ref, part_ref, terms_ref, rims_ref, sems):
    tiles = 2 * cols
    slots = hopping_ref.shape[0] // tiles
    parity = parity_ref[0]

    def fetch(kind, tile):
        row, col = divmod(tile, cols)
        origin = (row + parity - 2 * row * parity) * cols + col
        if kind == LEFT:
            code = 3
        elif kind == RIGHT:
            code = 5
        else:
            towards_high = (row == 0) == (kind == VERT)
            code = 7 - 6 * parity if towards_high else 1 + 6 * parity
        slot = jnp.int32(0)
        for k in range(1, slots):
            slot += jnp.where(offsets_ref[origin * slots + k] == code, k, 0)
        place = kind * tiles + tile
        target = rims_ref.at[tile] if kind == RIM else sorted_ref.at[place]
        return pltpu.make_async_copy(
            hopping_ref.at[origin * slots + slot], target, sems.at[place]
        )

    order = [(kind, tile) for kind in range(4) for tile in range(tiles)]
    copies = [fetch(kind, tile) for kind, tile in order]
    for copy in copies:
        copy.start()
    weight = coef_ref[0]
    for tile in range(tiles):
        row, col = divmod(tile, cols)
        probe = (outer_ref, inner_ref)[row][pl.ds(col * rows, rows), :]
        same, cross = overlap_terms(probe, probe.astype(jnp.float32))
        terms_ref[tile] = weight * same
        terms_ref[tiles + tile] = weight * cross
    for copy in copies:
        copy.wait()
    for tile in range(tiles):
        row, col = divmod(tile, cols)
        probe = (outer_ref, inner_ref)[row][pl.ds(col * rows, rows), :].astype(jnp.float32)
        total = local_hop(
            cols, rows, outer_ref, inner_ref, tile, lambda kind, t: sorted_ref[kind * tiles + t]
        )
        part_ref[tile] = 2.0 * total + kondo(
            probe, cos_ref[pl.ds(tile, 1), :], sin_ref[pl.ds(tile, 1), :]
        )
        sorted_ref[RIM * tiles + tile] = rims_ref[tile].T


def rim_body(cols, rows, rim_outer_ref, rim_inner_ref, sorted_ref, part_ref,
             field_ref, outer_ref, inner_ref):
    tiles = 2 * cols
    for tile in range(tiles):
        row, col = divmod(tile, cols)
        rim = (rim_outer_ref, rim_inner_ref)[row][pl.ds(col * rows, rows), :]
        field = part_ref[tile] + 2.0 * product(rim, sorted_ref[RIM * tiles + tile])
        field_ref[tile] = field
        (outer_ref, inner_ref)[row][pl.ds(col * rows, rows), :] = field.astype(jnp.bfloat16)


def local_body(cols, rows, level, last, coef_ref, probe_outer_ref, probe_inner_ref, field_ref,
               outer_ref, inner_ref, *rest):
    tiles = 2 * cols
    previous_ref = None
    if level > 1:
        previous_ref, *rest = rest
    sorted_ref, cos_ref, sin_ref, terms_ref = rest[:4]
    outs = rest[4:]
    weight = (level + 1) * coef_ref[level]
    weight_next = (level + 2) * coef_ref[level + 1]
    for tile in range(tiles):
        row, col = divmod(tile, cols)
        place = pl.ds(col * rows, rows)
        probe = (probe_outer_ref, probe_inner_ref)[row][place, :]
        field = field_ref[tile]
        total = local_hop(
            cols, rows, outer_ref, inner_ref, tile, lambda kind, t: sorted_ref[kind * tiles + t]
        )
        following = 2.0 * total + kondo(
            field, cos_ref[pl.ds(tile, 1), :], sin_ref[pl.ds(tile, 1), :]
        )
        if previous_ref is None:
            following -= probe.astype(jnp.float32)
        else:
            following -= previous_ref[tile]
        if last:
            same, cross = overlap_terms(probe, weight * field + weight_next * following)
        else:
            same, cross = overlap_terms(probe, field)
            same, cross = weight * same, weight * cross
            outs[1][tile] = following
        outs[0][tile] = terms_ref[tile] + same
        outs[0][tiles + tile] = terms_ref[tiles + tile] + cross


def last_body(cols, rows, level, coef_ref, probe_outer_ref, probe_inner_ref, rim_outer_ref,
              rim_inner_ref, sorted_ref, terms_ref, same_ref, cross_ref, out_ref):
    tiles = 2 * cols
    weight = 2.0 * (level + 1) * coef_ref[level]
    for tile in range(tiles):
        row, col = divmod(tile, cols)
        place = pl.ds(col * rows, rows)
        probe = (probe_outer_ref, probe_inner_ref)[row][place, :]
        rim = (rim_outer_ref, rim_inner_ref)[row][place, :]
        same, cross = overlap_terms(probe, product(rim, sorted_ref[RIM * tiles + tile]))
        same = jnp.sum(terms_ref[tile] + weight * same, axis=0, keepdims=True)
        cross = jnp.sum(terms_ref[tiles + tile] + weight * cross, axis=0, keepdims=True)
        share = same_ref[pl.ds(tile, 1), :] * same + cross_ref[pl.ds(tile, 1), :] * cross
        for peer in range(out_ref.shape[0]):
            out_ref[peer, pl.ds(tile, 1), :] = share


def force_body(shares_ref, force_ref, largest_ref):
    force = shares_ref[0]
    for peer in range(1, shares_ref.shape[0]):
        force += shares_ref[peer]
    force_ref[...] = force
    largest_ref[...] = jnp.full(largest_ref.shape, jnp.max(jnp.abs(force)), jnp.float32)


def move_body(parity_ref, largest_ref, force_ref, angles_ref, noise_ref, next_ref, out_ref):
    parity = parity_ref[0]
    cols = out_ref.shape[1]
    largest = jnp.max(largest_ref[...])
    step_size = jnp.full((1, 1), STEP_MAX, jnp.float32) / (largest + 1e-06)
    kick = jnp.sqrt(TWO_TEMP * step_size)
    for row in range(2):
        origin = row + parity - 2 * row * parity
        force = force_ref[pl.ds(row * cols, cols), :]
        out_ref[origin] = force
        next_ref[origin] = angles_ref[origin] + step_size * force + kick * noise_ref[origin]


def exchange(outer, inner):
    count = lax.axis_size("site")
    across = [(i, (i + 1) % count if i % 2 else (i - 1) % count) for i in range(count)]
    within = [(i, i ^ 1) for i in range(count)]
    return lax.ppermute(outer, "site", across), lax.ppermute(inner, "site", within)


def local(angles, coupling, thermal_noise, coefficients, probes, hopping, offsets):
    cols, orbitals, share, width = probes.shape[1:]
    rows = orbitals * share
    tiles = 2 * cols
    steps = coefficients.shape[0] - 1
    f32, bf16 = jnp.float32, jnp.bfloat16
    side = ((cols * rows, width), bf16)
    whole = ((tiles, rows, width), f32)
    terms_like = ((2 * tiles, 8, width), f32)
    probe_total = lax.axis_size("probe") * share

    parity = (lax.axis_index("site") % 2).astype(jnp.int32).reshape(1)
    outer, inner = call(
        split_body, [side, side], [IN_SMEM, IN_HBM],
        (parity, held(probes.reshape(2, cols * rows, width), pltpu.HBM)),
        scratch=[pltpu.SemaphoreType.DMA((2,))],
    )
    probe_outer, probe_inner = outer, inner
    rims = exchange(outer, inner)

    def ordered(array):
        return jnp.where(parity[0] == 0, array, array[::-1]).reshape(tiles, width)

    cosines, sine_values = ordered(jnp.cos(angles)), ordered(jnp.sin(angles))
    strength = ordered(coupling)
    twice_cos = 2.0 * strength * cosines
    twice_sin = 2.0 * strength * sine_values
    scale = (-BAND / probe_total) * strength
    same_factor = -scale * sine_values
    cross_factor = scale * cosines

    sorted_hop, part, terms = call(
        functools.partial(first_body, cols, rows),
        [((4 * tiles, width, width), bf16), whole, terms_like],
        [IN_SMEM, IN_SMEM, IN_SMEM, IN_HBM] + [IN_VMEM] * 4,
        (parity, offsets.reshape(-1), coefficients,
         held(hopping.reshape(-1, width, width), pltpu.HBM),
         held(outer), held(inner), held(twice_cos), held(twice_sin)),
        scratch=[pltpu.VMEM((tiles, width, width), bf16), pltpu.SemaphoreType.DMA((4 * tiles,))],
        flops=2 * 3 * tiles * rows * width * width, moved=hopping.size * 2,
    )
    field = previous = None
    for level in range(1, steps):
        previous, (field, outer, inner) = field, call(
            functools.partial(rim_body, cols, rows),
            [whole, side, side],
            [IN_VMEM] * 4,
            tuple(held(x) for x in (*rims, sorted_hop, part)),
            flops=2 * tiles * rows * width * width,
        )
        rims = exchange(outer, inner)
        last = level == steps - 1
        args = [probe_outer, probe_inner, field, outer, inner]
        if level > 1:
            args.append(previous)
        args += [sorted_hop, twice_cos, twice_sin, terms]
        terms, *rest = call(
            functools.partial(local_body, cols, rows, level, last),
            [terms_like] if last else [terms_like, whole],
            [IN_SMEM] + [IN_VMEM] * len(args),
            (coefficients, *(held(x) for x in args)),
            flops=2 * 3 * tiles * rows * width * width, moved=hopping.size * 2,
        )
        if not last:
            part = rest[0]

    peers = lax.axis_size("probe")
    shares = call(
        functools.partial(last_body, cols, rows, steps),
        [((peers, tiles, width), f32)],
        [IN_SMEM] + [IN_VMEM] * 8,
        (coefficients, *(held(x) for x in (
            probe_outer, probe_inner, *rims, sorted_hop, terms, same_factor, cross_factor))),
        flops=2 * tiles * rows * width * width,
    )[0]
    shares = lax.all_to_all(shares, "probe", 0, 0)
    force, largest = call(
        force_body,
        [((tiles, width), f32), ((lax.axis_size("site"), 1, 128), f32)],
        [IN_VMEM], (held(shares),),
    )
    largest = lax.all_to_all(largest, "site", 0, 0)
    return pl.pallas_call(
        move_body,
        out_shape=[jax.ShapeDtypeStruct(angles.shape, f32)] * 2,
        in_specs=[IN_SMEM] + [IN_VMEM] * 4,
        out_specs=[IN_VMEM] * 2,
    )(parity, held(largest), held(force), held(angles), held(thermal_noise))


def solution(mesh):
    in_specs = (
        P("site", None, None),
        P("site", None, None),
        P("site", None, None),
        P(),
        P("site", None, None, "probe", None),
        P("site", None, None, None, None),
        P("site", None, None),
    )
    out_specs = (P("site", None, None), P("site", None, None))
    return jax.shard_map(local, mesh=mesh, in_specs=in_specs, out_specs=out_specs, check_vma=False)
```

time: 248 us -> 91.8 us (0.37)
  blocking collectives: 156 us -> 33.7 us
  matrix products: 18.5 us -> 0 us
  Pallas kernels: 0 us -> 11.8 us
  other arithmetic: 12 us -> 0.8 us
  local copies, waits for them, and re-layouts: 11.2 us -> 2.22 us
  starting transfers between devices: 44.8 us -> 40.3 us
  between operations: 4.17 us -> 0.89 us
    pmax x1 -> x0, blocking collectives: 141 us -> none  [local(): largest = lax.pmax(jnp.max(jnp.abs(spin_force)), 'site')]
    all_to_all x0 -> x2, blocking collectives: none -> 33.7 us  [the longest x1 24.5 us: local(): largest = lax.all_to_all(largest, 'site', 0, 0)]
    dot_general x4 -> x0, matrix products: 18.5 us -> none  [apply_hop(): jnp.einsum('abkopj,abkij->abopi', picked, hopping, preferred_element_type...]
    psum x1 -> x0, blocking collectives: 15.3 us -> none  [local(): summed = lax.psum(partial_value, 'probe')]
    pallas_call x0 -> x11, Pallas kernels: none -> 11.8 us  [the longest x10 11.1 us: call(): pl.pallas_call(body, out_shape=[pltpu.VMEM(shape, dtype) for shape, dtype...]
    gather x4 -> x0, local copies, waits for them, and re-layouts: 8.03 us -> none  [apply_hop(): picked = jnp.take(flattened, sources, axis=0)]
    add x7 -> x0, other arithmetic: 6.82 us -> none  [the longest x4 4.07 us: kondo_term(): coupled_cos[:, :, None, :] * upper + coupled_sin[:, :, None, :] * lower]
    ppermute x8, starting transfers between devices: 44.8 us -> 40.3 us  [the longest x4 29.6 us: exchange(): lax.ppermute(inner, 'site', within)]
  transfers between devices with their start and end apart: 8 -> 8, of which waited for: 1 -> 1; matrix products, arithmetic and copies ran while one was open for 2% -> 3% of each run, Pallas kernels for 0% -> 9%
where the time goes in v1:
time: 91.8 us; the launch traced here: 91.2 us
  starting transfers between devices  40.3 us (44%)
  blocking collectives  33.7 us (37%)
  Pallas kernels  11.8 us (13%)
  local copies, waits for them, and re-layouts  2.22 us (2%)
  waiting for transfers between devices  1.41 us (2%)
    ppermute x4, starting transfers between devices, exchange(): lax.ppermute(inner, 'site', within)  29.6 us
    all_to_all x1, blocking collectives, local(): largest = lax.all_to_all(largest, 'site', 0, 0)  24.5 us
    pallas_call x10, Pallas kernels, call(): pl.pallas_call(body, out_shape=[pltpu.VMEM(shape, dtype) for shape, dtype...  11.1 us
    ppermute x4, starting transfers between devices, exchange(): lax.ppermute(outer, 'site', across)  10.7 us
    all_to_all x1, blocking collectives, local(): shares = lax.all_to_all(shares, 'probe', 0, 0)  9.14 us
  transfers between devices with their start and end apart: 8, of which 1 were waited for; matrix products, arithmetic and copies ran while one was open for 3% of the time, Pallas kernels for 9%

profile of v1, /device:TPU:1, one launch (start us, length us, event | category | flops | bytes accessed | tf_op | source)
XLA Modules:
  0.0 91.2 jit_solution(11513712748358095024)
XLA Ops:
  0.6 1.1 %shard_map.86 = (bf16[512,256]{1,0:T(8,128)(2,1)S(1)}, bf16[512,256]{1,0:T(8,128)(2,1)S(1)}) custom-call(s32[1]{0:T(128)} %bitcast.parity_ref, bf16[2,512,256]{2,1,0:T(8,128)(2,1)} %bitcast.8), custom_call_target="tpu_custom_call" | custom-call | tf_op jit(solution)/shard_map/pallas_call | solution.py:24
  1.7 4.9 %collective-permute-start = (bf16[512,256]{1,0:T(8,128)(2,1)S(1)}, bf16[512,256]{1,0:T(8,128)(2,1)S(1)}, u32[]{:S(2)}, u32[]{:S(2)}) collective-permute-start(bf16[512,256]{1,0:T(8,128)(2,1)S(1)} %get-tuple-element.22.outer_ref.probe_outer_ref), channel_id=1, source_target_pairs={{0,504},{8,16},{16,8},{24,32},{32,24},{40,48},{48,40},{56,64},{64,... | collective-permute-start | bytes 786440 | tf_op jit(solution)/shard_map/ppermute | solution.py:225
  6.6 11.9 %collective-permute-start.1 = (bf16[512,256]{1,0:T(8,128)(2,1)S(1)}, bf16[512,256]{1,0:T(8,128)(2,1)S(1)}, u32[]{:S(2)}, u32[]{:S(2)}) collective-permute-start(bf16[512,256]{1,0:T(8,128)(2,1)S(1)} %get-tuple-element.23.inner_ref.probe_inner_ref), channel_id=1, source_target_pairs={{0,8},{8,0},{16,24},{24,16},{32,40},{40,32},{48,56},{56,48},{64,72... | collective-permute-start | bytes 786440 | tf_op jit(solution)/shard_map/ppermute | solution.py:225
  18.6 0.8 reshape.29.offsets_ref
  19.4 0.8 fusion
  20.2 0.7 fusion.3
  21.0 0.0 copy-start.1
  21.0 0.6 copy-done.1
  21.6 3.8 %shard_map.87 = (bf16[32,256,256]{2,1,0:T(8,128)(2,1)S(1)}, f32[8,128,256]{2,1,0:T(8,128)S(1)}, f32[16,8,256]{2,1,0:T(8,128)S(1)}) custom-call(s32[1]{0:T(128)} %bitcast.parity_ref, s32[32]{0:T(128)S(1)} %reshape.29.offsets_ref, f32[5]{0:T(128)S(1)} %copy-done.1, bf16[32,256,256]{2,1,0:T(8,128)(2,1)} %bitcast.7, ...), custom_call_target="tpu_custom_call" | custom-call | flops 402653184 | bytes 4194304 | tf_op jit(solution)/shard_map/pallas_call | solution.py:24
  25.5 0.0 collective-permute-done.rim_outer_ref
  25.5 0.0 collective-permute-done.1.rim_inner_ref
  25.5 0.3 shard_map.88
  25.9 1.9 %collective-permute-start.2 = (bf16[512,256]{1,0:T(8,128)(2,1)S(1)}, bf16[512,256]{1,0:T(8,128)(2,1)S(1)}, u32[]{:S(2)}, u32[]{:S(2)}) collective-permute-start(bf16[512,256]{1,0:T(8,128)(2,1)S(1)} %get-tuple-element.26.outer_ref), channel_id=1, source_target_pairs={{0,504},{8,16},{16,8},{24,32},{32,24},{40,48},{48,40},{56,64},{64,... | collective-permute-start | bytes 786440 | tf_op jit(solution)/shard_map/ppermute | solution.py:225
  27.8 3.0 %collective-permute-start.3 = (bf16[512,256]{1,0:T(8,128)(2,1)S(1)}, bf16[512,256]{1,0:T(8,128)(2,1)S(1)}, u32[]{:S(2)}, u32[]{:S(2)}) collective-permute-start(bf16[512,256]{1,0:T(8,128)(2,1)S(1)} %get-tuple-element.27.inner_ref), channel_id=1, source_target_pairs={{0,8},{8,0},{16,24},{24,16},{32,40},{40,32},{48,56},{56,48},{64,72... | collective-permute-start | bytes 786440 | tf_op jit(solution)/shard_map/ppermute | solution.py:225
  30.8 1.3 %shard_map.89 = (f32[16,8,256]{2,1,0:T(8,128)S(1)}, f32[8,128,256]{2,1,0:T(8,128)S(1)}) custom-call(f32[5]{0:T(128)S(1)} %copy-done.1, bf16[512,256]{1,0:T(8,128)(2,1)S(1)} %get-tuple-element.22.outer_ref.probe_outer_ref, bf16[512,256]{1,0:T(8,128)(2,1)S(1)} %get-tuple-element.23.inner_ref.probe_inner_ref, ...), custom_call_target="tpu_custom_call" | custom-call | flops 402653184 | bytes 4194304 | tf_op jit(solution)/shard_map/pallas_call | solution.py:24
  32.2 1.4 %collective-permute-done.2.rim_outer_ref = bf16[512,256]{1,0:T(8,128)(2,1)S(1)} collective-permute-done((bf16[512,256]{1,0:T(8,128)(2,1)S(1)}, bf16[512,256]{1,0:T(8,128)(2,1)S(1)}, u32[]{:S(2)}, u32[]{:S(2)}) %collective-permute-start.2) | collective-permute-done | bytes 262176 | tf_op jit(solution)/shard_map/ppermute | solution.py:225
  33.5 0.0 collective-permute-done.3.rim_inner_ref
  33.5 0.3 shard_map.90
  33.9 1.9 %collective-permute-start.4 = (bf16[512,256]{1,0:T(8,128)(2,1)S(1)}, bf16[512,256]{1,0:T(8,128)(2,1)S(1)}, u32[]{:S(2)}, u32[]{:S(2)}) collective-permute-start(bf16[512,256]{1,0:T(8,128)(2,1)S(1)} %get-tuple-element.31.outer_ref), channel_id=1, source_target_pairs={{0,504},{8,16},{16,8},{24,32},{32,24},{40,48},{48,40},{56,64},{64,... | collective-permute-start | bytes 786440 | tf_op jit(solution)/shard_map/ppermute | solution.py:225
  35.8 6.6 %collective-permute-start.5 = (bf16[512,256]{1,0:T(8,128)(2,1)S(1)}, bf16[512,256]{1,0:T(8,128)(2,1)S(1)}, u32[]{:S(2)}, u32[]{:S(2)}) collective-permute-start(bf16[512,256]{1,0:T(8,128)(2,1)S(1)} %get-tuple-element.32.inner_ref), channel_id=1, source_target_pairs={{0,8},{8,0},{16,24},{24,16},{32,40},{40,32},{48,56},{56,48},{64,72... | collective-permute-start | bytes 786440 | tf_op jit(solution)/shard_map/ppermute | solution.py:225
  42.4 1.3 %shard_map.91 = (f32[16,8,256]{2,1,0:T(8,128)S(1)}, f32[8,128,256]{2,1,0:T(8,128)S(1)}) custom-call(f32[5]{0:T(128)S(1)} %copy-done.1, bf16[512,256]{1,0:T(8,128)(2,1)S(1)} %get-tuple-element.22.outer_ref.probe_outer_ref, bf16[512,256]{1,0:T(8,128)(2,1)S(1)} %get-tuple-element.23.inner_ref.probe_inner_ref, ...), custom_call_target="tpu_custom_call" | custom-call | flops 402653184 | bytes 4194304 | tf_op jit(solution)/shard_map/pallas_call | solution.py:24
  43.7 0.0 collective-permute-done.4.rim_outer_ref
  43.7 0.0 collective-permute-done.5.rim_inner_ref
  43.8 0.3 shard_map.92
  44.1 1.9 %collective-permute-start.6 = (bf16[512,256]{1,0:T(8,128)(2,1)S(1)}, bf16[512,256]{1,0:T(8,128)(2,1)S(1)}, u32[]{:S(2)}, u32[]{:S(2)}) collective-permute-start(bf16[512,256]{1,0:T(8,128)(2,1)S(1)} %get-tuple-element.36.outer_ref), channel_id=1, source_target_pairs={{0,504},{8,16},{16,8},{24,32},{32,24},{40,48},{48,40},{56,64},{64,... | collective-permute-start | bytes 786440 | tf_op jit(solution)/shard_map/ppermute | solution.py:225
  46.0 8.0 %collective-permute-start.7 = (bf16[512,256]{1,0:T(8,128)(2,1)S(1)}, bf16[512,256]{1,0:T(8,128)(2,1)S(1)}, u32[]{:S(2)}, u32[]{:S(2)}) collective-permute-start(bf16[512,256]{1,0:T(8,128)(2,1)S(1)} %get-tuple-element.37.inner_ref), channel_id=1, source_target_pairs={{0,8},{8,0},{16,24},{24,16},{32,40},{40,32},{48,56},{56,48},{64,72... | collective-permute-start | bytes 786440 | tf_op jit(solution)/shard_map/ppermute | solution.py:225
  54.1 1.4 %shard_map.93.terms_ref = f32[16,8,256]{2,1,0:T(8,128)S(1)} custom-call(f32[5]{0:T(128)S(1)} %copy-done.1, bf16[512,256]{1,0:T(8,128)(2,1)S(1)} %get-tuple-element.22.outer_ref.probe_outer_ref, bf16[512,256]{1,0:T(8,128)(2,1)S(1)} %get-tuple-element.23.inner_ref.probe_inner_ref, f32[8,128,256]{2,1,0:T(8,128)S(1)} %get-tuple-element.38.field_ref, ...), custom_call_target="tpu_custom_call" | custom-call | flops 402653184 | bytes 4194304 | tf_op jit(solution)/shard_map/pallas_call | solution.py:24
  55.5 0.0 copy-start
  55.5 0.0 copy-start.2
  55.6 0.0 collective-permute-done.6.rim_outer_ref
  55.6 0.0 collective-permute-done.7.rim_inner_ref
  55.6 1.0 %shard_map.94 = f32[8,8,256]{2,1,0:T(8,128)S(1)} custom-call(f32[5]{0:T(128)S(1)} %copy-done.1, bf16[512,256]{1,0:T(8,128)(2,1)S(1)} %get-tuple-element.22.outer_ref.probe_outer_ref, bf16[512,256]{1,0:T(8,128)(2,1)S(1)} %get-tuple-element.23.inner_ref.probe_inner_ref, bf16[512,256]{1,0:T(8,128)(2,1)S(1)} %collective-permute-done.6.rim_outer_ref, ...), custom_call_target="tpu_custom_call" | custom-call | flops 134217728 | tf_op jit(solution)/shard_map/pallas_call | solution.py:24
  56.6 9.1 %all_to_all.10.shares_ref = f32[8,8,256]{2,1,0:T(8,128)S(1)} all-to-all(f32[8,8,256]{2,1,0:T(8,128)S(1)} %shard_map.94), channel_id=1, replica_groups=mesh['site'=64,'probe'=8] {'probe'}, dimensions={0} | all-to-all | bytes 131072 | tf_op jit(solution)/shard_map/all_to_all | solution.py:303
  65.7 0.1 shard_map.95
  65.9 24.5 %all_to_all.11.largest_ref = f32[64,1,128]{2,1,0:T(1,128)S(1)} all-to-all(f32[64,1,128]{2,1,0:T(1,128)S(1)} %get-tuple-element.40), channel_id=1, replica_groups=mesh['site'=64,'probe'=8] {'site'}, dimensions={0} | all-to-all | bytes 65536 | tf_op jit(solution)/shard_map/all_to_all | solution.py:309
  90.4 0.0 copy-done
  90.4 0.0 copy-done.2
  90.4 0.8 shard_map.96
  (6 shorter events, 0.1 us)
Async XLA Ops:
  1.7 23.8 %collective-permute-start = (bf16[512,256]{1,0:T(8,128)(2,1)S(1)}, bf16[512,256]{1,0:T(8,128)(2,1)S(1)}, u32[]{:S(2)}, u32[]{:S(2)}) collective-permute-start(bf16[512,256]{1,0:T(8,128)(2,1)S(1)} %get-tuple-element.22.outer_ref.probe_outer_ref), channel_id=1, source_target_pairs={{0,504},{8,16},{16,8},{24,32},{32,24},{40,48},{48,40},{56,64},{64,... | collective-permute-start | bytes 786440 | tf_op jit(solution)/shard_map/ppermute | solution.py:225
  6.6 18.9 %collective-permute-start.1 = (bf16[512,256]{1,0:T(8,128)(2,1)S(1)}, bf16[512,256]{1,0:T(8,128)(2,1)S(1)}, u32[]{:S(2)}, u32[]{:S(2)}) collective-permute-start(bf16[512,256]{1,0:T(8,128)(2,1)S(1)} %get-tuple-element.23.inner_ref.probe_inner_ref), channel_id=1, source_target_pairs={{0,8},{8,0},{16,24},{24,16},{32,40},{40,32},{48,56},{56,48},{64,72... | collective-permute-start | bytes 786440 | tf_op jit(solution)/shard_map/ppermute | solution.py:225
  21.0 0.7 copy-start.1
  25.9 7.7 %collective-permute-start.2 = (bf16[512,256]{1,0:T(8,128)(2,1)S(1)}, bf16[512,256]{1,0:T(8,128)(2,1)S(1)}, u32[]{:S(2)}, u32[]{:S(2)}) collective-permute-start(bf16[512,256]{1,0:T(8,128)(2,1)S(1)} %get-tuple-element.26.outer_ref), channel_id=1, source_target_pairs={{0,504},{8,16},{16,8},{24,32},{32,24},{40,48},{48,40},{56,64},{64,... | collective-permute-start | bytes 786440 | tf_op jit(solution)/shard_map/ppermute | solution.py:225
  27.8 5.8 %collective-permute-start.3 = (bf16[512,256]{1,0:T(8,128)(2,1)S(1)}, bf16[512,256]{1,0:T(8,128)(2,1)S(1)}, u32[]{:S(2)}, u32[]{:S(2)}) collective-permute-start(bf16[512,256]{1,0:T(8,128)(2,1)S(1)} %get-tuple-element.27.inner_ref), channel_id=1, source_target_pairs={{0,8},{8,0},{16,24},{24,16},{32,40},{40,32},{48,56},{56,48},{64,72... | collective-permute-start | bytes 786440 | tf_op jit(solution)/shard_map/ppermute | solution.py:225
  33.9 9.9 %collective-permute-start.4 = (bf16[512,256]{1,0:T(8,128)(2,1)S(1)}, bf16[512,256]{1,0:T(8,128)(2,1)S(1)}, u32[]{:S(2)}, u32[]{:S(2)}) collective-permute-start(bf16[512,256]{1,0:T(8,128)(2,1)S(1)} %get-tuple-element.31.outer_ref), channel_id=1, source_target_pairs={{0,504},{8,16},{16,8},{24,32},{32,24},{40,48},{48,40},{56,64},{64,... | collective-permute-start | bytes 786440 | tf_op jit(solution)/shard_map/ppermute | solution.py:225
  35.8 8.0 %collective-permute-start.5 = (bf16[512,256]{1,0:T(8,128)(2,1)S(1)}, bf16[512,256]{1,0:T(8,128)(2,1)S(1)}, u32[]{:S(2)}, u32[]{:S(2)}) collective-permute-start(bf16[512,256]{1,0:T(8,128)(2,1)S(1)} %get-tuple-element.32.inner_ref), channel_id=1, source_target_pairs={{0,8},{8,0},{16,24},{24,16},{32,40},{40,32},{48,56},{56,48},{64,72... | collective-permute-start | bytes 786440 | tf_op jit(solution)/shard_map/ppermute | solution.py:225
  44.1 11.5 %collective-permute-start.6 = (bf16[512,256]{1,0:T(8,128)(2,1)S(1)}, bf16[512,256]{1,0:T(8,128)(2,1)S(1)}, u32[]{:S(2)}, u32[]{:S(2)}) collective-permute-start(bf16[512,256]{1,0:T(8,128)(2,1)S(1)} %get-tuple-element.36.outer_ref), channel_id=1, source_target_pairs={{0,504},{8,16},{16,8},{24,32},{32,24},{40,48},{48,40},{56,64},{64,... | collective-permute-start | bytes 786440 | tf_op jit(solution)/shard_map/ppermute | solution.py:225
  46.0 9.5 %collective-permute-start.7 = (bf16[512,256]{1,0:T(8,128)(2,1)S(1)}, bf16[512,256]{1,0:T(8,128)(2,1)S(1)}, u32[]{:S(2)}, u32[]{:S(2)}) collective-permute-start(bf16[512,256]{1,0:T(8,128)(2,1)S(1)} %get-tuple-element.37.inner_ref), channel_id=1, source_target_pairs={{0,8},{8,0},{16,24},{24,16},{32,40},{40,32},{48,56},{56,48},{64,72... | collective-permute-start | bytes 786440 | tf_op jit(solution)/shard_map/ppermute | solution.py:225
  55.5 34.9 %copy-start = (f32[2,4,256]{2,1,0:T(4,128)S(1)}, f32[2,4,256]{2,1,0:T(4,128)}, u32[]{:S(2)}) copy-start(f32[2,4,256]{2,1,0:T(4,128)} %angles_ref.1) | copy-start | bytes 24580
  55.5 34.9 %copy-start.2 = (f32[2,4,256]{2,1,0:T(4,128)S(1)}, f32[2,4,256]{2,1,0:T(4,128)}, u32[]{:S(2)}) copy-start(f32[2,4,256]{2,1,0:T(4,128)} %noise_ref.1) | copy-start | bytes 24580

commit v2 on v1

v2 whole, which is shorter than its diff:
```python
import functools
import jax
import jax.numpy as jnp
from jax import lax
from jax.experimental import pallas as pl
from jax.experimental.pallas import tpu as pltpu
from jax.sharding import PartitionSpec as P

BAND = 8.0
STEP_MAX = 0.3
TWO_TEMP = 0.1

VERT, LEFT, RIGHT, RIM, TURNED = range(5)
IN_VMEM = pl.BlockSpec(memory_space=pltpu.VMEM)
IN_SMEM = pl.BlockSpec(memory_space=pltpu.SMEM)
IN_HBM = pl.BlockSpec(memory_space=pltpu.HBM)


def held(array, space=pltpu.VMEM):
    return pltpu.with_memory_space_constraint(array, space)


def call(body, outs, in_specs, args, scratch=(), flops=0, moved=0):
    return pl.pallas_call(
        body,
        out_shape=[pltpu.VMEM(shape, dtype) for shape, dtype in outs],
        in_specs=in_specs,
        out_specs=[IN_VMEM] * len(outs),
        scratch_shapes=list(scratch),
        compiler_params=pltpu.CompilerParams(vmem_limit_bytes=16 * 1024 * 1024),
        cost_estimate=pl.CostEstimate(flops=flops, bytes_accessed=moved, transcendentals=0),
    )(*args)


def product(vectors, matrix):
    return jnp.dot(vectors, matrix, preferred_element_type=jnp.float32)


def folded(values):
    return jnp.sum(values.reshape(-1, 8, values.shape[-1]), axis=0)


def overlap_terms(probe, vectors):
    half = probe.shape[0] // 2
    upper_r = probe[:half].astype(jnp.float32)
    lower_r = probe[half:].astype(jnp.float32)
    upper_w, lower_w = vectors[:half], vectors[half:]
    same = folded(upper_r * upper_w - lower_r * lower_w)
    cross = folded(upper_r * lower_w + lower_r * upper_w)
    return same, cross


def split_body(parity_ref, probes_ref, outer_ref, inner_ref, sems):
    parity = parity_ref[0]
    copies = [
        pltpu.make_async_copy(probes_ref.at[parity], outer_ref, sems.at[0]),
        pltpu.make_async_copy(probes_ref.at[1 - parity], inner_ref, sems.at[1]),
    ]
    for copy in copies:
        copy.start()
    for copy in copies:
        copy.wait()


def local_hop(cols, rows, outer_ref, inner_ref, tile, matrix):
    refs = (outer_ref, inner_ref)
    row, col = divmod(tile, cols)

    def vectors(r, c):
        return refs[r][pl.ds(c * rows, rows), :]

    right, left = (col + 1) % cols, (col - 1) % cols
    total = product(vectors(1 - row, col), matrix(VERT, (1 - row) * cols + col))
    total += product(vectors(row, right), matrix(LEFT, row * cols + right))
    total += product(vectors(row, left), matrix(RIGHT, row * cols + left))
    return total


def kondo(vectors, twice_cos, twice_sin):
    half = vectors.shape[0] // 2
    upper, lower = vectors[:half], vectors[half:]
    return jnp.concatenate(
        [twice_cos * upper + twice_sin * lower, twice_sin * upper - twice_cos * lower], axis=0
    )


def first_body(cols, rows, probe_total, parity_ref, offsets_hbm, coef_hbm, hopping_hbm, angles_hbm,
               coupling_hbm, outer_ref, inner_ref, sorted_ref, part_ref, terms_ref, weights_ref,
               cos_ref, sin_ref, same_ref, cross_ref,
               offsets_ref, coef_ref, raw_ref, angles_ref, coupling_ref, sems):
    tiles = 2 * cols
    slots = offsets_ref.shape[2]
    steps = coef_ref.shape[0]
    parity = parity_ref[0]
    small = [
        pltpu.make_async_copy(source, target, sems.at[k])
        for k, (source, target) in enumerate((
            (offsets_hbm, offsets_ref), (coef_hbm, coef_ref),
            (angles_hbm, angles_ref), (coupling_hbm, coupling_ref),
        ))
    ]
    large = [
        pltpu.make_async_copy(
            hopping_hbm.at[pl.ds(tile * slots, slots)], raw_ref.at[pl.ds(tile * slots, slots)],
            sems.at[4 + tile],
        )
        for tile in range(tiles)
    ]
    for copy in small + large:
        copy.start()
    for copy in small:
        copy.wait()

    def tile_of(kind, tile):
        row, col = divmod(tile, cols)
        origin = row + parity - 2 * row * parity
        if kind == LEFT:
            code = 3
        elif kind == RIGHT:
            code = 5
        else:
            towards_high = (row == 0) == (kind == VERT)
            code = 7 - 6 * parity if towards_high else 1 + 6 * parity
        slot = jnp.int32(0)
        for k in range(1, slots):
            slot += jnp.where(offsets_ref[origin, col, k] == code, k, 0)
        return (origin * cols + col) * slots + slot

    for row in range(2):
        origin = row + parity - 2 * row * parity
        place = pl.ds(row * cols, cols)
        angles, strength = angles_ref[origin], coupling_ref[origin]
        cosines, sine_values = jnp.cos(angles), jnp.sin(angles)
        scale = (-BAND / probe_total) * strength
        cos_ref[place, :] = 2.0 * strength * cosines
        sin_ref[place, :] = 2.0 * strength * sine_values
        same_ref[place, :] = -scale * sine_values
        cross_ref[place, :] = scale * cosines
    for level in range(steps):
        weights_ref[pl.ds(level, 1), :] = jnp.full(
            (1, weights_ref.shape[1]), (level + 1) * coef_ref[level], jnp.float32
        )
    for tile in range(tiles):
        row, col = divmod(tile, cols)
        probe = (outer_ref, inner_ref)[row][pl.ds(col * rows, rows), :]
        same, cross = overlap_terms(probe, probe.astype(jnp.float32))
        terms_ref[tile] = coef_ref[0] * same
        terms_ref[tiles + tile] = coef_ref[0] * cross
    for copy in large:
        copy.wait()

    def matrix(kind, tile):
        found = raw_ref[tile_of(kind, tile)]
        sorted_ref[kind * tiles + tile] = found
        return found

    for tile in range(tiles):
        row, col = divmod(tile, cols)
        probe = (outer_ref, inner_ref)[row][pl.ds(col * rows, rows), :].astype(jnp.float32)
        total = local_hop(cols, rows, outer_ref, inner_ref, tile, matrix)
        part_ref[tile] = 2.0 * total + kondo(
            probe, cos_ref[pl.ds(tile, 1), :], sin_ref[pl.ds(tile, 1), :]
        )
    for tile in range(tiles):
        sorted_ref[TURNED * tiles + tile] = matrix(RIM, tile).T


def rim_body(cols, rows, rim_outer_ref, rim_inner_ref, sorted_ref, part_ref,
             field_ref, outer_ref, inner_ref):
    tiles = 2 * cols
    for tile in range(tiles):
        row, col = divmod(tile, cols)
        place = pl.ds(col * rows, rows)
        rim = (rim_outer_ref, rim_inner_ref)[row][place, :]
        field = part_ref[tile] + 2.0 * product(rim, sorted_ref[TURNED * tiles + tile])
        field_ref[tile] = field
        (outer_ref, inner_ref)[row][place, :] = field.astype(jnp.bfloat16)


def rim_sent_body(cols, rows, level, rim_outer_ref, rim_inner_ref, sorted_ref, part_ref,
                  probe_outer_ref, probe_inner_ref, weights_ref,
                  field_ref, outer_ref, inner_ref, sent_outer_ref, sent_inner_ref):
    tiles = 2 * cols
    rim_body(cols, rows, rim_outer_ref, rim_inner_ref, sorted_ref, part_ref,
             field_ref, outer_ref, inner_ref)
    weight = 2.0 * weights_ref[pl.ds(level + 1, 1), 0:1]
    for tile in range(tiles):
        row, col = divmod(tile, cols)
        place = pl.ds(col * rows, rows)
        field_low = (outer_ref, inner_ref)[row][place, :]
        probe = (probe_outer_ref, probe_inner_ref)[row][place, :]
        same, cross = overlap_terms(probe, product(field_low, sorted_ref[RIM * tiles + tile]))
        sent_ref = (sent_outer_ref, sent_inner_ref)[row]
        sent_ref[pl.ds(col, 1), :] = weight * jnp.sum(same, axis=0, keepdims=True)
        sent_ref[pl.ds(cols + col, 1), :] = weight * jnp.sum(cross, axis=0, keepdims=True)


def local_body(cols, rows, level, last, weights_ref, probe_outer_ref, probe_inner_ref, field_ref,
               outer_ref, inner_ref, *rest):
    tiles = 2 * cols
    previous_ref = None
    if level > 1:
        previous_ref, *rest = rest
    sorted_ref, cos_ref, sin_ref, terms_ref = rest[:4]
    rest = rest[4:]
    weight = weights_ref[pl.ds(level, 1), 0:1]
    weight_next = weights_ref[pl.ds(level + 1, 1), 0:1]

    def matrix(kind, source):
        return sorted_ref[kind * tiles + source]

    for tile in range(tiles):
        row, col = divmod(tile, cols)
        place = pl.ds(col * rows, rows)
        probe = (probe_outer_ref, probe_inner_ref)[row][place, :]
        field = field_ref[tile]
        total = local_hop(cols, rows, outer_ref, inner_ref, tile, matrix)
        following = 2.0 * total + kondo(
            field, cos_ref[pl.ds(tile, 1), :], sin_ref[pl.ds(tile, 1), :]
        )
        if previous_ref is None:
            following -= probe.astype(jnp.float32)
        else:
            following -= previous_ref[tile]
        if last:
            same_ref, cross_ref, share_ref = rest
            same, cross = overlap_terms(probe, weight * field + weight_next * following)
            same = jnp.sum(terms_ref[tile] + same, axis=0, keepdims=True)
            cross = jnp.sum(terms_ref[tiles + tile] + cross, axis=0, keepdims=True)
            one = pl.ds(tile, 1)
            share_ref[one, :] = same_ref[one, :] * same + cross_ref[one, :] * cross
        else:
            out_ref, following_ref = rest
            same, cross = overlap_terms(probe, field)
            out_ref[tile] = terms_ref[tile] + weight * same
            out_ref[tiles + tile] = terms_ref[tiles + tile] + weight * cross
            following_ref[tile] = following


def share_body(cols, parity_ref, share_ref, from_inner_ref, to_outer_ref, same_ref, cross_ref,
               out_ref):
    peers = out_ref.shape[0] // 2
    parity = parity_ref[0]
    same = same_ref[cols:, :] * from_inner_ref[:cols, :]
    cross = cross_ref[cols:, :] * from_inner_ref[cols:, :]
    share = jnp.concatenate([share_ref[:cols, :], share_ref[cols:, :] + same + cross], axis=0)
    for peer in range(peers):
        out_ref[(1 - parity) * peers + peer] = share
        out_ref[parity * peers + peer] = to_outer_ref[...]


def force_body(cols, parity_ref, shares_ref, same_ref, cross_ref, force_ref, largest_ref):
    peers = shares_ref.shape[0] // 2
    parity = parity_ref[0]
    own, across = shares_ref[(1 - parity) * peers], shares_ref[parity * peers]
    for peer in range(1, peers):
        own += shares_ref[(1 - parity) * peers + peer]
        across += shares_ref[parity * peers + peer]
    outer = same_ref[:cols, :] * across[:cols] + cross_ref[:cols, :] * across[cols:]
    force = jnp.concatenate([own[:cols] + outer, own[cols:]], axis=0)
    force_ref[...] = force
    largest_ref[...] = jnp.full(largest_ref.shape, jnp.max(jnp.abs(force)), jnp.float32)


def move_body(parity_ref, largest_ref, force_ref, angles_ref, noise_ref, next_ref, out_ref):
    parity = parity_ref[0]
    cols = out_ref.shape[1]
    largest = jnp.max(largest_ref[...])
    step_size = jnp.full((1, 1), STEP_MAX, jnp.float32) / (largest + 1e-06)
    kick = jnp.sqrt(TWO_TEMP * step_size)
    for row in range(2):
        origin = row + parity - 2 * row * parity
        force = force_ref[pl.ds(row * cols, cols), :]
        out_ref[origin] = force
        next_ref[origin] = angles_ref[origin] + step_size * force + kick * noise_ref[origin]


def exchange_outer(outer):
    count = lax.axis_size("site")
    pairs = [(i, (i + 1) % count if i % 2 else (i - 1) % count) for i in range(count)]
    return lax.ppermute(outer, "site", pairs)


def exchange_inner(inner):
    return lax.ppermute(inner, "site", [(i, i ^ 1) for i in range(lax.axis_size("site"))])


def local(angles, coupling, thermal_noise, coefficients, probes, hopping, offsets):
    cols, orbitals, share, width = probes.shape[1:]
    rows = orbitals * share
    tiles = 2 * cols
    steps = coefficients.shape[0] - 1
    f32, bf16 = jnp.float32, jnp.bfloat16
    side = ((cols * rows, width), bf16)
    whole = ((tiles, rows, width), f32)
    terms_like = ((2 * tiles, 8, width), f32)
    probe_total = lax.axis_size("probe") * share

    sites, peers = lax.axis_size("site"), lax.axis_size("probe")
    parity = (lax.axis_index("site") % 2).astype(jnp.int32).reshape(1)
    outer, inner = call(
        split_body, [side, side], [IN_SMEM, IN_HBM],
        (parity, held(probes.reshape(2, cols * rows, width), pltpu.HBM)),
        scratch=[pltpu.SemaphoreType.DMA((2,))],
    )
    probe_outer, probe_inner = outer, inner
    rims = rim_probes = exchange_outer(outer), exchange_inner(inner)

    local_flops = 2 * 3 * tiles * rows * width * width
    row_like = ((tiles, width), f32)
    sorted_hop, part, terms, weights, twice_cos, twice_sin, same_factor, cross_factor = call(
        functools.partial(first_body, cols, rows, probe_total),
        [((5 * tiles, width, width), bf16), whole, terms_like, ((8, 128), f32)] + [row_like] * 4,
        [IN_SMEM] + [IN_HBM] * 5 + [IN_VMEM] * 2,
        (parity, *(held(x, pltpu.HBM) for x in (
            offsets, coefficients, hopping.reshape(-1, width, width), angles, coupling)),
         held(outer), held(inner)),
        scratch=[
            pltpu.SMEM(offsets.shape, jnp.int32), pltpu.SMEM(coefficients.shape, f32),
            pltpu.VMEM((hopping.size // width**2, width, width), bf16),
            pltpu.VMEM(angles.shape, f32), pltpu.VMEM(coupling.shape, f32),
            pltpu.SemaphoreType.DMA((4 + tiles,)),
        ],
        flops=local_flops, moved=hopping.size * 2,
    )
    field = previous = None
    for level in range(1, steps):
        last = level == steps - 1
        previous = field
        args = [*rims, sorted_hop, part]
        if last:
            args += [*rim_probes, weights]
            field, outer, inner, to_outer, to_inner = call(
                functools.partial(rim_sent_body, cols, rows, level),
                [whole, side, side, row_like, row_like],
                [IN_VMEM] * len(args), tuple(held(x) for x in args), flops=local_flops,
            )
            from_inner = exchange_inner(to_inner)
        else:
            field, outer, inner = call(
                functools.partial(rim_body, cols, rows), [whole, side, side],
                [IN_VMEM] * len(args), tuple(held(x) for x in args), flops=local_flops // 3,
            )
            rims = exchange_outer(outer), exchange_inner(inner)
        args = [weights, probe_outer, probe_inner, field, outer, inner]
        if level > 1:
            args.append(previous)
        args += [sorted_hop, twice_cos, twice_sin, terms]
        if last:
            args += [same_factor, cross_factor]
        terms, *rest = call(
            functools.partial(local_body, cols, rows, level, last),
            [row_like] if last else [terms_like, whole],
            [IN_VMEM] * len(args), tuple(held(x) for x in args),
            flops=local_flops, moved=hopping.size * 2,
        )
        if not last:
            part = rest[0]

    pairs = [
        [site % sites * peers + peer for site in (2 * i - 1, 2 * i) for peer in range(peers)]
        for i in range(sites // 2)
    ]
    shares = call(
        functools.partial(share_body, cols), [((2 * peers, tiles, width), f32)],
        [IN_SMEM] + [IN_VMEM] * 5,
        (parity, *(held(x) for x in (terms, from_inner, to_outer, same_factor, cross_factor))),
    )[0]
    shares = lax.all_to_all(shares, ("site", "probe"), 0, 0, axis_index_groups=pairs)
    force, largest = call(
        functools.partial(force_body, cols), [row_like, ((sites, 1, 128), f32)],
        [IN_SMEM] + [IN_VMEM] * 3,
        (parity, *(held(x) for x in (shares, same_factor, cross_factor))),
    )
    largest = lax.all_to_all(largest, "site", 0, 0)
    return pl.pallas_call(
        move_body,
        out_shape=[jax.ShapeDtypeStruct(angles.shape, f32)] * 2,
        in_specs=[IN_SMEM] + [IN_VMEM] * 4,
        out_specs=[IN_VMEM] * 2,
    )(parity, held(largest), held(force), held(angles), held(thermal_noise))


def solution(mesh):
    in_specs = (
        P("site", None, None),
        P("site", None, None),
        P("site", None, None),
        P(),
        P("site", None, None, "probe", None),
        P("site", None, None, None, None),
        P("site", None, None),
    )
    out_specs = (P("site", None, None), P("site", None, None))
    return jax.shard_map(local, mesh=mesh, in_specs=in_specs, out_specs=out_specs, check_vma=False)
```

time: 91.8 us -> 84.9 us (0.925)
  Pallas kernels: 11.8 us -> 8.91 us
  local copies, waits for them, and re-layouts: 2.22 us -> 0.01 us
  blocking collectives: 33.7 us -> 34.9 us
  starting transfers between devices: 40.3 us -> 39.1 us
    pallas_call x10, Pallas kernels: 11.1 us -> 8.16 us  [call(): pl.pallas_call(body, out_shape=[pltpu.VMEM(shape, dtype) for shape, dtype...]
    all_to_all x1, blocking collectives: 9.14 us -> 11.4 us  [local(): lax.all_to_all(shares, ('site', 'probe'), 0, 0, axis_index_groups=pairs)]
    ppermute x8 -> x7, starting transfers between devices: 40.3 us -> 39.1 us  [the longest x4 30.3 us: exchange_inner(): lax.ppermute(inner, 'site', [(i, i ^ 1) for i in range(lax.axis_size('sit...]
    all_to_all x1, blocking collectives: 24.5 us -> 23.5 us  [local(): largest = lax.all_to_all(largest, 'site', 0, 0)]
  transfers between devices with their start and end apart: 8 -> 7, of which waited for: 1 -> 2; matrix products, arithmetic and copies ran while one was open for 3% -> 0% of each run, Pallas kernels for 9% -> 7%
where the time goes in v2:
time: 84.9 us; the launch traced here: 84.4 us
  starting transfers between devices  39.1 us (46%)
  blocking collectives  34.9 us (41%)
  Pallas kernels  8.91 us (10%)
    ppermute x4, starting transfers between devices, exchange_inner(): lax.ppermute(inner, 'site', [(i, i ^ 1) for i in range(lax.axis_size('sit...  30.3 us
    all_to_all x1, blocking collectives, local(): largest = lax.all_to_all(largest, 'site', 0, 0)  23.5 us
    all_to_all x1, blocking collectives, local(): lax.all_to_all(shares, ('site', 'probe'), 0, 0, axis_index_groups=pairs)  11.4 us
    ppermute x3, starting transfers between devices, exchange_outer(): return lax.ppermute(outer, 'site', pairs)  8.78 us
    pallas_call x10, Pallas kernels, call(): pl.pallas_call(body, out_shape=[pltpu.VMEM(shape, dtype) for shape, dtype...  8.16 us
  transfers between devices with their start and end apart: 7, of which 2 were waited for; matrix products, arithmetic and copies ran while one was open for 0% of the time, Pallas kernels for 7%

profile of v2, /device:TPU:1, one launch (start us, length us, event | category | flops | bytes accessed | tf_op | source)
XLA Modules:
  0.0 84.4 jit_solution(6636512916265436495)
XLA Ops:
  0.6 1.1 %shard_map.86 = (bf16[512,256]{1,0:T(8,128)(2,1)S(1)}, bf16[512,256]{1,0:T(8,128)(2,1)S(1)}) custom-call(s32[1]{0:T(128)} %bitcast.parity_ref, bf16[2,512,256]{2,1,0:T(8,128)(2,1)} %bitcast.4), custom_call_target="tpu_custom_call" | custom-call | tf_op jit(solution)/shard_map/pallas_call | solution.py:24
  1.7 4.9 %collective-permute-start = (bf16[512,256]{1,0:T(8,128)(2,1)S(1)}, bf16[512,256]{1,0:T(8,128)(2,1)S(1)}, u32[]{:S(2)}, u32[]{:S(2)}) collective-permute-start(bf16[512,256]{1,0:T(8,128)(2,1)S(1)} %get-tuple-element.29.outer_ref.probe_outer_ref), channel_id=1, source_target_pairs={{0,504},{8,16},{16,8},{24,32},{32,24},{40,48},{48,40},{56,64},{64,... | collective-permute-start | bytes 786440 | tf_op jit(solution)/shard_map/ppermute | solution.py:281
  6.6 11.9 %collective-permute-start.1 = (bf16[512,256]{1,0:T(8,128)(2,1)S(1)}, bf16[512,256]{1,0:T(8,128)(2,1)S(1)}, u32[]{:S(2)}, u32[]{:S(2)}) collective-permute-start(bf16[512,256]{1,0:T(8,128)(2,1)S(1)} %get-tuple-element.30.inner_ref.probe_inner_ref), channel_id=1, source_target_pairs={{0,8},{8,0},{16,24},{24,16},{32,40},{40,32},{48,56},{56,48},{64,72... | collective-permute-start | bytes 786440 | tf_op jit(solution)/shard_map/ppermute | solution.py:285
  18.6 3.2 %shard_map.87 = (bf16[40,256,256]{2,1,0:T(8,128)(2,1)S(1)}, f32[8,128,256]{2,1,0:T(8,128)S(1)}, f32[16,8,256]{2,1,0:T(8,128)S(1)}, f32[8,128]{1,0:T(8,128)S(1)},...) custom-call(s32[1]{0:T(128)} %bitcast.parity_ref, ...), custom_call_target="tpu_custom_call" | custom-call | flops 402653184 | bytes 4194304 | tf_op jit(solution)/shard_map/pallas_call | solution.py:24
  21.8 0.0 collective-permute-done.rim_outer_ref.probe_outer_ref
  21.8 0.0 collective-permute-done.1.rim_inner_ref.probe_inner_ref
  21.8 0.3 shard_map.88
  22.2 1.9 %collective-permute-start.2 = (bf16[512,256]{1,0:T(8,128)(2,1)S(1)}, bf16[512,256]{1,0:T(8,128)(2,1)S(1)}, u32[]{:S(2)}, u32[]{:S(2)}) collective-permute-start(bf16[512,256]{1,0:T(8,128)(2,1)S(1)} %get-tuple-element.34.outer_ref), channel_id=1, source_target_pairs={{0,504},{8,16},{16,8},{24,32},{32,24},{40,48},{48,40},{56,64},{64,... | collective-permute-start | bytes 786440 | tf_op jit(solution)/shard_map/ppermute | solution.py:281
  24.1 6.1 %collective-permute-start.3 = (bf16[512,256]{1,0:T(8,128)(2,1)S(1)}, bf16[512,256]{1,0:T(8,128)(2,1)S(1)}, u32[]{:S(2)}, u32[]{:S(2)}) collective-permute-start(bf16[512,256]{1,0:T(8,128)(2,1)S(1)} %get-tuple-element.35.inner_ref), channel_id=1, source_target_pairs={{0,8},{8,0},{16,24},{24,16},{32,40},{40,32},{48,56},{56,48},{64,72... | collective-permute-start | bytes 786440 | tf_op jit(solution)/shard_map/ppermute | solution.py:285
  30.2 0.8 shard_map.89
  31.0 0.0 collective-permute-done.2.rim_outer_ref
  31.0 0.3 collective-permute-done.3.rim_inner_ref
  31.4 0.3 shard_map.90
  31.7 1.9 %collective-permute-start.4 = (bf16[512,256]{1,0:T(8,128)(2,1)S(1)}, bf16[512,256]{1,0:T(8,128)(2,1)S(1)}, u32[]{:S(2)}, u32[]{:S(2)}) collective-permute-start(bf16[512,256]{1,0:T(8,128)(2,1)S(1)} %get-tuple-element.41.outer_ref), channel_id=1, source_target_pairs={{0,504},{8,16},{16,8},{24,32},{32,24},{40,48},{48,40},{56,64},{64,... | collective-permute-start | bytes 786440 | tf_op jit(solution)/shard_map/ppermute | solution.py:281
  33.6 8.2 %collective-permute-start.5 = (bf16[512,256]{1,0:T(8,128)(2,1)S(1)}, bf16[512,256]{1,0:T(8,128)(2,1)S(1)}, u32[]{:S(2)}, u32[]{:S(2)}) collective-permute-start(bf16[512,256]{1,0:T(8,128)(2,1)S(1)} %get-tuple-element.42.inner_ref), channel_id=1, source_target_pairs={{0,8},{8,0},{16,24},{24,16},{32,40},{40,32},{48,56},{56,48},{64,72... | collective-permute-start | bytes 786440 | tf_op jit(solution)/shard_map/ppermute | solution.py:285
  41.9 0.8 shard_map.91
  42.7 0.0 collective-permute-done.4.rim_outer_ref
  42.7 0.3 collective-permute-done.5.rim_inner_ref
  43.0 0.6 shard_map.92
  43.6 0.0 copy-start
  43.6 0.0 copy-start.1
  43.6 4.0 %collective-permute-start.6 = (f32[8,256]{1,0:T(8,128)S(1)}, f32[8,256]{1,0:T(8,128)S(1)}, u32[]{:S(2)}, u32[]{:S(2)}) collective-permute-start(f32[8,256]{1,0:T(8,128)S(1)} %get-tuple-element.52), channel_id=1, source_target_pairs={{0,8},{8,0},{16,24},{24,16},{32,40},{40,32},{48,56},{56,48},{64,72... | collective-permute-start | bytes 24584 | tf_op jit(solution)/shard_map/ppermute | solution.py:285
  47.7 0.9 %shard_map.93.share_ref = f32[8,256]{1,0:T(8,128)S(1)} custom-call(f32[8,128]{1,0:T(8,128)S(1)} %get-tuple-element.31.weights_ref, bf16[512,256]{1,0:T(8,128)(2,1)S(1)} %get-tuple-element.29.outer_ref.probe_outer_ref, bf16[512,256]{1,0:T(8,128)(2,1)S(1)} %get-tuple-element.30.inner_ref.probe_inner_ref, f32[8,128,256]{2,1,0:T(8,128)S(1)} %get-tuple-element.46.field_ref, ...), custom_call_target="tpu_custom_call" | custom-call | flops 402653184 | bytes 4194304 | tf_op jit(solution)/shard_map/pallas_call | solution.py:24
  48.6 0.0 collective-permute-done.6.from_inner_ref
  48.6 11.4 %all_to_all.10.shares_ref = f32[16,8,256]{2,1,0:T(8,128)S(1)} all-to-all(f32[16,8,256]{2,1,0:T(8,128)S(1)} %shard_map.94), channel_id=1, replica_groups={{504,505,506,507,508,509,510,511,0,1,2,3,4,5,6,7},{8,9,10,11,12,13,14,1..., dimensions={0} | all-to-all | bytes 262144 | tf_op jit(solution)/shard_map/all_to_all | solution.py:369
  60.0 0.1 shard_map.95
  60.2 23.5 %all_to_all.11.largest_ref = f32[64,1,128]{2,1,0:T(1,128)S(1)} all-to-all(f32[64,1,128]{2,1,0:T(1,128)S(1)} %get-tuple-element.54), channel_id=1, replica_groups=mesh['site'=64,'probe'=8] {'site'}, dimensions={0} | all-to-all | bytes 65536 | tf_op jit(solution)/shard_map/all_to_all | solution.py:375
  83.7 0.0 copy-done
  83.7 0.0 copy-done.1
  83.7 0.8 shard_map.96
  (1 shorter events, 0.0 us)
Async XLA Ops:
  1.7 20.1 %collective-permute-start = (bf16[512,256]{1,0:T(8,128)(2,1)S(1)}, bf16[512,256]{1,0:T(8,128)(2,1)S(1)}, u32[]{:S(2)}, u32[]{:S(2)}) collective-permute-start(bf16[512,256]{1,0:T(8,128)(2,1)S(1)} %get-tuple-element.29.outer_ref.probe_outer_ref), channel_id=1, source_target_pairs={{0,504},{8,16},{16,8},{24,32},{32,24},{40,48},{48,40},{56,64},{64,... | collective-permute-start | bytes 786440 | tf_op jit(solution)/shard_map/ppermute | solution.py:281
  6.6 15.2 %collective-permute-start.1 = (bf16[512,256]{1,0:T(8,128)(2,1)S(1)}, bf16[512,256]{1,0:T(8,128)(2,1)S(1)}, u32[]{:S(2)}, u32[]{:S(2)}) collective-permute-start(bf16[512,256]{1,0:T(8,128)(2,1)S(1)} %get-tuple-element.30.inner_ref.probe_inner_ref), channel_id=1, source_target_pairs={{0,8},{8,0},{16,24},{24,16},{32,40},{40,32},{48,56},{56,48},{64,72... | collective-permute-start | bytes 786440 | tf_op jit(solution)/shard_map/ppermute | solution.py:285
  22.2 8.9 %collective-permute-start.2 = (bf16[512,256]{1,0:T(8,128)(2,1)S(1)}, bf16[512,256]{1,0:T(8,128)(2,1)S(1)}, u32[]{:S(2)}, u32[]{:S(2)}) collective-permute-start(bf16[512,256]{1,0:T(8,128)(2,1)S(1)} %get-tuple-element.34.outer_ref), channel_id=1, source_target_pairs={{0,504},{8,16},{16,8},{24,32},{32,24},{40,48},{48,40},{56,64},{64,... | collective-permute-start | bytes 786440 | tf_op jit(solution)/shard_map/ppermute | solution.py:281
  24.1 7.3 %collective-permute-start.3 = (bf16[512,256]{1,0:T(8,128)(2,1)S(1)}, bf16[512,256]{1,0:T(8,128)(2,1)S(1)}, u32[]{:S(2)}, u32[]{:S(2)}) collective-permute-start(bf16[512,256]{1,0:T(8,128)(2,1)S(1)} %get-tuple-element.35.inner_ref), channel_id=1, source_target_pairs={{0,8},{8,0},{16,24},{24,16},{32,40},{40,32},{48,56},{56,48},{64,72... | collective-permute-start | bytes 786440 | tf_op jit(solution)/shard_map/ppermute | solution.py:285
  31.7 11.0 %collective-permute-start.4 = (bf16[512,256]{1,0:T(8,128)(2,1)S(1)}, bf16[512,256]{1,0:T(8,128)(2,1)S(1)}, u32[]{:S(2)}, u32[]{:S(2)}) collective-permute-start(bf16[512,256]{1,0:T(8,128)(2,1)S(1)} %get-tuple-element.41.outer_ref), channel_id=1, source_target_pairs={{0,504},{8,16},{16,8},{24,32},{32,24},{40,48},{48,40},{56,64},{64,... | collective-permute-start | bytes 786440 | tf_op jit(solution)/shard_map/ppermute | solution.py:281
  33.6 9.4 %collective-permute-start.5 = (bf16[512,256]{1,0:T(8,128)(2,1)S(1)}, bf16[512,256]{1,0:T(8,128)(2,1)S(1)}, u32[]{:S(2)}, u32[]{:S(2)}) collective-permute-start(bf16[512,256]{1,0:T(8,128)(2,1)S(1)} %get-tuple-element.42.inner_ref), channel_id=1, source_target_pairs={{0,8},{8,0},{16,24},{24,16},{32,40},{40,32},{48,56},{56,48},{64,72... | collective-permute-start | bytes 786440 | tf_op jit(solution)/shard_map/ppermute | solution.py:285
  43.6 40.1 %copy-start = (f32[2,4,256]{2,1,0:T(4,128)S(1)}, f32[2,4,256]{2,1,0:T(4,128)}, u32[]{:S(2)}) copy-start(f32[2,4,256]{2,1,0:T(4,128)} %angles_ref.1) | copy-start | bytes 24580
  43.6 40.1 %copy-start.1 = (f32[2,4,256]{2,1,0:T(4,128)S(1)}, f32[2,4,256]{2,1,0:T(4,128)}, u32[]{:S(2)}) copy-start(f32[2,4,256]{2,1,0:T(4,128)} %noise_ref.1) | copy-start | bytes 24580
  43.6 4.9 %collective-permute-start.6 = (f32[8,256]{1,0:T(8,128)S(1)}, f32[8,256]{1,0:T(8,128)S(1)}, u32[]{:S(2)}, u32[]{:S(2)}) collective-permute-start(f32[8,256]{1,0:T(8,128)S(1)} %get-tuple-element.52), channel_id=1, source_target_pairs={{0,8},{8,0},{16,24},{24,16},{32,40},{40,32},{48,56},{56,48},{64,72... | collective-permute-start | bytes 24584 | tf_op jit(solution)/shard_map/ppermute | solution.py:285

commit v3 on v2

v3 whole, which is shorter than its diff:
```python
import functools
import jax
import jax.numpy as jnp
from jax import lax
from jax.experimental import pallas as pl
from jax.experimental.pallas import tpu as pltpu
from jax.sharding import PartitionSpec as P

BAND = 8.0
STEP_MAX = 0.3
TWO_TEMP = 0.1

VERT, LEFT, RIGHT, RIM, TURNED = range(5)
IN_VMEM = pl.BlockSpec(memory_space=pltpu.VMEM)
IN_SMEM = pl.BlockSpec(memory_space=pltpu.SMEM)
IN_HBM = pl.BlockSpec(memory_space=pltpu.HBM)


def held(array, space=pltpu.VMEM):
    return pltpu.with_memory_space_constraint(array, space)


def call(body, outs, in_specs, args, scratch=(), flops=0, moved=0):
    return pl.pallas_call(
        body,
        out_shape=[pltpu.VMEM(shape, dtype) for shape, dtype in outs],
        in_specs=in_specs,
        out_specs=[IN_VMEM] * len(outs),
        scratch_shapes=list(scratch),
        compiler_params=pltpu.CompilerParams(vmem_limit_bytes=16 * 1024 * 1024),
        cost_estimate=pl.CostEstimate(flops=flops, bytes_accessed=moved, transcendentals=0),
    )(*args)


def product(vectors, matrix):
    return jnp.dot(vectors, matrix, preferred_element_type=jnp.float32)


def folded(values):
    return jnp.sum(values.reshape(-1, 8, values.shape[-1]), axis=0)


def overlap_terms(probe, vectors):
    half = probe.shape[0] // 2
    upper_r = probe[:half].astype(jnp.float32)
    lower_r = probe[half:].astype(jnp.float32)
    upper_w, lower_w = vectors[:half], vectors[half:]
    same = folded(upper_r * upper_w - lower_r * lower_w)
    cross = folded(upper_r * lower_w + lower_r * upper_w)
    return same, cross


def fetch_body(rows, parity_ref, probes_hbm, angles_hbm, coupling_hbm, hopping_hbm,
               outer_ref, inner_ref, angles_ref, coupling_ref, raw_ref, sems):
    parity = parity_ref[0]
    copies = [
        pltpu.make_async_copy(source, target, sems.at[k])
        for k, (source, target) in enumerate((
            (probes_hbm.at[parity], outer_ref),
            (probes_hbm.at[1 - parity], inner_ref),
            (angles_hbm, angles_ref),
            (coupling_hbm, coupling_ref),
            (hopping_hbm, raw_ref),
        ))
    ]
    for copy in copies:
        copy.start()
    for copy in copies:
        copy.wait()


def local_hop(cols, rows, outer_ref, inner_ref, tile, matrix):
    refs = (outer_ref, inner_ref)
    row, col = divmod(tile, cols)

    def vectors(r, c):
        return refs[r][pl.ds(c * rows, rows), :]

    right, left = (col + 1) % cols, (col - 1) % cols
    total = product(vectors(1 - row, col), matrix(VERT, (1 - row) * cols + col))
    total += product(vectors(row, right), matrix(LEFT, row * cols + right))
    total += product(vectors(row, left), matrix(RIGHT, row * cols + left))
    return total


def kondo(vectors, twice_cos, twice_sin):
    half = vectors.shape[0] // 2
    upper, lower = vectors[:half], vectors[half:]
    return jnp.concatenate(
        [twice_cos * upper + twice_sin * lower, twice_sin * upper - twice_cos * lower], axis=0
    )


def first_body(cols, rows, probe_total, parity_ref, offsets_hbm, coef_hbm, raw_ref, angles_ref,
               coupling_ref, outer_ref, inner_ref, sorted_ref, part_ref, send_ref, pair_ref,
               terms_ref, weights_ref, cos_ref, sin_ref, same_ref, cross_ref,
               offsets_ref, coef_ref, sems):
    tiles = 2 * cols
    slots = offsets_ref.shape[2]
    steps = coef_ref.shape[0]
    parity = parity_ref[0]
    small = [
        pltpu.make_async_copy(offsets_hbm, offsets_ref, sems.at[0]),
        pltpu.make_async_copy(coef_hbm, coef_ref, sems.at[1]),
    ]
    for copy in small:
        copy.start()

    def tile_of(kind, tile):
        row, col = divmod(tile, cols)
        origin = row + parity - 2 * row * parity
        if kind == LEFT:
            code = 3
        elif kind == RIGHT:
            code = 5
        else:
            towards_high = (row == 0) == (kind == VERT)
            code = 7 - 6 * parity if towards_high else 1 + 6 * parity
        slot = jnp.int32(0)
        for k in range(1, slots):
            slot += jnp.where(offsets_ref[origin, col, k] == code, k, 0)
        return (origin * cols + col) * slots + slot

    for row in range(2):
        origin = row + parity - 2 * row * parity
        place = pl.ds(row * cols, cols)
        angles, strength = angles_ref[origin], coupling_ref[origin]
        cosines, sine_values = jnp.cos(angles), jnp.sin(angles)
        scale = (-BAND / probe_total) * strength
        cos_ref[place, :] = 2.0 * strength * cosines
        sin_ref[place, :] = 2.0 * strength * sine_values
        same_ref[place, :] = -scale * sine_values
        cross_ref[place, :] = scale * cosines
    for tile in range(tiles):
        row, col = divmod(tile, cols)
        probe = (outer_ref, inner_ref)[row][pl.ds(col * rows, rows), :]
        terms_ref[tile], terms_ref[tiles + tile] = overlap_terms(
            probe, probe.astype(jnp.float32)
        )
    pair_ref[pl.ds(0, cols * rows), :] = inner_ref[...]
    for copy in small:
        copy.wait()
    for level in range(steps):
        weights_ref[pl.ds(level, 1), :] = jnp.full(
            (1, weights_ref.shape[1]), (level + 1) * coef_ref[level], jnp.float32
        )

    def matrix(kind, tile):
        found = raw_ref[tile_of(kind, tile)]
        sorted_ref[kind * tiles + tile] = found
        return found

    for tile in range(tiles):
        row, col = divmod(tile, cols)
        probe = (outer_ref, inner_ref)[row][pl.ds(col * rows, rows), :].astype(jnp.float32)
        total = local_hop(cols, rows, outer_ref, inner_ref, tile, matrix)
        part = 2.0 * total + kondo(
            probe, cos_ref[pl.ds(tile, 1), :], sin_ref[pl.ds(tile, 1), :]
        )
        part_ref[tile] = part
        low = part.astype(jnp.bfloat16)
        if row == 0:
            send_ref[pl.ds(col * rows, rows), :] = low
        else:
            pair_ref[pl.ds((cols + col) * rows, rows), :] = low
    for tile in range(tiles):
        sorted_ref[TURNED * tiles + tile] = matrix(RIM, tile).T


def rim_vectors(cols, rows, tile, got, half, low, sorted_ref):
    row, col = divmod(tile, cols)
    place = pl.ds(col * rows, rows)
    sent = got[row][pl.ds((half * row * cols + col) * rows, rows), :]
    if low is None:
        return sent
    share = product(low[row][place, :], sorted_ref[RIM * 2 * cols + tile])
    return (sent.astype(jnp.float32) + 2.0 * share).astype(jnp.bfloat16)


def completed(cols, rows, tile, got, half, low, sorted_ref, part_ref):
    rim = rim_vectors(cols, rows, tile, got, half, low, sorted_ref)
    return part_ref[tile] + 2.0 * product(rim, sorted_ref[TURNED * 2 * cols + tile])


def outer_body(cols, rows, level, *refs):
    refs = list(refs)
    got = refs.pop(0), None
    low_before = (refs.pop(0), None) if level > 1 else None
    sorted_ref, part_ref, field_ref, low_ref = refs
    for col in range(cols):
        field = completed(cols, rows, col, got, 0, low_before, sorted_ref, part_ref)
        field_ref[col] = field
        low_ref[pl.ds(col * rows, rows), :] = field.astype(jnp.bfloat16)


def step_body(cols, rows, level, last, *refs):
    tiles = 2 * cols
    refs = list(refs)

    def take(count):
        taken = refs[:count]
        del refs[:count]
        return taken

    probes = take(2)
    got = [None] + take(1)
    low_before, field_before = ([None] + take(1), take(2)) if level > 1 else (None, None)
    sorted_ref, part_ref, terms_ref, weights_ref, cos_ref, sin_ref = take(6)
    field_outer, low_outer = take(2)
    if last:
        same_ref, cross_ref, share_ref, field_inner, low_inner = refs
    else:
        field_inner, low_inner, next_ref, out_ref, send_ref, *pair = refs
    fields, low = (field_outer, field_inner), (low_outer, low_inner)

    for col in range(cols):
        field = completed(
            cols, rows, cols + col, got, (level - 1) % 2, low_before, sorted_ref, part_ref
        )
        field_inner[col] = field
        low_inner[pl.ds(col * rows, rows), :] = field.astype(jnp.bfloat16)

    weight = weights_ref[pl.ds(level, 1), 0:1]
    weight_next = weights_ref[pl.ds(level + 1, 1), 0:1]

    def matrix(kind, source):
        return sorted_ref[kind * tiles + source]

    for tile in range(tiles):
        row, col = divmod(tile, cols)
        place = pl.ds(col * rows, rows)
        probe = probes[row][place, :]
        field = fields[row][col]
        total = local_hop(cols, rows, *low, tile, matrix)
        following = 2.0 * total + kondo(
            field, cos_ref[pl.ds(tile, 1), :], sin_ref[pl.ds(tile, 1), :]
        )
        if field_before is None:
            following -= probe.astype(jnp.float32)
        else:
            following -= field_before[row][col]
        if last:
            same, cross = overlap_terms(probe, weight * field + weight_next * following)
            same = jnp.sum(terms_ref[tile] + same, axis=0, keepdims=True)
            cross = jnp.sum(terms_ref[tiles + tile] + cross, axis=0, keepdims=True)
            one = pl.ds(tile, 1)
            share_ref[one, :] = same_ref[one, :] * same + cross_ref[one, :] * cross
        else:
            next_ref[tile] = following
            if row == 0:
                send_ref[place, :] = following.astype(jnp.bfloat16)
            elif pair:
                pair[0][place, :] = part_ref[tile].astype(jnp.bfloat16)
                pair[0][pl.ds((cols + col) * rows, rows), :] = following.astype(jnp.bfloat16)
            same, cross = overlap_terms(probe, field)
            for at, term in ((tile, same), (tiles + tile, cross)):
                before = weights_ref[0:1, 0:1] * terms_ref[at] if level == 1 else terms_ref[at]
                out_ref[at] = before + weight * term


def last_body(cols, rows, level, probe_outer_ref, probe_inner_ref, got_outer_ref, got_inner_ref,
              low_outer_ref, low_inner_ref, sorted_ref, share_ref, weights_ref, same_ref,
              cross_ref, out_ref):
    tiles = 2 * cols
    weight = 2.0 * weights_ref[pl.ds(level, 1), 0:1]
    got, low = (got_outer_ref, got_inner_ref), (low_outer_ref, low_inner_ref)
    for tile in range(tiles):
        row, col = divmod(tile, cols)
        probe = (probe_outer_ref, probe_inner_ref)[row][pl.ds(col * rows, rows), :]
        rim = rim_vectors(cols, rows, tile, got, (level - 1) % 2, low, sorted_ref)
        same, cross = overlap_terms(probe, product(rim, sorted_ref[TURNED * tiles + tile]))
        same = weight * jnp.sum(same, axis=0, keepdims=True)
        cross = weight * jnp.sum(cross, axis=0, keepdims=True)
        one = pl.ds(tile, 1)
        share = share_ref[one, :] + same_ref[one, :] * same + cross_ref[one, :] * cross
        for peer in range(out_ref.shape[0]):
            out_ref[peer, one, :] = share


def force_body(upper_ref, shares_ref, force_ref, largest_ref):
    peers = shares_ref.shape[0] // 2
    strips = []
    for strip in range(2):
        total = shares_ref[strip * peers]
        for peer in range(1, peers):
            total += shares_ref[strip * peers + peer]
        strips.append(total)
    force_ref[...] = jnp.where(upper_ref[0] == 0, strips[0], strips[1])
    largest = jnp.max(jnp.maximum(jnp.abs(strips[0]), jnp.abs(strips[1])))
    largest_ref[...] = jnp.full(largest_ref.shape, largest, jnp.float32)


def move_body(parity_ref, largest_ref, force_ref, angles_ref, noise_ref, next_ref, out_ref):
    parity = parity_ref[0]
    cols = out_ref.shape[1]
    largest = jnp.max(largest_ref[...])
    step_size = jnp.full((1, 1), STEP_MAX, jnp.float32) / (largest + 1e-06)
    kick = jnp.sqrt(TWO_TEMP * step_size)
    for row in range(2):
        origin = row + parity - 2 * row * parity
        force = force_ref[pl.ds(row * cols, cols), :]
        out_ref[origin] = force
        next_ref[origin] = angles_ref[origin] + step_size * force + kick * noise_ref[origin]


def exchange_outer(outer):
    count = lax.axis_size("site")
    pairs = [(i, (i + 1) % count if i % 2 else (i - 1) % count) for i in range(count)]
    return lax.ppermute(outer, "site", pairs)


def exchange_inner(inner):
    return lax.ppermute(inner, "site", [(i, i ^ 1) for i in range(lax.axis_size("site"))])


def local(angles, coupling, thermal_noise, coefficients, probes, hopping, offsets):
    cols, orbitals, share, width = probes.shape[1:]
    rows = orbitals * share
    tiles = 2 * cols
    steps = coefficients.shape[0] - 1
    f32, bf16 = jnp.float32, jnp.bfloat16
    side = ((cols * rows, width), bf16)
    whole = ((tiles, rows, width), f32)
    terms_like = ((2 * tiles, 8, width), f32)
    probe_total = lax.axis_size("probe") * share

    pair = ((2 * cols * rows, width), bf16)
    row_like = ((tiles, width), f32)
    sites, peers = lax.axis_size("site"), lax.axis_size("probe")
    site = lax.axis_index("site")
    parity = (site % 2).astype(jnp.int32).reshape(1)
    upper = (site // (sites // 2)).astype(jnp.int32).reshape(1)
    raw = hopping.reshape(-1, width, width)
    outer, inner, angles_held, coupling_held, raw_held = call(
        functools.partial(fetch_body, rows),
        [side, side, (angles.shape, f32), (coupling.shape, f32), (raw.shape, bf16)],
        [IN_SMEM] + [IN_HBM] * 4,
        (parity, *(held(x, pltpu.HBM) for x in (
            probes.reshape(2, cols * rows, width), angles, coupling, raw))),
        scratch=[pltpu.SemaphoreType.DMA((5,))],
    )
    probe_rows = [outer, inner]
    from_outer = [exchange_outer(outer)]

    local_flops = 2 * 3 * tiles * rows * width * width
    (sorted_hop, part, send, send_pair, terms, weights, twice_cos, twice_sin, same_factor,
     cross_factor) = call(
        functools.partial(first_body, cols, rows, probe_total),
        [((5 * tiles, width, width), bf16), whole, side, pair, terms_like, ((8, 128), f32)]
        + [row_like] * 4,
        [IN_SMEM] + [IN_HBM] * 2 + [IN_VMEM] * 5,
        (parity, *(held(x, pltpu.HBM) for x in (offsets, coefficients)),
         *(held(x) for x in (raw_held, angles_held, coupling_held, outer, inner))),
        scratch=[
            pltpu.SMEM(offsets.shape, jnp.int32), pltpu.SMEM(coefficients.shape, f32),
            pltpu.SemaphoreType.DMA((2,)),
        ],
        flops=local_flops, moved=hopping.size * 2,
    )
    from_outer.append(exchange_outer(send))
    from_inner = exchange_inner(send_pair)
    rows_of, fields = [probe_rows], None
    row_whole = ((cols, rows, width), f32)
    for level in range(1, steps):
        last = level == steps - 1
        paired = level % 2 == 0
        before = level > 1
        args = [from_outer[level - 1]] + [rows_of[level - 2][0]] * before + [sorted_hop, part]
        field_outer, low_outer = call(
            functools.partial(outer_body, cols, rows, level), [row_whole, side],
            [IN_VMEM] * len(args), tuple(held(x) for x in args),
            flops=0 if paired else 20 * local_flops,
        )
        args = [*probe_rows, from_inner]
        if before:
            args += [rows_of[level - 2][1], *fields]
        args += [sorted_hop, part, terms, weights, twice_cos, twice_sin, field_outer, low_outer]
        if last:
            args += [same_factor, cross_factor]
        outs = call(
            functools.partial(step_body, cols, rows, level, last),
            [row_like] if last else [row_whole, side, whole, terms_like, side] + [pair] * paired,
            [IN_VMEM] * len(args), tuple(held(x) for x in args),
            scratch=[pltpu.VMEM(*row_whole), pltpu.VMEM(*side)] if last else (),
            flops=0 if paired else local_flops,
        )
        if last:
            share = outs[0]
        else:
            field_inner, low_inner, part, terms, send, *send_pair = outs
            fields = field_outer, field_inner
            rows_of.append((low_outer, low_inner))
            from_outer.append(exchange_outer(send))
            if paired:
                from_inner = exchange_inner(send_pair[0])

    args = [*probe_rows, from_outer[steps - 1], from_inner, *rows_of[steps - 2], sorted_hop,
            share, weights, same_factor, cross_factor]
    pairs = [
        [half * peers + peer for half in (i, i + sites // 2) for peer in range(peers)]
        for i in range(sites // 2)
    ]
    shares = call(
        functools.partial(last_body, cols, rows, steps), [((2 * peers, tiles, width), f32)],
        [IN_VMEM] * len(args), tuple(held(x) for x in args), flops=local_flops,
    )[0]
    shares = lax.all_to_all(shares, ("site", "probe"), 0, 0, axis_index_groups=pairs)
    force, largest = call(
        force_body, [row_like, ((sites // 2, 1, 128), f32)],
        [IN_SMEM, IN_VMEM], (upper, held(shares)),
    )
    halves = [list(range(sites // 2)), list(range(sites // 2, sites))]
    largest = lax.all_to_all(largest, "site", 0, 0, axis_index_groups=halves)
    return pl.pallas_call(
        move_body,
        out_shape=[jax.ShapeDtypeStruct(angles.shape, f32)] * 2,
        in_specs=[IN_SMEM] + [IN_VMEM] * 4,
        out_specs=[IN_VMEM] * 2,
    )(parity, held(largest), held(force), held(angles), held(thermal_noise))


def solution(mesh):
    in_specs = (
        P("site", None, None),
        P("site", None, None),
        P("site", None, None),
        P(),
        P("site", None, None, "probe", None),
        P("site", None, None, None, None),
        P("site", None, None),
    )
    out_specs = (P("site", None, None), P("site", None, None))
    return jax.shard_map(local, mesh=mesh, in_specs=in_specs, out_specs=out_specs, check_vma=False)
```

time: 84.9 us -> 76.7 us (0.903)
  blocking collectives: 34.9 us -> 20.7 us
  waiting for transfers between devices: 0.68 us -> 9.18 us
  starting transfers between devices: 39.1 us -> 34.9 us
  Pallas kernels: 8.91 us -> 10.7 us
    all_to_all x2 -> x1, blocking collectives: 34.9 us -> 20.7 us  [local(): largest = lax.all_to_all(largest, 'site', 0, 0, axis_index_groups=halves)]
    ppermute x4 -> x2, starting transfers between devices: 30.3 us -> 17.8 us  [exchange_inner(): lax.ppermute(inner, 'site', [(i, i ^ 1) for i in range(lax.axis_size('sit...]
    all_to_all x0 -> x1, waiting for transfers between devices: none -> 6.83 us  [local(): lax.all_to_all(shares, ('site', 'probe'), 0, 0, axis_index_groups=pairs)]
    all_to_all x0 -> x1, starting transfers between devices: none -> 4.62 us  [local(): lax.all_to_all(shares, ('site', 'probe'), 0, 0, axis_index_groups=pairs)]
    ppermute x3 -> x4, starting transfers between devices: 8.78 us -> 12.4 us  [exchange_outer(): return lax.ppermute(outer, 'site', pairs)]
    pallas_call x10, Pallas kernels: 8.16 us -> 9.91 us  [call(): pl.pallas_call(body, out_shape=[pltpu.VMEM(shape, dtype) for shape, dtype...]
    ppermute x4 -> x2, waiting for transfers between devices: 0.67 us -> 2.35 us  [exchange_inner(): lax.ppermute(inner, 'site', [(i, i ^ 1) for i in range(lax.axis_size('sit...]
  transfers between devices with their start and end apart: 7 -> 7, of which waited for: 2 -> 3; matrix products, arithmetic and copies ran while one was open for 0% -> 0% of each run, Pallas kernels for 7% -> 8%
where the time goes in v3:
time: 76.7 us; the launch traced here: 76.3 us
  starting transfers between devices  34.9 us (46%)
  blocking collectives  20.7 us (27%)
  Pallas kernels  10.7 us (14%)
  waiting for transfers between devices  9.18 us (12%)
  between operations  0.83 us (1%)
    all_to_all x1, blocking collectives, local(): largest = lax.all_to_all(largest, 'site', 0, 0, axis_index_groups=halves)  20.7 us
    ppermute x2, starting transfers between devices, exchange_inner(): lax.ppermute(inner, 'site', [(i, i ^ 1) for i in range(lax.axis_size('sit...  17.8 us
    ppermute x4, starting transfers between devices, exchange_outer(): return lax.ppermute(outer, 'site', pairs)  12.4 us
    pallas_call x10, Pallas kernels, call(): pl.pallas_call(body, out_shape=[pltpu.VMEM(shape, dtype) for shape, dtype...  9.91 us
    all_to_all x1, waiting for transfers between devices, local(): lax.all_to_all(shares, ('site', 'probe'), 0, 0, axis_index_groups=pairs)  6.83 us
    all_to_all x1, starting transfers between devices, local(): lax.all_to_all(shares, ('site', 'probe'), 0, 0, axis_index_groups=pairs)  4.62 us
    ppermute x2, waiting for transfers between devices, exchange_inner(): lax.ppermute(inner, 'site', [(i, i ^ 1) for i in range(lax.axis_size('sit...  2.35 us
  transfers between devices with their start and end apart: 7, of which 3 were waited for; matrix products, arithmetic and copies ran while one was open for 0% of the time, Pallas kernels for 8%

profile of v3, /device:TPU:1, one launch (start us, length us, event | category | flops | bytes accessed | tf_op | source)
XLA Modules:
  0.0 76.3 jit_solution(2693309107315663673)
XLA Ops:
  0.6 2.4 %shard_map.86 = (bf16[512,256]{1,0:T(8,128)(2,1)S(1)}, bf16[512,256]{1,0:T(8,128)(2,1)S(1)}, f32[2,4,256]{2,1,0:T(4,128)S(1)}, f32[2,4,256]{2,1,0:T(4,128)S(1)}, bf16[32,256,256]{2,1,0:T(8,128)(2,1)S(1)}) custom-call(s32[1]{0:T(128)} %bitcast.parity_ref, bf16[2,512,256]{2,1,0:T(8,128)(2,1)} %bitcast.5, f32[2,4,256]{2,1,0:T(4,128)} %angles_ref.1, ...), custom_call_target="tpu_custom_call" | custom-call | tf_op jit(solution)/shard_map/pallas_call | solution.py:24
  3.1 4.9 %collective-permute-start.1 = (bf16[512,256]{1,0:T(8,128)(2,1)S(1)}, bf16[512,256]{1,0:T(8,128)(2,1)S(1)}, u32[]{:S(2)}, u32[]{:S(2)}) collective-permute-start(bf16[512,256]{1,0:T(8,128)(2,1)S(1)} %get-tuple-element.36.outer_ref.refs_0_.refs_1_.probe_outer_ref), channel_id=1, source_target_pairs={{0,504},{8,16},{16,8},{24,32},{32,24},{40,48},{48,40},{56,64},{64,... | collective-permute-start | bytes 786440 | tf_op jit(solution)/shard_map/ppermute | solution.py:309
  8.0 1.8 %shard_map.87 = (bf16[40,256,256]{2,1,0:T(8,128)(2,1)S(1)}, f32[8,128,256]{2,1,0:T(8,128)S(1)}, bf16[512,256]{1,0:T(8,128)(2,1)S(1)}, bf16[1024,256]{1,0:T(8,128...) custom-call(s32[1]{0:T(128)} %bitcast.parity_ref, ...), custom_call_target="tpu_custom_call" | custom-call | flops 402653184 | bytes 4194304 | tf_op jit(solution)/shard_map/pallas_call | solution.py:24
  9.8 1.9 %collective-permute-start.2 = (bf16[512,256]{1,0:T(8,128)(2,1)S(1)}, bf16[512,256]{1,0:T(8,128)(2,1)S(1)}, u32[]{:S(2)}, u32[]{:S(2)}) collective-permute-start(bf16[512,256]{1,0:T(8,128)(2,1)S(1)} %get-tuple-element.53), channel_id=1, source_target_pairs={{0,504},{8,16},{16,8},{24,32},{32,24},{40,48},{48,40},{56,64},{64,... | collective-permute-start | bytes 786440 | tf_op jit(solution)/shard_map/ppermute | solution.py:309
  11.8 12.0 %collective-permute-start = (bf16[1024,256]{1,0:T(8,128)(2,1)S(1)}, bf16[1024,256]{1,0:T(8,128)(2,1)S(1)}, u32[]{:S(2)}, u32[]{:S(2)}) collective-permute-start(bf16[1024,256]{1,0:T(8,128)(2,1)S(1)} %get-tuple-element.41), channel_id=1, source_target_pairs={{0,8},{8,0},{16,24},{24,16},{32,40},{40,32},{48,56},{56,48},{64,72... | collective-permute-start | bytes 1572872 | tf_op jit(solution)/shard_map/ppermute | solution.py:313
  23.7 0.0 collective-permute-done.1.refs_0_
  23.7 0.2 shard_map.88
  24.0 1.3 %collective-permute-done.refs_2_ = bf16[1024,256]{1,0:T(8,128)(2,1)S(1)} collective-permute-done((bf16[1024,256]{1,0:T(8,128)(2,1)S(1)}, bf16[1024,256]{1,0:T(8,128)(2,1)S(1)}, u32[]{:S(2)}, u32[]{:S(2)}) %collective-permute-start) | collective-permute-done | bytes 524320 | tf_op jit(solution)/shard_map/ppermute | solution.py:313
  25.2 1.1 %shard_map.89 = (f32[4,128,256]{2,1,0:T(8,128)S(1)}, bf16[512,256]{1,0:T(8,128)(2,1)S(1)}, f32[8,128,256]{2,1,0:T(8,128)S(1)}, f32[16,8,256]{2,1,0:T(8,128)S(1)}, bf16[512,256]{1,0:T(8,128)(2,1)S(1)}) custom-call(bf16[512,256]{1,0:T(8,128)(2,1)S(1)} %get-tuple-element.36.outer_ref.refs_0_.refs_1_.probe_outer_ref, ...), custom_call_target="tpu_custom_call" | custom-call | flops 402653184 | tf_op jit(solution)/shard_map/pallas_call | solution.py:24
  26.3 1.9 %collective-permute-start.5 = (bf16[512,256]{1,0:T(8,128)(2,1)S(1)}, bf16[512,256]{1,0:T(8,128)(2,1)S(1)}, u32[]{:S(2)}, u32[]{:S(2)}) collective-permute-start(bf16[512,256]{1,0:T(8,128)(2,1)S(1)} %get-tuple-element.63), channel_id=1, source_target_pairs={{0,504},{8,16},{16,8},{24,32},{32,24},{40,48},{48,40},{56,64},{64,... | collective-permute-start | bytes 786440 | tf_op jit(solution)/shard_map/ppermute | solution.py:309
  28.2 0.0 collective-permute-done.2.refs_0_
  28.2 0.4 shard_map.90
  28.6 1.0 %shard_map.91 = (f32[4,128,256]{2,1,0:T(8,128)S(1)}, bf16[512,256]{1,0:T(8,128)(2,1)S(1)}, f32[8,128,256]{2,1,0:T(8,128)S(1)}, f32[16,8,256]{2,1,0:T(8,128)S(1)}...) custom-call(bf16[512,256]{1,0:T(8,128)(2,1)S(1)} %get-tuple-element.36.outer_ref.refs_0_.refs_1_.probe_outer_ref, ...), custom_call_target="tpu_custom_call" | custom-call | tf_op jit(solution)/shard_map/pallas_call | solution.py:24
  29.6 3.6 %collective-permute-start.3 = (bf16[512,256]{1,0:T(8,128)(2,1)S(1)}, bf16[512,256]{1,0:T(8,128)(2,1)S(1)}, u32[]{:S(2)}, u32[]{:S(2)}) collective-permute-start(bf16[512,256]{1,0:T(8,128)(2,1)S(1)} %get-tuple-element.56), channel_id=1, source_target_pairs={{0,504},{8,16},{16,8},{24,32},{32,24},{40,48},{48,40},{56,64},{64,... | collective-permute-start | bytes 786440 | tf_op jit(solution)/shard_map/ppermute | solution.py:309
  33.3 5.9 %collective-permute-start.4 = (bf16[1024,256]{1,0:T(8,128)(2,1)S(1)}, bf16[1024,256]{1,0:T(8,128)(2,1)S(1)}, u32[]{:S(2)}, u32[]{:S(2)}) collective-permute-start(bf16[1024,256]{1,0:T(8,128)(2,1)S(1)} %get-tuple-element.57), channel_id=1, source_target_pairs={{0,8},{8,0},{16,24},{24,16},{32,40},{40,32},{48,56},{56,48},{64,72... | collective-permute-start | bytes 1572872 | tf_op jit(solution)/shard_map/ppermute | solution.py:313
  39.2 0.0 collective-permute-done.5.refs_0_
  39.2 0.4 shard_map.92
  39.6 1.1 %collective-permute-done.4.refs_2_.got_inner_ref = bf16[1024,256]{1,0:T(8,128)(2,1)S(1)} collective-permute-done((bf16[1024,256]{1,0:T(8,128)(2,1)S(1)}, bf16[1024,256]{1,0:T(8,128)(2,1)S(1)}, u32[]{:S(2)}, u32[]{:S(2)}) %collective-permute-start.4) | collective-permute-done | bytes 524320 | tf_op jit(solution)/shard_map/ppermute | solution.py:313
  40.7 1.1 %shard_map.93.share_ref = f32[8,256]{1,0:T(8,128)S(1)} custom-call(bf16[512,256]{1,0:T(8,128)(2,1)S(1)} %get-tuple-element.36.outer_ref.refs_0_.refs_1_.probe_outer_ref, bf16[512,256]{1,0:T(8,128)(2,1)S(1)} %get-tuple-element.37.inner_ref.refs_1_.refs_3_.probe_inner_ref, bf16[1024,256]{1,0:T(8,128)(2,1)S(1)} %collective-permute-done.4.refs_2_.got_inner_ref, ...), custom_call_target="tpu_custom_call" | custom-call | flops 402653184 | tf_op jit(solution)/shard_map/pallas_call | solution.py:24
  41.8 0.0 copy-start
  41.9 0.0 copy-start.1
  41.9 0.0 collective-permute-done.3.got_outer_ref
  41.9 1.3 %shard_map.94 = f32[16,8,256]{2,1,0:T(8,128)} custom-call(bf16[512,256]{1,0:T(8,128)(2,1)S(1)} %get-tuple-element.36.outer_ref.refs_0_.refs_1_.probe_outer_ref, bf16[512,256]{1,0:T(8,128)(2,1)S(1)} %get-tuple-element.37.inner_ref.refs_1_.refs_3_.probe_inner_ref, bf16[512,256]{1,0:T(8,128)(2,1)S(1)} %collective-permute-done.3.got_outer_ref, ...), custom_call_target="tpu_custom_call" | custom-call | flops 402653184 | tf_op jit(solution)/shard_map/pallas_call | solution.py:24
  43.2 4.6 %all-to-all-start = ((f32[16,8,256]{2,1,0:T(8,128)}), f32[16,8,256]{2,1,0:T(8,128)S(1)}, u32[]{:S(2)}, u32[]{:S(2)}) async-start(f32[16,8,256]{2,1,0:T(8,128)} %shard_map.94), calls=%async_computation | async-start | bytes 262144 | tf_op jit(solution)/shard_map/all_to_all | solution.py:407
  47.8 6.8 %all-to-all-done.shares_ref = f32[16,8,256]{2,1,0:T(8,128)S(1)} async-done(((f32[16,8,256]{2,1,0:T(8,128)}), f32[16,8,256]{2,1,0:T(8,128)S(1)}, u32[]{:S(2)}, u32[]{:S(2)}) %all-to-all-start) | async-done | bytes 131104 | tf_op jit(solution)/shard_map/all_to_all | solution.py:407
  54.7 0.1 shard_map.95
  54.8 20.7 %all_to_all.10.largest_ref = f32[32,1,128]{2,1,0:T(1,128)S(1)} all-to-all(f32[32,1,128]{2,1,0:T(1,128)S(1)} %get-tuple-element.68), channel_id=1, replica_groups={{0,8,16,24,32,40,48,56,64,72,80,88,96,104,112,120,128,136,144,152,160,1..., dimensions={0} | all-to-all | bytes 32768 | tf_op jit(solution)/shard_map/all_to_all | solution.py:413
  75.5 0.0 copy-done
  75.5 0.0 copy-done.1
  75.5 0.7 shard_map.96
Async XLA Ops:
  3.1 20.6 %collective-permute-start.1 = (bf16[512,256]{1,0:T(8,128)(2,1)S(1)}, bf16[512,256]{1,0:T(8,128)(2,1)S(1)}, u32[]{:S(2)}, u32[]{:S(2)}) collective-permute-start(bf16[512,256]{1,0:T(8,128)(2,1)S(1)} %get-tuple-element.36.outer_ref.refs_0_.refs_1_.probe_outer_ref), channel_id=1, source_target_pairs={{0,504},{8,16},{16,8},{24,32},{32,24},{40,48},{48,40},{56,64},{64,... | collective-permute-start | bytes 786440 | tf_op jit(solution)/shard_map/ppermute | solution.py:309
  9.8 18.4 %collective-permute-start.2 = (bf16[512,256]{1,0:T(8,128)(2,1)S(1)}, bf16[512,256]{1,0:T(8,128)(2,1)S(1)}, u32[]{:S(2)}, u32[]{:S(2)}) collective-permute-start(bf16[512,256]{1,0:T(8,128)(2,1)S(1)} %get-tuple-element.53), channel_id=1, source_target_pairs={{0,504},{8,16},{16,8},{24,32},{32,24},{40,48},{48,40},{56,64},{64,... | collective-permute-start | bytes 786440 | tf_op jit(solution)/shard_map/ppermute | solution.py:309
  11.8 13.5 %collective-permute-start = (bf16[1024,256]{1,0:T(8,128)(2,1)S(1)}, bf16[1024,256]{1,0:T(8,128)(2,1)S(1)}, u32[]{:S(2)}, u32[]{:S(2)}) collective-permute-start(bf16[1024,256]{1,0:T(8,128)(2,1)S(1)} %get-tuple-element.41), channel_id=1, source_target_pairs={{0,8},{8,0},{16,24},{24,16},{32,40},{40,32},{48,56},{56,48},{64,72... | collective-permute-start | bytes 1572872 | tf_op jit(solution)/shard_map/ppermute | solution.py:313
  26.3 12.9 %collective-permute-start.5 = (bf16[512,256]{1,0:T(8,128)(2,1)S(1)}, bf16[512,256]{1,0:T(8,128)(2,1)S(1)}, u32[]{:S(2)}, u32[]{:S(2)}) collective-permute-start(bf16[512,256]{1,0:T(8,128)(2,1)S(1)} %get-tuple-element.63), channel_id=1, source_target_pairs={{0,504},{8,16},{16,8},{24,32},{32,24},{40,48},{48,40},{56,64},{64,... | collective-permute-start | bytes 786440 | tf_op jit(solution)/shard_map/ppermute | solution.py:309
  29.6 12.2 %collective-permute-start.3 = (bf16[512,256]{1,0:T(8,128)(2,1)S(1)}, bf16[512,256]{1,0:T(8,128)(2,1)S(1)}, u32[]{:S(2)}, u32[]{:S(2)}) collective-permute-start(bf16[512,256]{1,0:T(8,128)(2,1)S(1)} %get-tuple-element.56), channel_id=1, source_target_pairs={{0,504},{8,16},{16,8},{24,32},{32,24},{40,48},{48,40},{56,64},{64,... | collective-permute-start | bytes 786440 | tf_op jit(solution)/shard_map/ppermute | solution.py:309
  33.3 7.4 %collective-permute-start.4 = (bf16[1024,256]{1,0:T(8,128)(2,1)S(1)}, bf16[1024,256]{1,0:T(8,128)(2,1)S(1)}, u32[]{:S(2)}, u32[]{:S(2)}) collective-permute-start(bf16[1024,256]{1,0:T(8,128)(2,1)S(1)} %get-tuple-element.57), channel_id=1, source_target_pairs={{0,8},{8,0},{16,24},{24,16},{32,40},{40,32},{48,56},{56,48},{64,72... | collective-permute-start | bytes 1572872 | tf_op jit(solution)/shard_map/ppermute | solution.py:313
  41.8 33.7 %copy-start = (f32[2,4,256]{2,1,0:T(4,128)S(1)}, f32[2,4,256]{2,1,0:T(4,128)}, u32[]{:S(2)}) copy-start(f32[2,4,256]{2,1,0:T(4,128)} %angles_ref.1) | copy-start | bytes 24580
  41.9 33.6 %copy-start.1 = (f32[2,4,256]{2,1,0:T(4,128)S(1)}, f32[2,4,256]{2,1,0:T(4,128)}, u32[]{:S(2)}) copy-start(f32[2,4,256]{2,1,0:T(4,128)} %noise_ref.1) | copy-start | bytes 24580
  43.2 11.5 %all-to-all-start = ((f32[16,8,256]{2,1,0:T(8,128)}), f32[16,8,256]{2,1,0:T(8,128)S(1)}, u32[]{:S(2)}, u32[]{:S(2)}) async-start(f32[16,8,256]{2,1,0:T(8,128)} %shard_map.94), calls=%async_computation | async-start | bytes 262144 | tf_op jit(solution)/shard_map/all_to_all | solution.py:407

commit v4 on v3

--- a/solution.py
+++ b/solution.py
@@ -50,8 +50,8 @@
     return same, cross
 
 
-def fetch_body(rows, parity_ref, probes_hbm, angles_hbm, coupling_hbm, hopping_hbm,
-               outer_ref, inner_ref, angles_ref, coupling_ref, raw_ref, sems):
+def fetch_body(parity_ref, probes_hbm, angles_hbm, coupling_hbm,
+               outer_ref, inner_ref, angles_ref, coupling_ref, sems):
     parity = parity_ref[0]
     copies = [
         pltpu.make_async_copy(source, target, sems.at[k])
@@ -60,7 +60,6 @@
             (probes_hbm.at[1 - parity], inner_ref),
             (angles_hbm, angles_ref),
             (coupling_hbm, coupling_ref),
-            (hopping_hbm, raw_ref),
         ))
     ]
     for copy in copies:
@@ -69,18 +68,21 @@
         copy.wait()
 
 
+def beside(cols, rows, low_ref, tile, matrix):
+    row, col = divmod(tile, cols)
+    right, left = (col + 1) % cols, (col - 1) % cols
+    return product(
+        low_ref[pl.ds(right * rows, rows), :], matrix(LEFT, row * cols + right)
+    ) + product(low_ref[pl.ds(left * rows, rows), :], matrix(RIGHT, row * cols + left))
+
+
 def local_hop(cols, rows, outer_ref, inner_ref, tile, matrix):
     refs = (outer_ref, inner_ref)
     row, col = divmod(tile, cols)
-
-    def vectors(r, c):
-        return refs[r][pl.ds(c * rows, rows), :]
-
-    right, left = (col + 1) % cols, (col - 1) % cols
-    total = product(vectors(1 - row, col), matrix(VERT, (1 - row) * cols + col))
-    total += product(vectors(row, right), matrix(LEFT, row * cols + right))
-    total += product(vectors(row, left), matrix(RIGHT, row * cols + left))
-    return total
+    total = product(
+        refs[1 - row][pl.ds(col * rows, rows), :], matrix(VERT, (1 - row) * cols + col)
+    )
+    return total + beside(cols, rows, refs[row], tile, matrix)
 
 
 def kondo(vectors, twice_cos, twice_sin):
@@ -193,7 +195,7 @@
         low_ref[pl.ds(col * rows, rows), :] = field.astype(jnp.bfloat16)
 
 
-def step_body(cols, rows, level, last, *refs):
+def step_body(cols, rows, level, *refs):
     tiles = 2 * cols
     refs = list(refs)
 
@@ -206,11 +208,7 @@
     got = [None] + take(1)
     low_before, field_before = ([None] + take(1), take(2)) if level > 1 else (None, None)
     sorted_ref, part_ref, terms_ref, weights_ref, cos_ref, sin_ref = take(6)
-    field_outer, low_outer = take(2)
-    if last:
-        same_ref, cross_ref, share_ref, field_inner, low_inner = refs
-    else:
-        field_inner, low_inner, next_ref, out_ref, send_ref, *pair = refs
+    field_outer, low_outer, field_inner, low_inner, next_ref, out_ref, send_inner, *pair = refs
     fields, low = (field_outer, field_inner), (low_outer, low_inner)
 
     for col in range(cols):
@@ -221,7 +219,6 @@
         low_inner[pl.ds(col * rows, rows), :] = field.astype(jnp.bfloat16)
 
     weight = weights_ref[pl.ds(level, 1), 0:1]
-    weight_next = weights_ref[pl.ds(level + 1, 1), 0:1]
 
     def matrix(kind, source):
         return sorted_ref[kind * tiles + source]
@@ -239,42 +236,101 @@
             following -= probe.astype(jnp.float32)
         else:
             following -= field_before[row][col]
-        if last:
-            same, cross = overlap_terms(probe, weight * field + weight_next * following)
-            same = jnp.sum(terms_ref[tile] + same, axis=0, keepdims=True)
-            cross = jnp.sum(terms_ref[tiles + tile] + cross, axis=0, keepdims=True)
-            one = pl.ds(tile, 1)
-            share_ref[one, :] = same_ref[one, :] * same + cross_ref[one, :] * cross
+        next_ref[tile] = following
+        if row == 1:
+            send_inner[place, :] = following.astype(jnp.bfloat16)
+        elif pair:
+            pair[0][place, :] = part_ref[tile].astype(jnp.bfloat16)
+            pair[0][pl.ds((cols + col) * rows, rows), :] = following.astype(jnp.bfloat16)
+        same, cross = overlap_terms(probe, field)
+        for at, term in ((tile, same), (tiles + tile, cross)):
+            before = weights_ref[0:1, 0:1] * terms_ref[at] if level == 1 else terms_ref[at]
+            out_ref[at] = before + weight * term
+
+
+def inner_last_body(cols, rows, level, probe_outer, probe_inner, got_2, got_1, low_2_outer,
+                    low_2_inner, low_1_outer, low_1_inner, field_outer, field_inner,
+                    sorted_ref, part_ref, terms_ref, weights_ref, cos_ref, sin_ref,
+                    out_ref, halo_2_ref, halo_1_ref, low_ref):
+    tiles = 2 * cols
+    weight = weights_ref[pl.ds(level, 1), 0:1]
+    weight_next = weights_ref[pl.ds(level + 1, 1), 0:1]
+
+    def matrix(kind, tile):
+        return sorted_ref[kind * tiles + tile]
+
+    fields = []
+    for col in range(cols):
+        field = completed(
+            cols, rows, cols + col, (None, got_2), 0, (None, low_2_inner), sorted_ref, part_ref
+        )
+        fields.append(field)
+        low_ref[pl.ds(col * rows, rows), :] = field.astype(jnp.bfloat16)
+    for tile in range(tiles):
+        row, col = divmod(tile, cols)
+        place = pl.ds(col * rows, rows)
+        if row == 0:
+            following = 2.0 * product(low_ref[place, :], matrix(VERT, cols + col))
+            vectors = weight_next * (following - field_outer[col])
+            probe = probe_outer[place, :]
         else:
-            next_ref[tile] = following
-            if row == 0:
-                send_ref[place, :] = following.astype(jnp.bfloat16)
-            elif pair:
-                pair[0][place, :] = part_ref[tile].astype(jnp.bfloat16)
-                pair[0][pl.ds((cols + col) * rows, rows), :] = following.astype(jnp.bfloat16)
-            same, cross = overlap_terms(probe, field)
-            for at, term in ((tile, same), (tiles + tile, cross)):
-                before = weights_ref[0:1, 0:1] * terms_ref[at] if level == 1 else terms_ref[at]
-                out_ref[at] = before + weight * term
-
-
-def last_body(cols, rows, level, probe_outer_ref, probe_inner_ref, got_outer_ref, got_inner_ref,
-              low_outer_ref, low_inner_ref, sorted_ref, share_ref, weights_ref, same_ref,
-              cross_ref, out_ref):
+            rim = rim_vectors(
+                cols, rows, tile, (None, got_1), 0, (None, low_1_inner), sorted_ref
+            )
+            total = beside(cols, rows, low_ref, tile, matrix) + product(rim, matrix(TURNED, tile))
+            following = 2.0 * total - field_inner[col] + kondo(
+                fields[col], cos_ref[pl.ds(tile, 1), :], sin_ref[pl.ds(tile, 1), :]
+            )
+            vectors = weight * fields[col] + weight_next * following
+            probe = probe_inner[place, :]
+        same, cross = overlap_terms(probe, vectors)
+        out_ref[tile] = terms_ref[tile] + same
+        out_ref[tiles + tile] = terms_ref[tiles + tile] + cross
+    for col in range(cols):
+        place = pl.ds(col * rows, rows)
+        halo_2_ref[col] = 2.0 * product(low_2_outer[place, :], matrix(RIM, col))
+        halo_1_ref[col] = 2.0 * product(low_1_outer[place, :], matrix(RIM, col))
+
+
+def outer_last_body(cols, rows, level, probe_outer, probe_inner, got_ref, halo_2_ref, halo_1_ref,
+                    sorted_ref, part_ref, terms_ref, weights_ref, cos_ref, sin_ref, same_ref,
+                    cross_ref, out_ref, low_ref, share_ref):
     tiles = 2 * cols
-    weight = 2.0 * weights_ref[pl.ds(level, 1), 0:1]
-    got, low = (got_outer_ref, got_inner_ref), (low_outer_ref, low_inner_ref)
-    for tile in range(tiles):
-        row, col = divmod(tile, cols)
-        probe = (probe_outer_ref, probe_inner_ref)[row][pl.ds(col * rows, rows), :]
-        rim = rim_vectors(cols, rows, tile, got, (level - 1) % 2, low, sorted_ref)
-        same, cross = overlap_terms(probe, product(rim, sorted_ref[TURNED * tiles + tile]))
-        same = weight * jnp.sum(same, axis=0, keepdims=True)
-        cross = weight * jnp.sum(cross, axis=0, keepdims=True)
+    weight = weights_ref[pl.ds(level, 1), 0:1]
+    weight_next = weights_ref[pl.ds(level + 1, 1), 0:1]
+
+    def matrix(kind, tile):
+        return sorted_ref[kind * tiles + tile]
+
+    def halo(half, share_ref, col):
+        sent = got_ref[pl.ds((half * cols + col) * rows, rows), :].astype(jnp.float32)
+        return (sent + share_ref[col]).astype(jnp.bfloat16)
+
+    fields = []
+    for col in range(cols):
+        field = part_ref[col] + 2.0 * product(halo(0, halo_2_ref, col), matrix(TURNED, col))
+        fields.append(field)
+        low_ref[pl.ds(col * rows, rows), :] = field.astype(jnp.bfloat16)
+    for tile in range(tiles):
+        row, col = divmod(tile, cols)
+        place = pl.ds(col * rows, rows)
         one = pl.ds(tile, 1)
-        share = share_ref[one, :] + same_ref[one, :] * same + cross_ref[one, :] * cross
-        for peer in range(out_ref.shape[0]):
-            out_ref[peer, one, :] = share
+        if row == 0:
+            total = beside(cols, rows, low_ref, tile, matrix)
+            total += product(halo(1, halo_1_ref, col), matrix(TURNED, tile))
+            following = 2.0 * total + kondo(fields[col], cos_ref[one, :], sin_ref[one, :])
+            vectors = weight * fields[col] + weight_next * following
+            probe = probe_outer[place, :]
+        else:
+            vectors = (2.0 * weight_next) * product(low_ref[place, :], matrix(VERT, col))
+            probe = probe_inner[place, :]
+        same, cross = overlap_terms(probe, vectors)
+        same = jnp.sum(terms_ref[tile] + same, axis=0, keepdims=True)
+        cross = jnp.sum(terms_ref[tiles + tile] + cross, axis=0, keepdims=True)
+        share_ref[one, :] = same_ref[one, :] * same + cross_ref[one, :] * cross
+    share = share_ref[...]
+    for peer in range(out_ref.shape[0]):
+        out_ref[peer] = share
 
 
 def force_body(upper_ref, shares_ref, force_ref, largest_ref):
@@ -330,19 +386,17 @@
     site = lax.axis_index("site")
     parity = (site % 2).astype(jnp.int32).reshape(1)
     upper = (site // (sites // 2)).astype(jnp.int32).reshape(1)
-    raw = hopping.reshape(-1, width, width)
-    outer, inner, angles_held, coupling_held, raw_held = call(
-        functools.partial(fetch_body, rows),
-        [side, side, (angles.shape, f32), (coupling.shape, f32), (raw.shape, bf16)],
-        [IN_SMEM] + [IN_HBM] * 4,
+    local_flops = 2 * 3 * tiles * rows * width * width
+    outer, inner, angles_held, coupling_held = call(
+        fetch_body, [side, side, (angles.shape, f32), (coupling.shape, f32)],
+        [IN_SMEM] + [IN_HBM] * 3,
         (parity, *(held(x, pltpu.HBM) for x in (
-            probes.reshape(2, cols * rows, width), angles, coupling, raw))),
-        scratch=[pltpu.SemaphoreType.DMA((5,))],
+            probes.reshape(2, cols * rows, width), angles, coupling))),
+        scratch=[pltpu.SemaphoreType.DMA((4,))], flops=20 * local_flops,
     )
     probe_rows = [outer, inner]
     from_outer = [exchange_outer(outer)]
 
-    local_flops = 2 * 3 * tiles * rows * width * width
     (sorted_hop, part, send, send_pair, terms, weights, twice_cos, twice_sin, same_factor,
      cross_factor) = call(
         functools.partial(first_body, cols, rows, probe_total),
@@ -350,7 +404,7 @@
         + [row_like] * 4,
         [IN_SMEM] + [IN_HBM] * 2 + [IN_VMEM] * 5,
         (parity, *(held(x, pltpu.HBM) for x in (offsets, coefficients)),
-         *(held(x) for x in (raw_held, angles_held, coupling_held, outer, inner))),
+         *(held(x) for x in (hopping.reshape(-1, width, width), angles_held, coupling_held, outer, inner))),
         scratch=[
             pltpu.SMEM(offsets.shape, jnp.int32), pltpu.SMEM(coefficients.shape, f32),
             pltpu.SemaphoreType.DMA((2,)),
@@ -359,10 +413,9 @@
     )
     from_outer.append(exchange_outer(send))
     from_inner = exchange_inner(send_pair)
-    rows_of, fields = [probe_rows], None
+    rows_of, fields, later_inner = [probe_rows], None, []
     row_whole = ((cols, rows, width), f32)
-    for level in range(1, steps):
-        last = level == steps - 1
+    for level in range(1, steps - 1):
         paired = level % 2 == 0
         before = level > 1
         args = [from_outer[level - 1]] + [rows_of[level - 2][0]] * before + [sorted_hop, part]
@@ -375,35 +428,36 @@
         if before:
             args += [rows_of[level - 2][1], *fields]
         args += [sorted_hop, part, terms, weights, twice_cos, twice_sin, field_outer, low_outer]
-        if last:
-            args += [same_factor, cross_factor]
-        outs = call(
-            functools.partial(step_body, cols, rows, level, last),
-            [row_like] if last else [row_whole, side, whole, terms_like, side] + [pair] * paired,
-            [IN_VMEM] * len(args), tuple(held(x) for x in args),
-            scratch=[pltpu.VMEM(*row_whole), pltpu.VMEM(*side)] if last else (),
-            flops=0 if paired else local_flops,
-        )
-        if last:
-            share = outs[0]
-        else:
-            field_inner, low_inner, part, terms, send, *send_pair = outs
-            fields = field_outer, field_inner
-            rows_of.append((low_outer, low_inner))
-            from_outer.append(exchange_outer(send))
-            if paired:
-                from_inner = exchange_inner(send_pair[0])
-
-    args = [*probe_rows, from_outer[steps - 1], from_inner, *rows_of[steps - 2], sorted_hop,
-            share, weights, same_factor, cross_factor]
+        field_inner, low_inner, part, terms, send_inner, *send_pair = call(
+            functools.partial(step_body, cols, rows, level),
+            [row_whole, side, whole, terms_like, side] + [pair] * paired,
+            [IN_VMEM] * len(args), tuple(held(x) for x in args), flops=local_flops,
+        )
+        fields = field_outer, field_inner
+        rows_of.append((low_outer, low_inner))
+        if paired:
+            from_outer.append(exchange_outer(send_pair[0]))
+        later_inner.append(exchange_inner(send_inner))
+
+    level = steps - 1
+    args = [*probe_rows, *later_inner, *rows_of[level - 2], *rows_of[level - 1], *fields,
+            sorted_hop, part, terms, weights, twice_cos, twice_sin]
+    terms, halo_2, halo_1 = call(
+        functools.partial(inner_last_body, cols, rows, level), [terms_like, row_whole, row_whole],
+        [IN_VMEM] * len(args), tuple(held(x) for x in args),
+        scratch=[pltpu.VMEM(*side)],
+    )
+    args = [*probe_rows, from_outer[-1], halo_2, halo_1, sorted_hop, part, terms, weights,
+            twice_cos, twice_sin, same_factor, cross_factor]
+    shares = call(
+        functools.partial(outer_last_body, cols, rows, level), [((2 * peers, tiles, width), f32)],
+        [IN_VMEM] * len(args), tuple(held(x) for x in args),
+        scratch=[pltpu.VMEM(*side), pltpu.VMEM(*row_like)], flops=local_flops,
+    )[0]
     pairs = [
         [half * peers + peer for half in (i, i + sites // 2) for peer in range(peers)]
         for i in range(sites // 2)
     ]
-    shares = call(
-        functools.partial(last_body, cols, rows, steps), [((2 * peers, tiles, width), f32)],
-        [IN_VMEM] * len(args), tuple(held(x) for x in args), flops=local_flops,
-    )[0]
     shares = lax.all_to_all(shares, ("site", "probe"), 0, 0, axis_index_groups=pairs)
     force, largest = call(
         force_body, [row_like, ((sites // 2, 1, 128), f32)],

time: 76.7 us -> 75.9 us (0.990)
  Pallas kernels: 10.7 us -> 9.32 us
    ppermute x2 -> x3, starting transfers between devices: 17.8 us -> 21.5 us  [exchange_inner(): lax.ppermute(inner, 'site', [(i, i ^ 1) for i in range(lax.axis_size('sit...]
    ppermute x4 -> x3, starting transfers between devices: 12.4 us -> 8.91 us  [exchange_outer(): return lax.ppermute(outer, 'site', pairs)]
    pallas_call x10 -> x9, Pallas kernels: 9.91 us -> 8.57 us  [call(): pl.pallas_call(body, out_shape=[pltpu.VMEM(shape, dtype) for shape, dtype...]
    ppermute x2 -> x3, waiting for transfers between devices: 2.35 us -> 2.75 us  [exchange_inner(): lax.ppermute(inner, 'site', [(i, i ^ 1) for i in range(lax.axis_size('sit...]
  transfers between devices with their start and end apart: 7 -> 7, of which waited for: 3 -> 3; matrix products, arithmetic and copies ran while one was open for 0% -> 0% of each run, Pallas kernels for 8% -> 6%
where the time goes in v4:
time: 75.9 us; the launch traced here: 75.5 us
  starting transfers between devices  35 us (46%)
  blocking collectives  20.7 us (27%)
  waiting for transfers between devices  9.59 us (13%)
  Pallas kernels  9.32 us (12%)
  between operations  0.84 us (1%)
    ppermute x3, starting transfers between devices, exchange_inner(): lax.ppermute(inner, 'site', [(i, i ^ 1) for i in range(lax.axis_size('sit...  21.5 us
    all_to_all x1, blocking collectives, local(): largest = lax.all_to_all(largest, 'site', 0, 0, axis_index_groups=halves)  20.7 us
    ppermute x3, starting transfers between devices, exchange_outer(): return lax.ppermute(outer, 'site', pairs)  8.91 us
    pallas_call x9, Pallas kernels, call(): pl.pallas_call(body, out_shape=[pltpu.VMEM(shape, dtype) for shape, dtype...  8.57 us
    all_to_all x1, waiting for transfers between devices, local(): lax.all_to_all(shares, ('site', 'probe'), 0, 0, axis_index_groups=pairs)  6.83 us
    all_to_all x1, starting transfers between devices, local(): lax.all_to_all(shares, ('site', 'probe'), 0, 0, axis_index_groups=pairs)  4.62 us
    ppermute x3, waiting for transfers between devices, exchange_inner(): lax.ppermute(inner, 'site', [(i, i ^ 1) for i in range(lax.axis_size('sit...  2.75 us
  transfers between devices with their start and end apart: 7, of which 3 were waited for; matrix products, arithmetic and copies ran while one was open for 0% of the time, Pallas kernels for 6%

profile of v4, /device:TPU:1, one launch (start us, length us, event | category | flops | bytes accessed | tf_op | source)
XLA Modules:
  0.0 75.5 jit_solution(17968334717353841864)
XLA Ops:
  0.6 0.0 copy-start
  0.7 1.2 %shard_map.86 = (bf16[512,256]{1,0:T(8,128)(2,1)S(1)}, bf16[512,256]{1,0:T(8,128)(2,1)S(1)}, f32[2,4,256]{2,1,0:T(4,128)S(1)}, f32[2,4,256]{2,1,0:T(4,128)S(1)}) custom-call(s32[1]{0:T(128)} %bitcast.parity_ref, bf16[2,512,256]{2,1,0:T(8,128)(2,1)} %bitcast.5, f32[2,4,256]{2,1,0:T(4,128)} %angles_ref.1, f32[2,4,256]{2,1,0:T(4,128)} %coupling_hbm.1), custom_call_target="tpu_custom_call" | custom-call | flops 8053063680 | tf_op jit(solution)/shard_map/pallas_call | solution.py:24
  1.9 5.1 %collective-permute-start.1 = (bf16[512,256]{1,0:T(8,128)(2,1)S(1)}, bf16[512,256]{1,0:T(8,128)(2,1)S(1)}, u32[]{:S(2)}, u32[]{:S(2)}) collective-permute-start(bf16[512,256]{1,0:T(8,128)(2,1)S(1)} %get-tuple-element.36.outer_ref.refs_0_.refs_1_.probe_outer), channel_id=1, source_target_pairs={{0,504},{8,16},{16,8},{24,32},{32,24},{40,48},{48,40},{56,64},{64,... | collective-permute-start | bytes 786440 | tf_op jit(solution)/shard_map/ppermute | solution.py:365
  7.0 0.0 copy-done
  7.0 1.8 %shard_map.87 = (bf16[40,256,256]{2,1,0:T(8,128)(2,1)S(1)}, f32[8,128,256]{2,1,0:T(8,128)S(1)}, bf16[512,256]{1,0:T(8,128)(2,1)S(1)}, bf16[1024,256]{1,0:T(8,128...) custom-call(s32[1]{0:T(128)} %bitcast.parity_ref, ...), custom_call_target="tpu_custom_call" | custom-call | flops 402653184 | bytes 4194304 | tf_op jit(solution)/shard_map/pallas_call | solution.py:24
  8.8 1.9 %collective-permute-start.2 = (bf16[512,256]{1,0:T(8,128)(2,1)S(1)}, bf16[512,256]{1,0:T(8,128)(2,1)S(1)}, u32[]{:S(2)}, u32[]{:S(2)}) collective-permute-start(bf16[512,256]{1,0:T(8,128)(2,1)S(1)} %get-tuple-element.52), channel_id=1, source_target_pairs={{0,504},{8,16},{16,8},{24,32},{32,24},{40,48},{48,40},{56,64},{64,... | collective-permute-start | bytes 786440 | tf_op jit(solution)/shard_map/ppermute | solution.py:365
  10.7 11.9 %collective-permute-start = (bf16[1024,256]{1,0:T(8,128)(2,1)S(1)}, bf16[1024,256]{1,0:T(8,128)(2,1)S(1)}, u32[]{:S(2)}, u32[]{:S(2)}) collective-permute-start(bf16[1024,256]{1,0:T(8,128)(2,1)S(1)} %get-tuple-element.40), channel_id=1, source_target_pairs={{0,8},{8,0},{16,24},{24,16},{32,40},{40,32},{48,56},{56,48},{64,72... | collective-permute-start | bytes 1572872 | tf_op jit(solution)/shard_map/ppermute | solution.py:369
  22.6 0.0 collective-permute-done.1.refs_0_
  22.7 0.2 shard_map.88
  22.9 1.3 %collective-permute-done.refs_2_ = bf16[1024,256]{1,0:T(8,128)(2,1)S(1)} collective-permute-done((bf16[1024,256]{1,0:T(8,128)(2,1)S(1)}, bf16[1024,256]{1,0:T(8,128)(2,1)S(1)}, u32[]{:S(2)}, u32[]{:S(2)}) %collective-permute-start) | collective-permute-done | bytes 524320 | tf_op jit(solution)/shard_map/ppermute | solution.py:369
  24.2 1.0 %shard_map.89 = (f32[4,128,256]{2,1,0:T(8,128)S(1)}, bf16[512,256]{1,0:T(8,128)(2,1)S(1)}, f32[8,128,256]{2,1,0:T(8,128)S(1)}, f32[16,8,256]{2,1,0:T(8,128)S(1)}, bf16[512,256]{1,0:T(8,128)(2,1)S(1)}) custom-call(bf16[512,256]{1,0:T(8,128)(2,1)S(1)} %get-tuple-element.36.outer_ref.refs_0_.refs_1_.probe_outer, ...), custom_call_target="tpu_custom_call" | custom-call | flops 402653184 | tf_op jit(solution)/shard_map/pallas_call | solution.py:24
  25.2 0.0 collective-permute-done.2.refs_0_
  25.2 0.4 shard_map.90
  25.6 0.9 %shard_map.91 = (f32[4,128,256]{2,1,0:T(8,128)S(1)}, bf16[512,256]{1,0:T(8,128)(2,1)S(1)}, f32[8,128,256]{2,1,0:T(8,128)S(1)}, f32[16,8,256]{2,1,0:T(8,128)S(1)}...) custom-call(bf16[512,256]{1,0:T(8,128)(2,1)S(1)} %get-tuple-element.36.outer_ref.refs_0_.refs_1_.probe_outer, ...), custom_call_target="tpu_custom_call" | custom-call | flops 402653184 | tf_op jit(solution)/shard_map/pallas_call | solution.py:24
  26.6 1.9 %collective-permute-start.3 = (bf16[1024,256]{1,0:T(8,128)(2,1)S(1)}, bf16[1024,256]{1,0:T(8,128)(2,1)S(1)}, u32[]{:S(2)}, u32[]{:S(2)}) collective-permute-start(bf16[1024,256]{1,0:T(8,128)(2,1)S(1)} %get-tuple-element.55), channel_id=1, source_target_pairs={{0,504},{8,16},{16,8},{24,32},{32,24},{40,48},{48,40},{56,64},{64,... | collective-permute-start | bytes 1572872 | tf_op jit(solution)/shard_map/ppermute | solution.py:365
  28.5 7.6 %collective-permute-start.4 = (bf16[512,256]{1,0:T(8,128)(2,1)S(1)}, bf16[512,256]{1,0:T(8,128)(2,1)S(1)}, u32[]{:S(2)}, u32[]{:S(2)}) collective-permute-start(bf16[512,256]{1,0:T(8,128)(2,1)S(1)} %get-tuple-element.56), channel_id=1, source_target_pairs={{0,8},{8,0},{16,24},{24,16},{32,40},{40,32},{48,56},{56,48},{64,72... | collective-permute-start | bytes 786440 | tf_op jit(solution)/shard_map/ppermute | solution.py:369
  36.1 1.9 %collective-permute-start.5 = (bf16[512,256]{1,0:T(8,128)(2,1)S(1)}, bf16[512,256]{1,0:T(8,128)(2,1)S(1)}, u32[]{:S(2)}, u32[]{:S(2)}) collective-permute-start(bf16[512,256]{1,0:T(8,128)(2,1)S(1)} %get-tuple-element.57), channel_id=1, source_target_pairs={{0,8},{8,0},{16,24},{24,16},{32,40},{40,32},{48,56},{56,48},{64,72... | collective-permute-start | bytes 786440 | tf_op jit(solution)/shard_map/ppermute | solution.py:369
  38.1 0.0 collective-permute-done.4.got_2
  38.1 1.5 %collective-permute-done.5.got_1 = bf16[512,256]{1,0:T(8,128)(2,1)S(1)} collective-permute-done((bf16[512,256]{1,0:T(8,128)(2,1)S(1)}, bf16[512,256]{1,0:T(8,128)(2,1)S(1)}, u32[]{:S(2)}, u32[]{:S(2)}) %collective-permute-start.5) | collective-permute-done | bytes 262176 | tf_op jit(solution)/shard_map/ppermute | solution.py:369
  39.6 1.2 %shard_map.92 = (f32[16,8,256]{2,1,0:T(8,128)S(1)}, f32[4,128,256]{2,1,0:T(8,128)S(1)}, f32[4,128,256]{2,1,0:T(8,128)S(1)}) custom-call(bf16[512,256]{1,0:T(8,128)(2,1)S(1)} %get-tuple-element.36.outer_ref.refs_0_.refs_1_.probe_outer, bf16[512,256]{1,0:T(8,128)(2,1)S(1)} %get-tuple-element.37.inner_ref.refs_1_.refs_3_.probe_inner, ...), custom_call_target="tpu_custom_call" | custom-call | tf_op jit(solution)/shard_map/pallas_call | solution.py:24
  40.8 0.0 copy-start.1
  40.8 0.0 copy-start.2
  40.8 0.0 collective-permute-done.3.got_ref
  40.8 1.6 %shard_map.93 = f32[16,8,256]{2,1,0:T(8,128)} custom-call(bf16[512,256]{1,0:T(8,128)(2,1)S(1)} %get-tuple-element.36.outer_ref.refs_0_.refs_1_.probe_outer, bf16[512,256]{1,0:T(8,128)(2,1)S(1)} %get-tuple-element.37.inner_ref.refs_1_.refs_3_.probe_inner, bf16[1024,256]{1,0:T(8,128)(2,1)S(1)} %collective-permute-done.3.got_ref, ...), custom_call_target="tpu_custom_call" | custom-call | flops 402653184 | tf_op jit(solution)/shard_map/pallas_call | solution.py:24
  42.4 4.6 %all-to-all-start = ((f32[16,8,256]{2,1,0:T(8,128)}), f32[16,8,256]{2,1,0:T(8,128)S(1)}, u32[]{:S(2)}, u32[]{:S(2)}) async-start(f32[16,8,256]{2,1,0:T(8,128)} %shard_map.93), calls=%async_computation | async-start | bytes 262144 | tf_op jit(solution)/shard_map/all_to_all | solution.py:461
  47.1 6.8 %all-to-all-done.shares_ref = f32[16,8,256]{2,1,0:T(8,128)S(1)} async-done(((f32[16,8,256]{2,1,0:T(8,128)}), f32[16,8,256]{2,1,0:T(8,128)S(1)}, u32[]{:S(2)}, u32[]{:S(2)}) %all-to-all-start) | async-done | bytes 131104 | tf_op jit(solution)/shard_map/all_to_all | solution.py:461
  53.9 0.1 shard_map.94
  54.0 20.7 %all_to_all.10.largest_ref = f32[32,1,128]{2,1,0:T(1,128)S(1)} all-to-all(f32[32,1,128]{2,1,0:T(1,128)S(1)} %get-tuple-element.68), channel_id=1, replica_groups={{0,8,16,24,32,40,48,56,64,72,80,88,96,104,112,120,128,136,144,152,160,1..., dimensions={0} | all-to-all | bytes 32768 | tf_op jit(solution)/shard_map/all_to_all | solution.py:467
  74.7 0.0 copy-done.1
  74.7 0.0 copy-done.2
  74.7 0.7 shard_map.95
Async XLA Ops:
  0.6 6.3 %copy-start = (bf16[2,4,4,256,256]{4,3,2,1,0:T(8,128)(2,1)S(1)}, bf16[2,4,4,256,256]{4,3,2,1,0:T(8,128)(2,1)}, u32[]{:S(2)}) copy-start(bf16[2,4,4,256,256]{4,3,2,1,0:T(8,128)(2,1)} %param.12) | copy-start | bytes 12582916
  1.9 20.8 %collective-permute-start.1 = (bf16[512,256]{1,0:T(8,128)(2,1)S(1)}, bf16[512,256]{1,0:T(8,128)(2,1)S(1)}, u32[]{:S(2)}, u32[]{:S(2)}) collective-permute-start(bf16[512,256]{1,0:T(8,128)(2,1)S(1)} %get-tuple-element.36.outer_ref.refs_0_.refs_1_.probe_outer), channel_id=1, source_target_pairs={{0,504},{8,16},{16,8},{24,32},{32,24},{40,48},{48,40},{56,64},{64,... | collective-permute-start | bytes 786440 | tf_op jit(solution)/shard_map/ppermute | solution.py:365
  8.8 16.5 %collective-permute-start.2 = (bf16[512,256]{1,0:T(8,128)(2,1)S(1)}, bf16[512,256]{1,0:T(8,128)(2,1)S(1)}, u32[]{:S(2)}, u32[]{:S(2)}) collective-permute-start(bf16[512,256]{1,0:T(8,128)(2,1)S(1)} %get-tuple-element.52), channel_id=1, source_target_pairs={{0,504},{8,16},{16,8},{24,32},{32,24},{40,48},{48,40},{56,64},{64,... | collective-permute-start | bytes 786440 | tf_op jit(solution)/shard_map/ppermute | solution.py:365
  10.7 13.5 %collective-permute-start = (bf16[1024,256]{1,0:T(8,128)(2,1)S(1)}, bf16[1024,256]{1,0:T(8,128)(2,1)S(1)}, u32[]{:S(2)}, u32[]{:S(2)}) collective-permute-start(bf16[1024,256]{1,0:T(8,128)(2,1)S(1)} %get-tuple-element.40), channel_id=1, source_target_pairs={{0,8},{8,0},{16,24},{24,16},{32,40},{40,32},{48,56},{56,48},{64,72... | collective-permute-start | bytes 1572872 | tf_op jit(solution)/shard_map/ppermute | solution.py:369
  26.6 14.2 %collective-permute-start.3 = (bf16[1024,256]{1,0:T(8,128)(2,1)S(1)}, bf16[1024,256]{1,0:T(8,128)(2,1)S(1)}, u32[]{:S(2)}, u32[]{:S(2)}) collective-permute-start(bf16[1024,256]{1,0:T(8,128)(2,1)S(1)} %get-tuple-element.55), channel_id=1, source_target_pairs={{0,504},{8,16},{16,8},{24,32},{32,24},{40,48},{48,40},{56,64},{64,... | collective-permute-start | bytes 1572872 | tf_op jit(solution)/shard_map/ppermute | solution.py:365
  28.5 9.6 %collective-permute-start.4 = (bf16[512,256]{1,0:T(8,128)(2,1)S(1)}, bf16[512,256]{1,0:T(8,128)(2,1)S(1)}, u32[]{:S(2)}, u32[]{:S(2)}) collective-permute-start(bf16[512,256]{1,0:T(8,128)(2,1)S(1)} %get-tuple-element.56), channel_id=1, source_target_pairs={{0,8},{8,0},{16,24},{24,16},{32,40},{40,32},{48,56},{56,48},{64,72... | collective-permute-start | bytes 786440 | tf_op jit(solution)/shard_map/ppermute | solution.py:369
  36.1 3.4 %collective-permute-start.5 = (bf16[512,256]{1,0:T(8,128)(2,1)S(1)}, bf16[512,256]{1,0:T(8,128)(2,1)S(1)}, u32[]{:S(2)}, u32[]{:S(2)}) collective-permute-start(bf16[512,256]{1,0:T(8,128)(2,1)S(1)} %get-tuple-element.57), channel_id=1, source_target_pairs={{0,8},{8,0},{16,24},{24,16},{32,40},{40,32},{48,56},{56,48},{64,72... | collective-permute-start | bytes 786440 | tf_op jit(solution)/shard_map/ppermute | solution.py:369
  40.8 33.9 %copy-start.1 = (f32[2,4,256]{2,1,0:T(4,128)S(1)}, f32[2,4,256]{2,1,0:T(4,128)}, u32[]{:S(2)}) copy-start(f32[2,4,256]{2,1,0:T(4,128)} %angles_ref.1) | copy-start | bytes 24580
  40.8 33.9 %copy-start.2 = (f32[2,4,256]{2,1,0:T(4,128)S(1)}, f32[2,4,256]{2,1,0:T(4,128)}, u32[]{:S(2)}) copy-start(f32[2,4,256]{2,1,0:T(4,128)} %noise_ref.1) | copy-start | bytes 24580
  42.4 11.5 %all-to-all-start = ((f32[16,8,256]{2,1,0:T(8,128)}), f32[16,8,256]{2,1,0:T(8,128)S(1)}, u32[]{:S(2)}, u32[]{:S(2)}) async-start(f32[16,8,256]{2,1,0:T(8,128)} %shard_map.93), calls=%async_computation | async-start | bytes 262144 | tf_op jit(solution)/shard_map/all_to_all | solution.py:461

commit v5 on v4

v5 whole, which is shorter than its diff:
```python
import functools
import jax
import jax.numpy as jnp
from jax import lax
from jax.experimental import pallas as pl
from jax.experimental.pallas import tpu as pltpu
from jax.sharding import PartitionSpec as P

BAND = 8.0
STEP_MAX = 0.3
TWO_TEMP = 0.1

VERT, LEFT, RIGHT, RIM = range(4)
IN_VMEM = pl.BlockSpec(memory_space=pltpu.VMEM)
IN_SMEM = pl.BlockSpec(memory_space=pltpu.SMEM)
IN_HBM = pl.BlockSpec(memory_space=pltpu.HBM)


def held(array, space=pltpu.VMEM):
    return pltpu.with_memory_space_constraint(array, space)


def call(body, outs, in_specs, args, scratch=(), flops=0, moved=0):
    return pl.pallas_call(
        body,
        out_shape=[pltpu.VMEM(shape, dtype) for shape, dtype in outs],
        in_specs=in_specs,
        out_specs=[IN_VMEM] * len(outs),
        scratch_shapes=list(scratch),
        compiler_params=pltpu.CompilerParams(vmem_limit_bytes=16 * 1024 * 1024),
        cost_estimate=pl.CostEstimate(flops=flops, bytes_accessed=moved, transcendentals=0),
    )(*args)


def product(vectors, matrix):
    return jnp.dot(vectors, matrix, preferred_element_type=jnp.float32)


def folded(values):
    return jnp.sum(values.reshape(-1, 8, values.shape[-1]), axis=0)


def overlap_terms(probe, vectors):
    half = probe.shape[0] // 2
    upper_r = probe[:half].astype(jnp.float32)
    lower_r = probe[half:].astype(jnp.float32)
    upper_w, lower_w = vectors[:half], vectors[half:]
    same = folded(upper_r * upper_w - lower_r * lower_w)
    cross = folded(upper_r * lower_w + lower_r * upper_w)
    return same, cross


def fetch_body(parity_ref, probes_hbm, offsets_hbm, coef_hbm, angles_hbm, coupling_hbm,
               outer_ref, inner_ref, offsets_ref, coef_ref, angles_ref, coupling_ref, sems):
    parity = parity_ref[0]
    copies = [
        pltpu.make_async_copy(source, target, sems.at[k])
        for k, (source, target) in enumerate((
            (probes_hbm.at[parity], outer_ref),
            (probes_hbm.at[1 - parity], inner_ref),
            (offsets_hbm, offsets_ref),
            (coef_hbm, coef_ref),
            (angles_hbm, angles_ref),
            (coupling_hbm, coupling_ref),
        ))
    ]
    for copy in copies:
        copy.start()
    for copy in copies:
        copy.wait()


def beside(cols, rows, low_ref, tile, matrix):
    row, col = divmod(tile, cols)
    right, left = (col + 1) % cols, (col - 1) % cols
    return product(
        low_ref[pl.ds(right * rows, rows), :], matrix(LEFT, row * cols + right)
    ) + product(low_ref[pl.ds(left * rows, rows), :], matrix(RIGHT, row * cols + left))


def local_hop(cols, rows, outer_ref, inner_ref, tile, matrix):
    refs = (outer_ref, inner_ref)
    row, col = divmod(tile, cols)
    total = product(
        refs[1 - row][pl.ds(col * rows, rows), :], matrix(VERT, (1 - row) * cols + col)
    )
    return total + beside(cols, rows, refs[row], tile, matrix)


def kondo(vectors, twice_cos, twice_sin):
    half = vectors.shape[0] // 2
    upper, lower = vectors[:half], vectors[half:]
    return jnp.concatenate(
        [twice_cos * upper + twice_sin * lower, twice_sin * upper - twice_cos * lower], axis=0
    )


def first_body(cols, rows, probe_total, parity_ref, offsets_ref, coef_ref, raw_ref, angles_ref,
               coupling_ref, outer_ref, inner_ref, sorted_ref, part_outer, part_inner, send_ref,
               pair_ref, weights_ref, cos_ref, sin_ref, same_ref, cross_ref):
    tiles = 2 * cols
    slots = offsets_ref.shape[2]
    parity = parity_ref[0]

    def tile_of(kind, tile):
        row, col = divmod(tile, cols)
        origin = row + parity - 2 * row * parity
        if kind == LEFT:
            code = 3
        elif kind == RIGHT:
            code = 5
        else:
            towards_high = (row == 0) == (kind == VERT)
            code = 7 - 6 * parity if towards_high else 1 + 6 * parity
        slot = jnp.int32(0)
        for k in range(1, slots):
            slot += jnp.where(offsets_ref[origin, col, k] == code, k, 0)
        return (origin * cols + col) * slots + slot

    def matrix(kind, tile):
        found = raw_ref[tile_of(kind, tile)]
        sorted_ref[kind * tiles + tile] = found
        return found

    for row in range(2):
        origin = row + parity - 2 * row * parity
        place = pl.ds(row * cols, cols)
        angles, strength = angles_ref[origin], coupling_ref[origin]
        cosines, sine_values = jnp.cos(angles), jnp.sin(angles)
        scale = (-BAND / probe_total) * strength
        cos_ref[place, :] = 2.0 * strength * cosines
        sin_ref[place, :] = 2.0 * strength * sine_values
        same_ref[place, :] = -scale * sine_values
        cross_ref[place, :] = scale * cosines
    for level in range(coef_ref.shape[0]):
        weights_ref[pl.ds(level, 1), :] = jnp.full(
            (1, weights_ref.shape[1]), (level + 1) * coef_ref[level], jnp.float32
        )
    for tile in range(tiles):
        row, col = divmod(tile, cols)
        place = pl.ds(col * rows, rows)
        probe = (outer_ref, inner_ref)[row][place, :]
        total = local_hop(cols, rows, outer_ref, inner_ref, tile, matrix)
        part = 2.0 * total + kondo(
            probe.astype(jnp.float32), cos_ref[pl.ds(tile, 1), :], sin_ref[pl.ds(tile, 1), :]
        )
        (part_outer, part_inner)[row][col] = part
        if row == 0:
            send_ref[place, :] = part.astype(jnp.bfloat16)
        else:
            pair_ref[place, :] = probe
            pair_ref[pl.ds((cols + col) * rows, rows), :] = part.astype(jnp.bfloat16)
    for tile in range(tiles):
        matrix(RIM, tile)


def first_outer_body(cols, rows, got_ref, sorted_ref, part_ref, field_ref, low_ref, turned_ref):
    for col in range(cols):
        place = pl.ds(col * rows, rows)
        turned = sorted_ref[RIM * 2 * cols + col].T
        turned_ref[col] = turned
        field = part_ref[col] + 2.0 * product(got_ref[place, :], turned)
        field_ref[col] = field
        low_ref[place, :] = field.astype(jnp.bfloat16)


def first_inner_body(cols, rows, probe_outer, probe_inner, got_ref, sorted_ref, part_ref,
                     weights_ref, cos_ref, sin_ref, field_outer, low_outer,
                     field_inner, low_inner, part_outer, part_inner, send_ref, terms_ref,
                     turned_ref):
    tiles = 2 * cols
    fields, low, probes = (field_outer, field_inner), (low_outer, low_inner), (probe_outer, probe_inner)
    for col in range(cols):
        place = pl.ds(col * rows, rows)
        turned = sorted_ref[RIM * tiles + cols + col].T
        turned_ref[col] = turned
        field = part_ref[col] + 2.0 * product(got_ref[place, :], turned)
        field_inner[col] = field
        low_inner[place, :] = field.astype(jnp.bfloat16)

    def matrix(kind, source):
        return sorted_ref[kind * tiles + source]

    for tile in range(tiles):
        row, col = divmod(tile, cols)
        place = pl.ds(col * rows, rows)
        probe_low = probes[row][place, :]
        probe = probe_low.astype(jnp.float32)
        field = fields[row][col]
        total = local_hop(cols, rows, *low, tile, matrix)
        following = 2.0 * total - probe + kondo(
            field, cos_ref[pl.ds(tile, 1), :], sin_ref[pl.ds(tile, 1), :]
        )
        (part_outer, part_inner)[row][col] = following
        if row == 1:
            send_ref[place, :] = following.astype(jnp.bfloat16)
        terms_ref[tile], terms_ref[tiles + tile] = overlap_terms(
            probe_low, weights_ref[0:1, 0:1] * probe + weights_ref[1:2, 0:1] * field
        )


def second_inner_body(cols, rows, probe_outer, probe_inner, got_ref, sorted_ref, turned_ref,
                      part_ref, field_ref, low_ref, share_ref, vert_ref):
    tiles = 2 * cols
    for col in range(cols):
        place = pl.ds(col * rows, rows)
        own = 2.0 * product(probe_inner[place, :], sorted_ref[RIM * tiles + cols + col])
        sent = got_ref[pl.ds((cols + col) * rows, rows), :].astype(jnp.float32)
        rim = (sent + own).astype(jnp.bfloat16)
        field = part_ref[col] + 2.0 * product(rim, turned_ref[col])
        field_ref[col] = field
        low = field.astype(jnp.bfloat16)
        low_ref[place, :] = low
        vert_ref[col] = 2.0 * product(low, sorted_ref[VERT * tiles + cols + col])
        share_ref[col] = 2.0 * product(probe_outer[place, :], sorted_ref[RIM * tiles + col])


def second_outer_body(cols, rows, got_ref, share_ref, vert_ref, sorted_ref, turned_ref, part_ref,
                      field_before, cos_ref, sin_ref, field_ref, low_ref, next_ref, pair_ref):
    tiles = 2 * cols
    for col in range(cols):
        place = pl.ds(col * rows, rows)
        rim = (got_ref[place, :].astype(jnp.float32) + share_ref[col]).astype(jnp.bfloat16)
        field = part_ref[col] + 2.0 * product(rim, turned_ref[col])
        field_ref[col] = field
        low_ref[place, :] = field.astype(jnp.bfloat16)

    def matrix(kind, source):
        return sorted_ref[kind * tiles + source]

    for col in range(cols):
        following = 2.0 * beside(cols, rows, low_ref, col, matrix) + vert_ref[col] + kondo(
            field_ref[col], cos_ref[pl.ds(col, 1), :], sin_ref[pl.ds(col, 1), :]
        ) - field_before[col]
        next_ref[col] = following
        pair_ref[pl.ds(col * rows, rows), :] = part_ref[col].astype(jnp.bfloat16)
        pair_ref[pl.ds((cols + col) * rows, rows), :] = following.astype(jnp.bfloat16)


def second_rest_body(cols, rows, probe_outer, probe_inner, sorted_ref, terms_ref, weights_ref,
                     cos_ref, sin_ref, field_outer, field_inner, low_outer, low_inner,
                     field_before, next_ref, send_ref, out_ref):
    tiles = 2 * cols

    def matrix(kind, source):
        return sorted_ref[kind * tiles + source]

    for col in range(cols):
        tile = cols + col
        place = pl.ds(col * rows, rows)
        total = local_hop(cols, rows, low_outer, low_inner, tile, matrix)
        following = 2.0 * total - field_before[col] + kondo(
            field_inner[col], cos_ref[pl.ds(tile, 1), :], sin_ref[pl.ds(tile, 1), :]
        )
        next_ref[col] = following
        send_ref[place, :] = following.astype(jnp.bfloat16)
    weight = weights_ref[2:3, 0:1]
    for tile in range(tiles):
        row, col = divmod(tile, cols)
        probe = (probe_outer, probe_inner)[row][pl.ds(col * rows, rows), :]
        same, cross = overlap_terms(probe, (field_outer, field_inner)[row][col])
        out_ref[tile] = terms_ref[tile] + weight * same
        out_ref[tiles + tile] = terms_ref[tiles + tile] + weight * cross


def last_inner_body(cols, rows, probe_outer, probe_inner, got_2, got_3, low_1_outer, low_1_inner,
                    low_2_outer, low_2_inner, field_outer, field_inner, sorted_ref, turned_ref,
                    part_ref, terms_ref, weights_ref, cos_ref, sin_ref,
                    out_ref, halo_2_ref, halo_3_ref, low_ref):
    tiles = 2 * cols
    weight, weight_next = weights_ref[3:4, 0:1], weights_ref[4:5, 0:1]

    def matrix(kind, tile):
        return sorted_ref[kind * tiles + tile]

    def rim(got_ref, low_before, col):
        place = pl.ds(col * rows, rows)
        own = 2.0 * product(low_before[place, :], matrix(RIM, cols + col))
        return (got_ref[place, :].astype(jnp.float32) + own).astype(jnp.bfloat16)

    fields = []
    for col in range(cols):
        field = part_ref[col] + 2.0 * product(rim(got_2, low_1_inner, col), turned_ref[col])
        fields.append(field)
        low_ref[pl.ds(col * rows, rows), :] = field.astype(jnp.bfloat16)
    for tile in range(tiles):
        row, col = divmod(tile, cols)
        place = pl.ds(col * rows, rows)
        if row == 0:
            following = 2.0 * product(low_ref[place, :], matrix(VERT, cols + col))
            vectors = weight_next * (following - field_outer[col])
            probe = probe_outer[place, :]
        else:
            total = beside(cols, rows, low_ref, tile, matrix)
            total += product(rim(got_3, low_2_inner, col), turned_ref[col])
            following = 2.0 * total - field_inner[col] + kondo(
                fields[col], cos_ref[pl.ds(tile, 1), :], sin_ref[pl.ds(tile, 1), :]
            )
            vectors = weight * fields[col] + weight_next * following
            probe = probe_inner[place, :]
        same, cross = overlap_terms(probe, vectors)
        out_ref[tile] = terms_ref[tile] + same
        out_ref[tiles + tile] = terms_ref[tiles + tile] + cross
    for col in range(cols):
        place = pl.ds(col * rows, rows)
        halo_2_ref[col] = 2.0 * product(low_1_outer[place, :], matrix(RIM, col))
        halo_3_ref[col] = 2.0 * product(low_2_outer[place, :], matrix(RIM, col))


def row_sums(blocks):
    index = lax.broadcasted_iota(jnp.int32, blocks[0].shape, 0)
    shift = 4
    while shift:
        low = (index & shift) == 0
        half = len(blocks) // 2
        joined = []
        for first, second in zip(blocks[:half], blocks[half:]):
            kept, moved = jnp.where(low, first, second), jnp.where(low, second, first)
            down = pltpu.roll(moved, shift, 0)
            if shift == 4:
                joined.append(kept + down)
            else:
                joined.append(kept + jnp.where(low, pltpu.roll(moved, 8 - shift, 0), down))
        blocks = joined
        shift //= 2
    return blocks[0]


def last_outer_body(cols, rows, probe_outer, probe_inner, got_ref, halo_2_ref, halo_3_ref,
                    sorted_ref, turned_ref, part_ref, terms_ref, weights_ref, cos_ref, sin_ref,
                    same_ref, cross_ref, out_ref, low_ref):
    tiles = 2 * cols
    weight, weight_next = weights_ref[3:4, 0:1], weights_ref[4:5, 0:1]

    def matrix(kind, tile):
        return sorted_ref[kind * tiles + tile]

    def halo(half, share_ref, col):
        sent = got_ref[pl.ds((half * cols + col) * rows, rows), :].astype(jnp.float32)
        return (sent + share_ref[col]).astype(jnp.bfloat16)

    fields = []
    for col in range(cols):
        field = part_ref[col] + 2.0 * product(halo(0, halo_2_ref, col), turned_ref[col])
        fields.append(field)
        low_ref[pl.ds(col * rows, rows), :] = field.astype(jnp.bfloat16)
    shares = []
    for tile in range(tiles):
        row, col = divmod(tile, cols)
        place = pl.ds(col * rows, rows)
        one = pl.ds(tile, 1)
        if row == 0:
            total = beside(cols, rows, low_ref, tile, matrix)
            total += product(halo(1, halo_3_ref, col), turned_ref[col])
            following = 2.0 * total + kondo(fields[col], cos_ref[one, :], sin_ref[one, :])
            vectors = weight * fields[col] + weight_next * following
            probe = probe_outer[place, :]
        else:
            vectors = (2.0 * weight_next) * product(low_ref[place, :], matrix(VERT, col))
            probe = probe_inner[place, :]
        same, cross = overlap_terms(probe, vectors)
        shares.append(
            same_ref[one, :] * (terms_ref[tile] + same)
            + cross_ref[one, :] * (terms_ref[tiles + tile] + cross)
        )
    share = row_sums(shares)
    for peer in range(out_ref.shape[0]):
        out_ref[peer] = share


def force_body(upper_ref, shares_ref, force_ref, largest_ref):
    peers = shares_ref.shape[0] // 2
    strips = []
    for strip in range(2):
        total = shares_ref[strip * peers]
        for peer in range(1, peers):
            total += shares_ref[strip * peers + peer]
        strips.append(total)
    force_ref[...] = jnp.where(upper_ref[0] == 0, strips[0], strips[1])
    largest = jnp.max(jnp.maximum(jnp.abs(strips[0]), jnp.abs(strips[1])))
    largest_ref[...] = jnp.full(largest_ref.shape, largest, jnp.float32)


def move_body(parity_ref, largest_ref, force_ref, angles_ref, noise_ref, next_ref, out_ref):
    parity = parity_ref[0]
    cols = out_ref.shape[1]
    largest = jnp.max(largest_ref[...])
    step_size = jnp.full((1, 1), STEP_MAX, jnp.float32) / (largest + 1e-06)
    kick = jnp.sqrt(TWO_TEMP * step_size)
    for row in range(2):
        origin = row + parity - 2 * row * parity
        force = force_ref[pl.ds(row * cols, cols), :]
        out_ref[origin] = force
        next_ref[origin] = angles_ref[origin] + step_size * force + kick * noise_ref[origin]


def exchange_outer(outer):
    count = lax.axis_size("site")
    pairs = [(i, (i + 1) % count if i % 2 else (i - 1) % count) for i in range(count)]
    return lax.ppermute(outer, "site", pairs)


def exchange_inner(inner):
    return lax.ppermute(inner, "site", [(i, i ^ 1) for i in range(lax.axis_size("site"))])


def local(angles, coupling, thermal_noise, coefficients, probes, hopping, offsets):
    cols, orbitals, share, width = probes.shape[1:]
    rows = orbitals * share
    tiles = 2 * cols
    f32, bf16 = jnp.float32, jnp.bfloat16
    side = ((cols * rows, width), bf16)
    pair = ((2 * cols * rows, width), bf16)
    row = ((cols, rows, width), f32)
    matrices = ((cols, width, width), bf16)
    terms_like = ((2 * tiles, 8, width), f32)
    row_like = ((tiles, width), f32)
    sites, peers = lax.axis_size("site"), lax.axis_size("probe")
    probe_total = peers * share
    local_flops = 2 * 3 * tiles * rows * width * width
    site = lax.axis_index("site")
    parity = (site % 2).astype(jnp.int32).reshape(1)
    upper = (site // (sites // 2)).astype(jnp.int32).reshape(1)

    def run(body, outs, args, scratch=(), flops=0):
        return call(
            functools.partial(body, cols, rows), outs, [IN_VMEM] * len(args),
            tuple(held(x) for x in args), scratch=scratch, flops=flops,
        )

    fetched = pl.pallas_call(
        fetch_body,
        out_shape=[
            pltpu.VMEM(*side), pltpu.VMEM(*side), pltpu.SMEM(offsets.shape, jnp.int32),
            pltpu.SMEM(coefficients.shape, f32), pltpu.VMEM(angles.shape, f32),
            pltpu.VMEM(coupling.shape, f32),
        ],
        in_specs=[IN_SMEM] + [IN_HBM] * 5,
        out_specs=[IN_VMEM, IN_VMEM, IN_SMEM, IN_SMEM, IN_VMEM, IN_VMEM],
        scratch_shapes=[pltpu.SemaphoreType.DMA((6,))],
        compiler_params=pltpu.CompilerParams(vmem_limit_bytes=16 * 1024 * 1024),
        cost_estimate=pl.CostEstimate(flops=20 * local_flops, bytes_accessed=0, transcendentals=0),
    )(parity, *(held(x, pltpu.HBM) for x in (
        probes.reshape(2, cols * rows, width), offsets, coefficients, angles, coupling)))
    outer, inner, offsets_held, coef_held, angles_held, coupling_held = fetched
    probe_rows = [outer, inner]
    got_0 = exchange_outer(outer)

    (sorted_hop, part_outer, part_inner, send, send_pair, weights, twice_cos, twice_sin,
     same_factor, cross_factor) = call(
        functools.partial(first_body, cols, rows, probe_total),
        [((4 * tiles, width, width), bf16), row, row, side, pair, ((8, 128), f32)]
        + [row_like] * 4,
        [IN_SMEM] * 3 + [IN_VMEM] * 5,
        (parity, held(offsets_held, pltpu.SMEM), held(coef_held, pltpu.SMEM),
         *(held(x) for x in (hopping.reshape(-1, width, width), angles_held, coupling_held,
                             outer, inner))),
        flops=local_flops, moved=hopping.size * 2,
    )
    got_1 = exchange_outer(send)
    from_inner = exchange_inner(send_pair)
    trig = [twice_cos, twice_sin]

    field_1_outer, low_1_outer, turned_outer = run(
        first_outer_body, [row, side, matrices], [got_0, sorted_hop, part_outer],
        flops=20 * local_flops,
    )
    (field_1_inner, low_1_inner, part_outer, part_inner, send, terms, turned_inner) = run(
        first_inner_body, [row, side, row, row, side, terms_like, matrices],
        [*probe_rows, from_inner, sorted_hop, part_inner, weights, *trig,
         field_1_outer, low_1_outer],
        flops=local_flops,
    )
    inner_2 = exchange_inner(send)
    field_2_inner, low_2_inner, rim_share, vert = run(
        second_inner_body, [row, side, row, row],
        [*probe_rows, from_inner, sorted_hop, turned_inner, part_inner],
    )
    field_2_outer, low_2_outer, part_outer, send_pair = run(
        second_outer_body, [row, side, row, pair],
        [got_1, rim_share, vert, sorted_hop, turned_outer, part_outer, field_1_outer, *trig],
    )
    got_pair = exchange_outer(send_pair)
    part_inner, send, terms = run(
        second_rest_body, [row, side, terms_like],
        [*probe_rows, sorted_hop, terms, weights, *trig, field_2_outer, field_2_inner,
         low_2_outer, low_2_inner, field_1_inner],
    )
    inner_3 = exchange_inner(send)
    terms, halo_2, halo_3 = run(
        last_inner_body, [terms_like, row, row],
        [*probe_rows, inner_2, inner_3, low_1_outer, low_1_inner, low_2_outer, low_2_inner,
         field_2_outer, field_2_inner, sorted_hop, turned_inner, part_inner, terms, weights,
         *trig],
        scratch=[pltpu.VMEM(*side)],
    )
    shares = run(
        last_outer_body, [((2 * peers, tiles, width), f32)],
        [*probe_rows, got_pair, halo_2, halo_3, sorted_hop, turned_outer, part_outer, terms,
         weights, *trig, same_factor, cross_factor],
        scratch=[pltpu.VMEM(*side)], flops=local_flops,
    )[0]
    pairs = [
        [half * peers + peer for half in (i, i + sites // 2) for peer in range(peers)]
        for i in range(sites // 2)
    ]
    shares = lax.all_to_all(shares, ("site", "probe"), 0, 0, axis_index_groups=pairs)
    force, largest = call(
        force_body, [row_like, ((sites // 2, 1, 128), f32)],
        [IN_SMEM, IN_VMEM], (upper, held(shares)),
    )
    halves = [list(range(sites // 2)), list(range(sites // 2, sites))]
    largest = lax.all_to_all(largest, "site", 0, 0, axis_index_groups=halves)
    return pl.pallas_call(
        move_body,
        out_shape=[jax.ShapeDtypeStruct(angles.shape, f32)] * 2,
        in_specs=[IN_SMEM] + [IN_VMEM] * 4,
        out_specs=[IN_VMEM] * 2,
    )(parity, held(largest), held(force), held(angles), held(thermal_noise))


def solution(mesh):
    in_specs = (
        P("site", None, None),
        P("site", None, None),
        P("site", None, None),
        P(),
        P("site", None, None, "probe", None),
        P("site", None, None, None, None),
        P("site", None, None),
    )
    out_specs = (P("site", None, None), P("site", None, None))
    return jax.shard_map(local, mesh=mesh, in_specs=in_specs, out_specs=out_specs, check_vma=False)
```

time: 75.9 us -> 74.6 us (0.983)
  blocking collectives: 20.7 us -> 18.8 us
  Pallas kernels: 9.32 us -> 10.1 us
    all_to_all x1, blocking collectives: 20.7 us -> 18.8 us  [local(): largest = lax.all_to_all(largest, 'site', 0, 0, axis_index_groups=halves)]
    pallas_call x0 -> x1, Pallas kernels: none -> 1.26 us  [local(): pl.pallas_call(fetch_body, out_shape=[pltpu.VMEM(*side), pltpu.VMEM(*side...]
  transfers between devices with their start and end apart: 7 -> 7, of which waited for: 3 -> 3; matrix products, arithmetic and copies ran while one was open for 0% -> 0% of each run, Pallas kernels for 6% -> 8%
where the time goes in v5:
time: 74.6 us; the launch traced here: 74.2 us
  starting transfers between devices  35 us (47%)
  blocking collectives  18.8 us (25%)
  Pallas kernels  10.1 us (14%)
  waiting for transfers between devices  9.46 us (13%)
  between operations  0.84 us (1%)
    ppermute x3, starting transfers between devices, exchange_inner(): lax.ppermute(inner, 'site', [(i, i ^ 1) for i in range(lax.axis_size('sit...  21.5 us
    all_to_all x1, blocking collectives, local(): largest = lax.all_to_all(largest, 'site', 0, 0, axis_index_groups=halves)  18.8 us
    ppermute x3, starting transfers between devices, exchange_outer(): return lax.ppermute(outer, 'site', pairs)  8.91 us
    pallas_call x9, Pallas kernels, call(): pl.pallas_call(body, out_shape=[pltpu.VMEM(shape, dtype) for shape, dtype...  8.09 us
    all_to_all x1, waiting for transfers between devices, local(): lax.all_to_all(shares, ('site', 'probe'), 0, 0, axis_index_groups=pairs)  6.83 us
    all_to_all x1, starting transfers between devices, local(): lax.all_to_all(shares, ('site', 'probe'), 0, 0, axis_index_groups=pairs)  4.62 us
    ppermute x3, waiting for transfers between devices, exchange_inner(): lax.ppermute(inner, 'site', [(i, i ^ 1) for i in range(lax.axis_size('sit...  2.62 us
  transfers between devices with their start and end apart: 7, of which 3 were waited for; matrix products, arithmetic and copies ran while one was open for 0% of the time, Pallas kernels for 8%

profile of v5, /device:TPU:1, one launch (start us, length us, event | category | flops | bytes accessed | tf_op | source)
XLA Modules:
  0.0 74.2 jit_solution(7860395013490209021)
XLA Ops:
  0.6 0.0 copy-start
  0.7 1.3 %shard_map.86 = (bf16[512,256]{1,0:T(8,128)(2,1)S(1)}, bf16[512,256]{1,0:T(8,128)(2,1)S(1)}, s32[2,4,4]{2,1,0:T(4,128)S(4)}, f32[5]{0:T(128)S(4)}, f32[2,4,256]{2,1,0:T(4,128)S(1)}, /*index=5*/f32[2,4,256]{2,1,0:T(4,128)S(1)}) custom-call(s32[1]{0:T(128)} %bitcast.parity_ref, bf16[2,512,256]{2,1,0:T(8,128)(2,1)} %bitcast.5, s32[2,4,4]{2,1,0:T(4,128)} %offsets_hbm.1, ...), custom_call_target="tpu_custom_call" | custom-call | flops 8053063680 | tf_op jit(solution)/shard_map/pallas_call | solution.py:431
  1.9 5.1 %collective-permute-start.2 = (bf16[512,256]{1,0:T(8,128)(2,1)S(1)}, bf16[512,256]{1,0:T(8,128)(2,1)S(1)}, u32[]{:S(2)}, u32[]{:S(2)}) collective-permute-start(bf16[512,256]{1,0:T(8,128)(2,1)S(1)} %get-tuple-element.44.outer_ref.probe_outer), channel_id=1, source_target_pairs={{0,504},{8,16},{16,8},{24,32},{32,24},{40,48},{48,40},{56,64},{64,... | collective-permute-start | bytes 786440 | tf_op jit(solution)/shard_map/ppermute | solution.py:400
  7.0 0.0 copy-done
  7.0 0.9 %shard_map.87 = (bf16[32,256,256]{2,1,0:T(8,128)(2,1)S(1)}, f32[4,128,256]{2,1,0:T(8,128)S(1)}, f32[4,128,256]{2,1,0:T(8,128)S(1)}, bf16[512,256]{1,0:T(8,128)(2...) custom-call(s32[1]{0:T(128)} %bitcast.parity_ref, ...), custom_call_target="tpu_custom_call" | custom-call | flops 402653184 | bytes 4194304 | tf_op jit(solution)/shard_map/pallas_call | solution.py:24
  7.9 1.9 %collective-permute-start = (bf16[512,256]{1,0:T(8,128)(2,1)S(1)}, bf16[512,256]{1,0:T(8,128)(2,1)S(1)}, u32[]{:S(2)}, u32[]{:S(2)}) collective-permute-start(bf16[512,256]{1,0:T(8,128)(2,1)S(1)} %get-tuple-element.50), channel_id=1, source_target_pairs={{0,504},{8,16},{16,8},{24,32},{32,24},{40,48},{48,40},{56,64},{64,... | collective-permute-start | bytes 786440 | tf_op jit(solution)/shard_map/ppermute | solution.py:400
  9.8 12.0 %collective-permute-start.1 = (bf16[1024,256]{1,0:T(8,128)(2,1)S(1)}, bf16[1024,256]{1,0:T(8,128)(2,1)S(1)}, u32[]{:S(2)}, u32[]{:S(2)}) collective-permute-start(bf16[1024,256]{1,0:T(8,128)(2,1)S(1)} %get-tuple-element.51), channel_id=1, source_target_pairs={{0,8},{8,0},{16,24},{24,16},{32,40},{40,32},{48,56},{56,48},{64,72... | collective-permute-start | bytes 1572872 | tf_op jit(solution)/shard_map/ppermute | solution.py:404
  21.8 0.0 collective-permute-done.2.got_ref
  21.8 0.4 shard_map.88
  22.2 1.1 %collective-permute-done.1.got_ref = bf16[1024,256]{1,0:T(8,128)(2,1)S(1)} collective-permute-done((bf16[1024,256]{1,0:T(8,128)(2,1)S(1)}, bf16[1024,256]{1,0:T(8,128)(2,1)S(1)}, u32[]{:S(2)}, u32[]{:S(2)}) %collective-permute-start.1) | collective-permute-done | bytes 524320 | tf_op jit(solution)/shard_map/ppermute | solution.py:404
  23.3 1.2 %shard_map.89 = (f32[4,128,256]{2,1,0:T(8,128)S(1)}, bf16[512,256]{1,0:T(8,128)(2,1)S(1)}, f32[4,128,256]{2,1,0:T(8,128)S(1)}, f32[4,128,256]{2,1,0:T(8,128)S(1)...) custom-call(bf16[512,256]{1,0:T(8,128)(2,1)S(1)} %get-tuple-element.44.outer_ref.probe_o, ...), custom_call_target="tpu_custom_call" | custom-call | flops 402653184 | tf_op jit(solution)/shard_map/pallas_call | solution.py:24
  24.5 1.3 %shard_map.90 = (f32[4,128,256]{2,1,0:T(8,128)S(1)}, bf16[512,256]{1,0:T(8,128)(2,1)S(1)}, f32[4,128,256]{2,1,0:T(8,128)S(1)}, f32[4,128,256]{2,1,0:T(8,128)S(1)}) custom-call(bf16[512,256]{1,0:T(8,128)(2,1)S(1)} %get-tuple-element.44.outer_ref.probe_outer, bf16[512,256]{1,0:T(8,128)(2,1)S(1)} %get-tuple-element.45.inner_ref.probe_inner, ...), custom_call_target="tpu_custom_call" | custom-call | tf_op jit(solution)/shard_map/pallas_call | solution.py:24
  25.8 0.0 collective-permute-done.got_ref
  25.8 0.6 shard_map.91
  26.4 1.9 %collective-permute-start.3 = (bf16[1024,256]{1,0:T(8,128)(2,1)S(1)}, bf16[1024,256]{1,0:T(8,128)(2,1)S(1)}, u32[]{:S(2)}, u32[]{:S(2)}) collective-permute-start(bf16[1024,256]{1,0:T(8,128)(2,1)S(1)} %get-tuple-element.66), channel_id=1, source_target_pairs={{0,504},{8,16},{16,8},{24,32},{32,24},{40,48},{48,40},{56,64},{64,... | collective-permute-start | bytes 1572872 | tf_op jit(solution)/shard_map/ppermute | solution.py:400
  28.3 7.6 %collective-permute-start.4 = (bf16[512,256]{1,0:T(8,128)(2,1)S(1)}, bf16[512,256]{1,0:T(8,128)(2,1)S(1)}, u32[]{:S(2)}, u32[]{:S(2)}) collective-permute-start(bf16[512,256]{1,0:T(8,128)(2,1)S(1)} %get-tuple-element.67), channel_id=1, source_target_pairs={{0,8},{8,0},{16,24},{24,16},{32,40},{40,32},{48,56},{56,48},{64,72... | collective-permute-start | bytes 786440 | tf_op jit(solution)/shard_map/ppermute | solution.py:404
  35.9 0.6 shard_map.92
  36.6 1.9 %collective-permute-start.5 = (bf16[512,256]{1,0:T(8,128)(2,1)S(1)}, bf16[512,256]{1,0:T(8,128)(2,1)S(1)}, u32[]{:S(2)}, u32[]{:S(2)}) collective-permute-start(bf16[512,256]{1,0:T(8,128)(2,1)S(1)} %get-tuple-element.74), channel_id=1, source_target_pairs={{0,8},{8,0},{16,24},{24,16},{32,40},{40,32},{48,56},{56,48},{64,72... | collective-permute-start | bytes 786440 | tf_op jit(solution)/shard_map/ppermute | solution.py:404
  38.5 0.0 collective-permute-done.4.got_2
  38.5 1.5 %collective-permute-done.5.got_3 = bf16[512,256]{1,0:T(8,128)(2,1)S(1)} collective-permute-done((bf16[512,256]{1,0:T(8,128)(2,1)S(1)}, bf16[512,256]{1,0:T(8,128)(2,1)S(1)}, u32[]{:S(2)}, u32[]{:S(2)}) %collective-permute-start.5) | collective-permute-done | bytes 262176 | tf_op jit(solution)/shard_map/ppermute | solution.py:404
  40.0 1.5 %shard_map.93 = (f32[16,8,256]{2,1,0:T(8,128)S(1)}, f32[4,128,256]{2,1,0:T(8,128)S(1)}, f32[4,128,256]{2,1,0:T(8,128)S(1)}) custom-call(bf16[512,256]{1,0:T(8,128)(2,1)S(1)} %get-tuple-element.44.outer_ref.probe_outer, bf16[512,256]{1,0:T(8,128)(2,1)S(1)} %get-tuple-element.45.inner_ref.probe_inner, bf16[512,256]{1,0:T(8,128)(2,1)S(1)} %collective-permute-done.4.got_2, ...), custom_call_target="tpu_custom_call" | custom-call | tf_op jit(solution)/shard_map/pallas_call | solution.py:24
  41.4 0.0 copy-start.1
  41.5 0.0 copy-start.2
  41.5 0.0 collective-permute-done.3.got_ref
  41.5 1.6 %shard_map.94 = f32[16,8,256]{2,1,0:T(8,128)} custom-call(bf16[512,256]{1,0:T(8,128)(2,1)S(1)} %get-tuple-element.44.outer_ref.probe_outer, bf16[512,256]{1,0:T(8,128)(2,1)S(1)} %get-tuple-element.45.inner_ref.probe_inner, bf16[1024,256]{1,0:T(8,128)(2,1)S(1)} %collective-permute-done.3.got_ref, f32[4,128,256]{2,1,0:T(8,128)S(1)} %get-tuple-element.78.halo_2_ref, ...), custom_call_target="tpu_custom_call" | custom-call | flops 402653184 | tf_op jit(solution)/shard_map/pallas_call | solution.py:24
  43.1 4.6 %all-to-all-start = ((f32[16,8,256]{2,1,0:T(8,128)}), f32[16,8,256]{2,1,0:T(8,128)S(1)}, u32[]{:S(2)}, u32[]{:S(2)}) async-start(f32[16,8,256]{2,1,0:T(8,128)} %shard_map.94), calls=%async_computation | async-start | bytes 262144 | tf_op jit(solution)/shard_map/all_to_all | solution.py:507
  47.7 6.8 %all-to-all-done.shares_ref = f32[16,8,256]{2,1,0:T(8,128)S(1)} async-done(((f32[16,8,256]{2,1,0:T(8,128)}), f32[16,8,256]{2,1,0:T(8,128)S(1)}, u32[]{:S(2)}, u32[]{:S(2)}) %all-to-all-start) | async-done | bytes 131104 | tf_op jit(solution)/shard_map/all_to_all | solution.py:507
  54.5 0.1 shard_map.95
  54.7 18.8 %all_to_all.10.largest_ref = f32[32,1,128]{2,1,0:T(1,128)S(1)} all-to-all(f32[32,1,128]{2,1,0:T(1,128)S(1)} %get-tuple-element.84), channel_id=1, replica_groups={{0,8,16,24,32,40,48,56,64,72,80,88,96,104,112,120,128,136,144,152,160,1..., dimensions={0} | all-to-all | bytes 32768 | tf_op jit(solution)/shard_map/all_to_all | solution.py:513
  73.4 0.0 copy-done.1
  73.4 0.0 copy-done.2
  73.4 0.7 %shard_map.96 = (f32[2,4,256]{2,1,0:T(4,128)}, f32[2,4,256]{2,1,0:T(4,128)}) custom-call(s32[1]{0:T(128)} %bitcast.parity_ref, f32[32,1,128]{2,1,0:T(1,128)S(1)} %all_to_all.10.largest_ref, f32[8,256]{1,0:T(8,128)S(1)} %get-tuple-element.85.force_ref, f32[2,4,256]{2,1,0:T(4,128)S(1)} %copy-done.1, f32[2,4,256]{2,1,0:T(4,128)S(1)} %copy-done.2), custom_call_target="tpu_custom_call" | custom-call | tf_op jit(solution)/shard_map/pallas_call | solution.py:514
Async XLA Ops:
  0.6 6.4 %copy-start = (bf16[2,4,4,256,256]{4,3,2,1,0:T(8,128)(2,1)S(1)}, bf16[2,4,4,256,256]{4,3,2,1,0:T(8,128)(2,1)}, u32[]{:S(2)}) copy-start(bf16[2,4,4,256,256]{4,3,2,1,0:T(8,128)(2,1)} %param.12) | copy-start | bytes 12582916
  1.9 19.9 %collective-permute-start.2 = (bf16[512,256]{1,0:T(8,128)(2,1)S(1)}, bf16[512,256]{1,0:T(8,128)(2,1)S(1)}, u32[]{:S(2)}, u32[]{:S(2)}) collective-permute-start(bf16[512,256]{1,0:T(8,128)(2,1)S(1)} %get-tuple-element.44.outer_ref.probe_outer), channel_id=1, source_target_pairs={{0,504},{8,16},{16,8},{24,32},{32,24},{40,48},{48,40},{56,64},{64,... | collective-permute-start | bytes 786440 | tf_op jit(solution)/shard_map/ppermute | solution.py:400
  7.9 17.9 %collective-permute-start = (bf16[512,256]{1,0:T(8,128)(2,1)S(1)}, bf16[512,256]{1,0:T(8,128)(2,1)S(1)}, u32[]{:S(2)}, u32[]{:S(2)}) collective-permute-start(bf16[512,256]{1,0:T(8,128)(2,1)S(1)} %get-tuple-element.50), channel_id=1, source_target_pairs={{0,504},{8,16},{16,8},{24,32},{32,24},{40,48},{48,40},{56,64},{64,... | collective-permute-start | bytes 786440 | tf_op jit(solution)/shard_map/ppermute | solution.py:400
  9.8 13.5 %collective-permute-start.1 = (bf16[1024,256]{1,0:T(8,128)(2,1)S(1)}, bf16[1024,256]{1,0:T(8,128)(2,1)S(1)}, u32[]{:S(2)}, u32[]{:S(2)}) collective-permute-start(bf16[1024,256]{1,0:T(8,128)(2,1)S(1)} %get-tuple-element.51), channel_id=1, source_target_pairs={{0,8},{8,0},{16,24},{24,16},{32,40},{40,32},{48,56},{56,48},{64,72... | collective-permute-start | bytes 1572872 | tf_op jit(solution)/shard_map/ppermute | solution.py:404
  26.4 15.1 %collective-permute-start.3 = (bf16[1024,256]{1,0:T(8,128)(2,1)S(1)}, bf16[1024,256]{1,0:T(8,128)(2,1)S(1)}, u32[]{:S(2)}, u32[]{:S(2)}) collective-permute-start(bf16[1024,256]{1,0:T(8,128)(2,1)S(1)} %get-tuple-element.66), channel_id=1, source_target_pairs={{0,504},{8,16},{16,8},{24,32},{32,24},{40,48},{48,40},{56,64},{64,... | collective-permute-start | bytes 1572872 | tf_op jit(solution)/shard_map/ppermute | solution.py:400
  28.3 10.2 %collective-permute-start.4 = (bf16[512,256]{1,0:T(8,128)(2,1)S(1)}, bf16[512,256]{1,0:T(8,128)(2,1)S(1)}, u32[]{:S(2)}, u32[]{:S(2)}) collective-permute-start(bf16[512,256]{1,0:T(8,128)(2,1)S(1)} %get-tuple-element.67), channel_id=1, source_target_pairs={{0,8},{8,0},{16,24},{24,16},{32,40},{40,32},{48,56},{56,48},{64,72... | collective-permute-start | bytes 786440 | tf_op jit(solution)/shard_map/ppermute | solution.py:404
  36.6 3.4 %collective-permute-start.5 = (bf16[512,256]{1,0:T(8,128)(2,1)S(1)}, bf16[512,256]{1,0:T(8,128)(2,1)S(1)}, u32[]{:S(2)}, u32[]{:S(2)}) collective-permute-start(bf16[512,256]{1,0:T(8,128)(2,1)S(1)} %get-tuple-element.74), channel_id=1, source_target_pairs={{0,8},{8,0},{16,24},{24,16},{32,40},{40,32},{48,56},{56,48},{64,72... | collective-permute-start | bytes 786440 | tf_op jit(solution)/shard_map/ppermute | solution.py:404
  41.4 32.0 %copy-start.1 = (f32[2,4,256]{2,1,0:T(4,128)S(1)}, f32[2,4,256]{2,1,0:T(4,128)}, u32[]{:S(2)}) copy-start(f32[2,4,256]{2,1,0:T(4,128)} %angles_ref.1) | copy-start | bytes 24580
  41.5 32.0 %copy-start.2 = (f32[2,4,256]{2,1,0:T(4,128)S(1)}, f32[2,4,256]{2,1,0:T(4,128)}, u32[]{:S(2)}) copy-start(f32[2,4,256]{2,1,0:T(4,128)} %noise_ref.1) | copy-start | bytes 24580
  43.1 11.5 %all-to-all-start = ((f32[16,8,256]{2,1,0:T(8,128)}), f32[16,8,256]{2,1,0:T(8,128)S(1)}, u32[]{:S(2)}, u32[]{:S(2)}) async-start(f32[16,8,256]{2,1,0:T(8,128)} %shard_map.94), calls=%async_computation | async-start | bytes 262144 | tf_op jit(solution)/shard_map/all_to_all | solution.py:507

commit v6 on v5

--- a/solution.py
+++ b/solution.py
@@ -202,109 +202,26 @@
 def second_inner_body(cols, rows, probe_outer, probe_inner, got_ref, sorted_ref, turned_ref,
                       part_ref, field_ref, low_ref, share_ref, vert_ref):
     tiles = 2 * cols
-    for col in range(cols):
-        place = pl.ds(col * rows, rows)
-        own = 2.0 * product(probe_inner[place, :], sorted_ref[RIM * tiles + cols + col])
-        sent = got_ref[pl.ds((cols + col) * rows, rows), :].astype(jnp.float32)
-        rim = (sent + own).astype(jnp.bfloat16)
-        field = part_ref[col] + 2.0 * product(rim, turned_ref[col])
-        field_ref[col] = field
-        low = field.astype(jnp.bfloat16)
-        low_ref[place, :] = low
-        vert_ref[col] = 2.0 * product(low, sorted_ref[VERT * tiles + cols + col])
-        share_ref[col] = 2.0 * product(probe_outer[place, :], sorted_ref[RIM * tiles + col])
-
-
-def second_outer_body(cols, rows, got_ref, share_ref, vert_ref, sorted_ref, turned_ref, part_ref,
-                      field_before, cos_ref, sin_ref, field_ref, low_ref, next_ref, pair_ref):
-    tiles = 2 * cols
-    for col in range(cols):
-        place = pl.ds(col * rows, rows)
-        rim = (got_ref[place, :].astype(jnp.float32) + share_ref[col]).astype(jnp.bfloat16)
-        field = part_ref[col] + 2.0 * product(rim, turned_ref[col])
-        field_ref[col] = field
-        low_ref[place, :] = field.astype(jnp.bfloat16)
-
-    def matrix(kind, source):
-        return sorted_ref[kind * tiles + source]
-
-    for col in range(cols):
-        following = 2.0 * beside(cols, rows, low_ref, col, matrix) + vert_ref[col] + kondo(
-            field_ref[col], cos_ref[pl.ds(col, 1), :], sin_ref[pl.ds(col, 1), :]
-        ) - field_before[col]
-        next_ref[col] = following
-        pair_ref[pl.ds(col * rows, rows), :] = part_ref[col].astype(jnp.bfloat16)
-        pair_ref[pl.ds((cols + col) * rows, rows), :] = following.astype(jnp.bfloat16)
-
-
-def second_rest_body(cols, rows, probe_outer, probe_inner, sorted_ref, terms_ref, weights_ref,
-                     cos_ref, sin_ref, field_outer, field_inner, low_outer, low_inner,
-                     field_before, next_ref, send_ref, out_ref):
-    tiles = 2 * cols
-
-    def matrix(kind, source):
-        return sorted_ref[kind * tiles + source]
-
-    for col in range(cols):
-        tile = cols + col
-        place = pl.ds(col * rows, rows)
-        total = local_hop(cols, rows, low_outer, low_inner, tile, matrix)
-        following = 2.0 * total - field_before[col] + kondo(
-            field_inner[col], cos_ref[pl.ds(tile, 1), :], sin_ref[pl.ds(tile, 1), :]
-        )
-        next_ref[col] = following
-        send_ref[place, :] = following.astype(jnp.bfloat16)
-    weight = weights_ref[2:3, 0:1]
-    for tile in range(tiles):
-        row, col = divmod(tile, cols)
-        probe = (probe_outer, probe_inner)[row][pl.ds(col * rows, rows), :]
-        same, cross = overlap_terms(probe, (field_outer, field_inner)[row][col])
-        out_ref[tile] = terms_ref[tile] + weight * same
-        out_ref[tiles + tile] = terms_ref[tiles + tile] + weight * cross
-
-
-def last_inner_body(cols, rows, probe_outer, probe_inner, got_2, got_3, low_1_outer, low_1_inner,
-                    low_2_outer, low_2_inner, field_outer, field_inner, sorted_ref, turned_ref,
-                    part_ref, terms_ref, weights_ref, cos_ref, sin_ref,
-                    out_ref, halo_2_ref, halo_3_ref, low_ref):
-    tiles = 2 * cols
-    weight, weight_next = weights_ref[3:4, 0:1], weights_ref[4:5, 0:1]
-
-    def matrix(kind, tile):
-        return sorted_ref[kind * tiles + tile]
-
-    def rim(got_ref, low_before, col):
-        place = pl.ds(col * rows, rows)
-        own = 2.0 * product(low_before[place, :], matrix(RIM, cols + col))
-        return (got_ref[place, :].astype(jnp.float32) + own).astype(jnp.bfloat16)
-
-    fields = []
-    for col in range(cols):
-        field = part_ref[col] + 2.0 * product(rim(got_2, low_1_inner, col), turned_ref[col])
-        fields.append(field)
-        low_ref[pl.ds(col * rows, rows), :] = field.astype(jnp.bfloat16)
-    for tile in range(tiles):
-        row, col = divmod(tile, cols)
-        place = pl.ds(col * rows, rows)
-        if row == 0:
-            following = 2.0 * product(low_ref[place, :], matrix(VERT, cols + col))
-            vectors = weight_next * (following - field_outer[col])
-            probe = probe_outer[place, :]
-        else:
-            total = beside(cols, rows, low_ref, tile, matrix)
-            total += product(rim(got_3, low_2_inner, col), turned_ref[col])
-            following = 2.0 * total - field_inner[col] + kondo(
-                fields[col], cos_ref[pl.ds(tile, 1), :], sin_ref[pl.ds(tile, 1), :]
-            )
-            vectors = weight * fields[col] + weight_next * following
-            probe = probe_inner[place, :]
-        same, cross = overlap_terms(probe, vectors)
-        out_ref[tile] = terms_ref[tile] + same
-        out_ref[tiles + tile] = terms_ref[tiles + tile] + cross
-    for col in range(cols):
-        place = pl.ds(col * rows, rows)
-        halo_2_ref[col] = 2.0 * product(low_1_outer[place, :], matrix(RIM, col))
-        halo_3_ref[col] = 2.0 * product(low_2_outer[place, :], matrix(RIM, col))
+    places = [pl.ds(col * rows, rows) for col in range(cols)]
+    own = [
+        2.0 * product(probe_inner[places[col], :], sorted_ref[RIM * tiles + cols + col])
+        for col in range(cols)
+    ]
+    for col in range(cols):
+        share_ref[col] = 2.0 * product(probe_outer[places[col], :], sorted_ref[RIM * tiles + col])
+    sent = [
+        got_ref[pl.ds((cols + col) * rows, rows), :].astype(jnp.float32) for col in range(cols)
+    ]
+    rims = [(sent[col] + own[col]).astype(jnp.bfloat16) for col in range(cols)]
+    fields = [
+        part_ref[col] + 2.0 * product(rims[col], turned_ref[col]) for col in range(cols)
+    ]
+    lows = [field.astype(jnp.bfloat16) for field in fields]
+    verts = [product(lows[col], sorted_ref[VERT * tiles + cols + col]) for col in range(cols)]
+    for col in range(cols):
+        field_ref[col] = fields[col]
+        low_ref[places[col], :] = lows[col]
+        vert_ref[col] = 2.0 * verts[col]
 
 
 def row_sums(blocks):
@@ -326,44 +243,165 @@
     return blocks[0]
 
 
-def last_outer_body(cols, rows, probe_outer, probe_inner, got_ref, halo_2_ref, halo_3_ref,
-                    sorted_ref, turned_ref, part_ref, terms_ref, weights_ref, cos_ref, sin_ref,
-                    same_ref, cross_ref, out_ref, low_ref):
+def second_outer_body(cols, rows, got_ref, share_ref, vert_ref, sorted_ref, turned_ref, part_ref,
+                      field_before, cos_ref, sin_ref, rim_probe, weights_ref,
+                      field_ref, low_ref, next_ref, send_ref):
+    tiles = 2 * cols
+    places = [pl.ds(col * rows, rows) for col in range(cols)]
+    rims = [
+        (got_ref[places[col], :].astype(jnp.float32) + share_ref[col]).astype(jnp.bfloat16)
+        for col in range(cols)
+    ]
+    fields = [
+        part_ref[col] + 2.0 * product(rims[col], turned_ref[col]) for col in range(cols)
+    ]
+    for col in range(cols):
+        field_ref[col] = fields[col]
+        low_ref[places[col], :] = fields[col].astype(jnp.bfloat16)
+
+    def matrix(kind, source):
+        return sorted_ref[kind * tiles + source]
+
+    totals = [beside(cols, rows, low_ref, col, matrix) for col in range(cols)]
+    following = [
+        2.0 * totals[col] + vert_ref[col] + kondo(
+            fields[col], cos_ref[pl.ds(col, 1), :], sin_ref[pl.ds(col, 1), :]
+        ) - field_before[col]
+        for col in range(cols)
+    ]
+    crossed = [
+        product(following[col].astype(jnp.bfloat16), matrix(RIM, col)) for col in range(cols)
+    ]
+    terms = [overlap_terms(rim_probe[places[col], :], crossed[col]) for col in range(cols)]
+    sums = (2.0 * weights_ref[4:5, 0:1]) * row_sums(
+        [same for same, _ in terms] + [cross for _, cross in terms]
+    )
+    rest = sums - sums.astype(jnp.bfloat16).astype(jnp.float32)
+    for col in range(cols):
+        next_ref[col] = following[col]
+        send_ref[places[col], :] = part_ref[col].astype(jnp.bfloat16)
+    send_ref[pl.ds(cols * rows, 16), :] = jnp.concatenate([sums, rest], axis=0).astype(jnp.bfloat16)
+
+
+def second_rest_body(cols, rows, probe_outer, probe_inner, sorted_ref, terms_ref, weights_ref,
+                     cos_ref, sin_ref, field_outer, field_inner, low_outer, low_inner,
+                     field_before, next_ref, send_ref, out_ref):
+    tiles = 2 * cols
+
+    def matrix(kind, source):
+        return sorted_ref[kind * tiles + source]
+
+    for col in range(cols):
+        tile = cols + col
+        place = pl.ds(col * rows, rows)
+        total = local_hop(cols, rows, low_outer, low_inner, tile, matrix)
+        following = 2.0 * total - field_before[col] + kondo(
+            field_inner[col], cos_ref[pl.ds(tile, 1), :], sin_ref[pl.ds(tile, 1), :]
+        )
+        next_ref[col] = following
+        send_ref[place, :] = following.astype(jnp.bfloat16)
+    weight = weights_ref[2:3, 0:1]
+    for tile in range(tiles):
+        row, col = divmod(tile, cols)
+        probe = (probe_outer, probe_inner)[row][pl.ds(col * rows, rows), :]
+        same, cross = overlap_terms(probe, (field_outer, field_inner)[row][col])
+        out_ref[tile] = terms_ref[tile] + weight * same
+        out_ref[tiles + tile] = terms_ref[tiles + tile] + weight * cross
+
+
+def last_inner_body(cols, rows, probe_outer, probe_inner, got_2, got_3, low_1_outer, low_1_inner,
+                    low_2_outer, low_2_inner, field_outer, field_inner, sorted_ref, turned_outer,
+                    turned_inner, part_ref, terms_ref, weights_ref, cos_ref, sin_ref,
+                    out_ref, halo_2_ref, low_ref):
     tiles = 2 * cols
     weight, weight_next = weights_ref[3:4, 0:1], weights_ref[4:5, 0:1]
+    places = [pl.ds(col * rows, rows) for col in range(cols)]
 
     def matrix(kind, tile):
         return sorted_ref[kind * tiles + tile]
 
-    def halo(half, share_ref, col):
-        sent = got_ref[pl.ds((half * cols + col) * rows, rows), :].astype(jnp.float32)
-        return (sent + share_ref[col]).astype(jnp.bfloat16)
-
-    fields = []
-    for col in range(cols):
-        field = part_ref[col] + 2.0 * product(halo(0, halo_2_ref, col), turned_ref[col])
-        fields.append(field)
-        low_ref[pl.ds(col * rows, rows), :] = field.astype(jnp.bfloat16)
+    def rims(got_ref, low_before):
+        own = [
+            2.0 * product(low_before[places[col], :], matrix(RIM, cols + col))
+            for col in range(cols)
+        ]
+        return [
+            (got_ref[places[col], :].astype(jnp.float32) + own[col]).astype(jnp.bfloat16)
+            for col in range(cols)
+        ]
+
+    rim_2, rim_3 = rims(got_2, low_1_inner), rims(got_3, low_2_inner)
+    crossed = [
+        (2.0 * product(low_2_outer[places[col], :], matrix(RIM, col))).astype(jnp.bfloat16)
+        for col in range(cols)
+    ]
+    fields = [
+        part_ref[col] + 2.0 * product(rim_2[col], turned_inner[col]) for col in range(cols)
+    ]
+    for col in range(cols):
+        low_ref[places[col], :] = fields[col].astype(jnp.bfloat16)
+        halo_2_ref[col] = 2.0 * product(low_1_outer[places[col], :], matrix(RIM, col))
+    for tile in range(tiles):
+        row, col = divmod(tile, cols)
+        if row == 0:
+            total = product(low_ref[places[col], :], matrix(VERT, cols + col))
+            total += product(crossed[col], turned_outer[col])
+            vectors = weight_next * (2.0 * total - field_outer[col])
+            probe = probe_outer[places[col], :]
+        else:
+            total = beside(cols, rows, low_ref, tile, matrix)
+            total += product(rim_3[col], turned_inner[col])
+            following = 2.0 * total - field_inner[col] + kondo(
+                fields[col], cos_ref[pl.ds(tile, 1), :], sin_ref[pl.ds(tile, 1), :]
+            )
+            vectors = weight * fields[col] + weight_next * following
+            probe = probe_inner[places[col], :]
+        same, cross = overlap_terms(probe, vectors)
+        out_ref[tile] = terms_ref[tile] + same
+        out_ref[tiles + tile] = terms_ref[tiles + tile] + cross
+
+
+def last_outer_body(cols, rows, probe_outer, probe_inner, got_ref, halo_2_ref, sorted_ref,
+                    turned_ref, part_ref, terms_ref, weights_ref, cos_ref, sin_ref, same_ref,
+                    cross_ref, out_ref, low_ref):
+    tiles = 2 * cols
+    weight, weight_next = weights_ref[3:4, 0:1], weights_ref[4:5, 0:1]
+    places = [pl.ds(col * rows, rows) for col in range(cols)]
+
+    def matrix(kind, tile):
+        return sorted_ref[kind * tiles + tile]
+
+    rims = [
+        (got_ref[places[col], :].astype(jnp.float32) + halo_2_ref[col]).astype(jnp.bfloat16)
+        for col in range(cols)
+    ]
+    fields = [
+        part_ref[col] + 2.0 * product(rims[col], turned_ref[col]) for col in range(cols)
+    ]
+    for col in range(cols):
+        low_ref[places[col], :] = fields[col].astype(jnp.bfloat16)
+    totals = [beside(cols, rows, low_ref, col, matrix) for col in range(cols)]
+    verts = [product(low_ref[places[col], :], matrix(VERT, col)) for col in range(cols)]
     shares = []
     for tile in range(tiles):
         row, col = divmod(tile, cols)
-        place = pl.ds(col * rows, rows)
         one = pl.ds(tile, 1)
         if row == 0:
-            total = beside(cols, rows, low_ref, tile, matrix)
-            total += product(halo(1, halo_3_ref, col), turned_ref[col])
-            following = 2.0 * total + kondo(fields[col], cos_ref[one, :], sin_ref[one, :])
+            following = 2.0 * totals[col] + kondo(fields[col], cos_ref[one, :], sin_ref[one, :])
             vectors = weight * fields[col] + weight_next * following
-            probe = probe_outer[place, :]
+            probe = probe_outer[places[col], :]
         else:
-            vectors = (2.0 * weight_next) * product(low_ref[place, :], matrix(VERT, col))
-            probe = probe_inner[place, :]
+            vectors = (2.0 * weight_next) * verts[col]
+            probe = probe_inner[places[col], :]
         same, cross = overlap_terms(probe, vectors)
         shares.append(
             same_ref[one, :] * (terms_ref[tile] + same)
             + cross_ref[one, :] * (terms_ref[tiles + tile] + cross)
         )
-    share = row_sums(shares)
+    sent = got_ref[pl.ds(cols * rows, 16), :].astype(jnp.float32)
+    sent = sent[:tiles] + sent[tiles:]
+    across = same_ref[:cols, :] * sent[:cols] + cross_ref[:cols, :] * sent[cols:]
+    share = row_sums(shares) + jnp.concatenate([across, jnp.zeros_like(across)], axis=0)
     for peer in range(out_ref.shape[0]):
         out_ref[peer] = share
 
@@ -476,27 +514,28 @@
         second_inner_body, [row, side, row, row],
         [*probe_rows, from_inner, sorted_hop, turned_inner, part_inner],
     )
-    field_2_outer, low_2_outer, part_outer, send_pair = run(
-        second_outer_body, [row, side, row, pair],
-        [got_1, rim_share, vert, sorted_hop, turned_outer, part_outer, field_1_outer, *trig],
-    )
-    got_pair = exchange_outer(send_pair)
+    field_2_outer, low_2_outer, part_outer, send = run(
+        second_outer_body, [row, side, row, ((cols * rows + 16, width), bf16)],
+        [got_1, rim_share, vert, sorted_hop, turned_outer, part_outer, field_1_outer, *trig,
+         got_0, weights],
+    )
+    got_2 = exchange_outer(send)
     part_inner, send, terms = run(
         second_rest_body, [row, side, terms_like],
         [*probe_rows, sorted_hop, terms, weights, *trig, field_2_outer, field_2_inner,
          low_2_outer, low_2_inner, field_1_inner],
     )
     inner_3 = exchange_inner(send)
-    terms, halo_2, halo_3 = run(
-        last_inner_body, [terms_like, row, row],
+    terms, halo_2 = run(
+        last_inner_body, [terms_like, row],
         [*probe_rows, inner_2, inner_3, low_1_outer, low_1_inner, low_2_outer, low_2_inner,
-         field_2_outer, field_2_inner, sorted_hop, turned_inner, part_inner, terms, weights,
-         *trig],
+         field_2_outer, field_2_inner, sorted_hop, turned_outer, turned_inner, part_inner,
+         terms, weights, *trig],
         scratch=[pltpu.VMEM(*side)],
     )
     shares = run(
         last_outer_body, [((2 * peers, tiles, width), f32)],
-        [*probe_rows, got_pair, halo_2, halo_3, sorted_hop, turned_outer, part_outer, terms,
+        [*probe_rows, got_2, halo_2, sorted_hop, turned_outer, part_outer, terms,
          weights, *trig, same_factor, cross_factor],
         scratch=[pltpu.VMEM(*side)], flops=local_flops,
     )[0]

time: 74.6 us -> 73 us (0.979)
  Pallas kernels: 10.1 us -> 9.14 us
    pallas_call x9, Pallas kernels: 8.09 us -> 7.13 us  [call(): pl.pallas_call(body, out_shape=[pltpu.VMEM(shape, dtype) for shape, dtype...]
  transfers between devices with their start and end apart: 7 -> 7, of which waited for: 3 -> 3; matrix products, arithmetic and copies ran while one was open for 0% -> 0% of each run, Pallas kernels for 8% -> 7%
where the time goes in v6:
time: 73 us; the launch traced here: 72.6 us
  starting transfers between devices  35 us (48%)
  blocking collectives  18.2 us (25%)
  waiting for transfers between devices  9.48 us (13%)
  Pallas kernels  9.14 us (13%)
  between operations  0.84 us (1%)
    ppermute x3, starting transfers between devices, exchange_inner(): lax.ppermute(inner, 'site', [(i, i ^ 1) for i in range(lax.axis_size('sit...  21.5 us
    all_to_all x1, blocking collectives, local(): largest = lax.all_to_all(largest, 'site', 0, 0, axis_index_groups=halves)  18.2 us
    ppermute x3, starting transfers between devices, exchange_outer(): return lax.ppermute(outer, 'site', pairs)  8.91 us
    pallas_call x9, Pallas kernels, call(): pl.pallas_call(body, out_shape=[pltpu.VMEM(shape, dtype) for shape, dtype...  7.13 us
    all_to_all x1, waiting for transfers between devices, local(): lax.all_to_all(shares, ('site', 'probe'), 0, 0, axis_index_groups=pairs)  6.85 us
    all_to_all x1, starting transfers between devices, local(): lax.all_to_all(shares, ('site', 'probe'), 0, 0, axis_index_groups=pairs)  4.62 us
    ppermute x3, waiting for transfers between devices, exchange_inner(): lax.ppermute(inner, 'site', [(i, i ^ 1) for i in range(lax.axis_size('sit...  2.62 us
  transfers between devices with their start and end apart: 7, of which 3 were waited for; matrix products, arithmetic and copies ran while one was open for 0% of the time, Pallas kernels for 7%

profile of v6, /device:TPU:1, one launch (start us, length us, event | category | flops | bytes accessed | tf_op | source)
XLA Modules:
  0.0 72.6 jit_solution(6840855041422756729)
XLA Ops:
  0.6 0.0 copy-start
  0.7 1.3 %shard_map.86 = (bf16[512,256]{1,0:T(8,128)(2,1)S(1)}, bf16[512,256]{1,0:T(8,128)(2,1)S(1)}, s32[2,4,4]{2,1,0:T(4,128)S(4)}, f32[5]{0:T(128)S(4)}, f32[2,4,256]{2,1,0:T(4,128)S(1)}, /*index=5*/f32[2,4,256]{2,1,0:T(4,128)S(1)}) custom-call(s32[1]{0:T(128)} %bitcast.parity_ref, bf16[2,512,256]{2,1,0:T(8,128)(2,1)} %bitcast.5, s32[2,4,4]{2,1,0:T(4,128)} %offsets_hbm.1, ...), custom_call_target="tpu_custom_call" | custom-call | flops 8053063680 | tf_op jit(solution)/shard_map/pallas_call | solution.py:469
  1.9 5.1 %collective-permute-start.2 = (bf16[512,256]{1,0:T(8,128)(2,1)S(1)}, bf16[512,256]{1,0:T(8,128)(2,1)S(1)}, u32[]{:S(2)}, u32[]{:S(2)}) collective-permute-start(bf16[512,256]{1,0:T(8,128)(2,1)S(1)} %get-tuple-element.43.outer_ref.probe_outer), channel_id=1, source_target_pairs={{0,504},{8,16},{16,8},{24,32},{32,24},{40,48},{48,40},{56,64},{64,... | collective-permute-start | bytes 786440 | tf_op jit(solution)/shard_map/ppermute | solution.py:438
  7.0 0.0 copy-done
  7.0 0.9 %shard_map.87 = (bf16[32,256,256]{2,1,0:T(8,128)(2,1)S(1)}, f32[4,128,256]{2,1,0:T(8,128)S(1)}, f32[4,128,256]{2,1,0:T(8,128)S(1)}, bf16[512,256]{1,0:T(8,128)(2...) custom-call(s32[1]{0:T(128)} %bitcast.parity_ref, ...), custom_call_target="tpu_custom_call" | custom-call | flops 402653184 | bytes 4194304 | tf_op jit(solution)/shard_map/pallas_call | solution.py:24
  7.9 1.9 %collective-permute-start = (bf16[512,256]{1,0:T(8,128)(2,1)S(1)}, bf16[512,256]{1,0:T(8,128)(2,1)S(1)}, u32[]{:S(2)}, u32[]{:S(2)}) collective-permute-start(bf16[512,256]{1,0:T(8,128)(2,1)S(1)} %get-tuple-element.49), channel_id=1, source_target_pairs={{0,504},{8,16},{16,8},{24,32},{32,24},{40,48},{48,40},{56,64},{64,... | collective-permute-start | bytes 786440 | tf_op jit(solution)/shard_map/ppermute | solution.py:438
  9.8 11.9 %collective-permute-start.1 = (bf16[1024,256]{1,0:T(8,128)(2,1)S(1)}, bf16[1024,256]{1,0:T(8,128)(2,1)S(1)}, u32[]{:S(2)}, u32[]{:S(2)}) collective-permute-start(bf16[1024,256]{1,0:T(8,128)(2,1)S(1)} %get-tuple-element.50), channel_id=1, source_target_pairs={{0,8},{8,0},{16,24},{24,16},{32,40},{40,32},{48,56},{56,48},{64,72... | collective-permute-start | bytes 1572872 | tf_op jit(solution)/shard_map/ppermute | solution.py:442
  21.8 0.0 collective-permute-done.2.got_ref.rim_probe
  21.8 0.4 shard_map.88
  22.2 1.1 %collective-permute-done.1.got_ref = bf16[1024,256]{1,0:T(8,128)(2,1)S(1)} collective-permute-done((bf16[1024,256]{1,0:T(8,128)(2,1)S(1)}, bf16[1024,256]{1,0:T(8,128)(2,1)S(1)}, u32[]{:S(2)}, u32[]{:S(2)}) %collective-permute-start.1) | collective-permute-done | bytes 524320 | tf_op jit(solution)/shard_map/ppermute | solution.py:442
  23.3 1.2 %shard_map.89 = (f32[4,128,256]{2,1,0:T(8,128)S(1)}, bf16[512,256]{1,0:T(8,128)(2,1)S(1)}, f32[4,128,256]{2,1,0:T(8,128)S(1)}, f32[4,128,256]{2,1,0:T(8,128)S(1)...) custom-call(bf16[512,256]{1,0:T(8,128)(2,1)S(1)} %get-tuple-element.43.outer_ref.probe_o, ...), custom_call_target="tpu_custom_call" | custom-call | flops 402653184 | tf_op jit(solution)/shard_map/pallas_call | solution.py:24
  24.5 0.5 shard_map.90
  25.0 0.0 collective-permute-done.got_ref
  25.0 0.7 shard_map.91
  25.8 1.9 %collective-permute-start.3 = (bf16[528,256]{1,0:T(8,128)(2,1)S(1)}, bf16[528,256]{1,0:T(8,128)(2,1)S(1)}, u32[]{:S(2)}, u32[]{:S(2)}) collective-permute-start(bf16[528,256]{1,0:T(8,128)(2,1)S(1)} %get-tuple-element.65), channel_id=1, source_target_pairs={{0,504},{8,16},{16,8},{24,32},{32,24},{40,48},{48,40},{56,64},{64,... | collective-permute-start | bytes 811016 | tf_op jit(solution)/shard_map/ppermute | solution.py:438
  27.7 7.6 %collective-permute-start.4 = (bf16[512,256]{1,0:T(8,128)(2,1)S(1)}, bf16[512,256]{1,0:T(8,128)(2,1)S(1)}, u32[]{:S(2)}, u32[]{:S(2)}) collective-permute-start(bf16[512,256]{1,0:T(8,128)(2,1)S(1)} %get-tuple-element.66), channel_id=1, source_target_pairs={{0,8},{8,0},{16,24},{24,16},{32,40},{40,32},{48,56},{56,48},{64,72... | collective-permute-start | bytes 786440 | tf_op jit(solution)/shard_map/ppermute | solution.py:442
  35.3 0.6 shard_map.92
  35.9 1.9 %collective-permute-start.5 = (bf16[512,256]{1,0:T(8,128)(2,1)S(1)}, bf16[512,256]{1,0:T(8,128)(2,1)S(1)}, u32[]{:S(2)}, u32[]{:S(2)}) collective-permute-start(bf16[512,256]{1,0:T(8,128)(2,1)S(1)} %get-tuple-element.73), channel_id=1, source_target_pairs={{0,8},{8,0},{16,24},{24,16},{32,40},{40,32},{48,56},{56,48},{64,72... | collective-permute-start | bytes 786440 | tf_op jit(solution)/shard_map/ppermute | solution.py:442
  37.9 0.0 collective-permute-done.4.got_2
  37.9 1.5 %collective-permute-done.5.got_3 = bf16[512,256]{1,0:T(8,128)(2,1)S(1)} collective-permute-done((bf16[512,256]{1,0:T(8,128)(2,1)S(1)}, bf16[512,256]{1,0:T(8,128)(2,1)S(1)}, u32[]{:S(2)}, u32[]{:S(2)}) %collective-permute-start.5) | collective-permute-done | bytes 262176 | tf_op jit(solution)/shard_map/ppermute | solution.py:442
  39.4 1.2 %shard_map.93 = (f32[16,8,256]{2,1,0:T(8,128)S(1)}, f32[4,128,256]{2,1,0:T(8,128)S(1)}) custom-call(bf16[512,256]{1,0:T(8,128)(2,1)S(1)} %get-tuple-element.43.outer_ref.probe_outer, bf16[512,256]{1,0:T(8,128)(2,1)S(1)} %get-tuple-element.44.inner_ref.probe_inner, bf16[512,256]{1,0:T(8,128)(2,1)S(1)} %collective-permute-done.4.got_2, ...), custom_call_target="tpu_custom_call" | custom-call | tf_op jit(solution)/shard_map/pallas_call | solution.py:24
  40.6 0.0 copy-start.1
  40.6 0.0 copy-start.2
  40.6 0.0 collective-permute-done.3.got_ref
  40.7 1.4 %shard_map.94 = f32[16,8,256]{2,1,0:T(8,128)} custom-call(bf16[512,256]{1,0:T(8,128)(2,1)S(1)} %get-tuple-element.43.outer_ref.probe_outer, bf16[512,256]{1,0:T(8,128)(2,1)S(1)} %get-tuple-element.44.inner_ref.probe_inner, bf16[528,256]{1,0:T(8,128)(2,1)S(1)} %collective-permute-done.3.got_ref, f32[4,128,256]{2,1,0:T(8,128)S(1)} %get-tuple-element.77.halo_2_ref, ...), custom_call_target="tpu_custom_call" | custom-call | flops 402653184 | tf_op jit(solution)/shard_map/pallas_call | solution.py:24
  42.1 4.6 %all-to-all-start = ((f32[16,8,256]{2,1,0:T(8,128)}), f32[16,8,256]{2,1,0:T(8,128)S(1)}, u32[]{:S(2)}, u32[]{:S(2)}) async-start(f32[16,8,256]{2,1,0:T(8,128)} %shard_map.94), calls=%async_computation | async-start | bytes 262144 | tf_op jit(solution)/shard_map/all_to_all | solution.py:546
  46.7 6.9 %all-to-all-done.shares_ref = f32[16,8,256]{2,1,0:T(8,128)S(1)} async-done(((f32[16,8,256]{2,1,0:T(8,128)}), f32[16,8,256]{2,1,0:T(8,128)S(1)}, u32[]{:S(2)}, u32[]{:S(2)}) %all-to-all-start) | async-done | bytes 131104 | tf_op jit(solution)/shard_map/all_to_all | solution.py:546
  53.6 0.1 shard_map.95
  53.7 18.2 %all_to_all.10.largest_ref = f32[32,1,128]{2,1,0:T(1,128)S(1)} all-to-all(f32[32,1,128]{2,1,0:T(1,128)S(1)} %get-tuple-element.82), channel_id=1, replica_groups={{0,8,16,24,32,40,48,56,64,72,80,88,96,104,112,120,128,136,144,152,160,1..., dimensions={0} | all-to-all | bytes 32768 | tf_op jit(solution)/shard_map/all_to_all | solution.py:552
  71.9 0.0 copy-done.1
  71.9 0.0 copy-done.2
  71.9 0.7 %shard_map.96 = (f32[2,4,256]{2,1,0:T(4,128)}, f32[2,4,256]{2,1,0:T(4,128)}) custom-call(s32[1]{0:T(128)} %bitcast.parity_ref, f32[32,1,128]{2,1,0:T(1,128)S(1)} %all_to_all.10.largest_ref, f32[8,256]{1,0:T(8,128)S(1)} %get-tuple-element.83.force_ref, f32[2,4,256]{2,1,0:T(4,128)S(1)} %copy-done.1, f32[2,4,256]{2,1,0:T(4,128)S(1)} %copy-done.2), custom_call_target="tpu_custom_call" | custom-call | tf_op jit(solution)/shard_map/pallas_call | solution.py:553
Async XLA Ops:
  0.6 6.4 %copy-start = (bf16[2,4,4,256,256]{4,3,2,1,0:T(8,128)(2,1)S(1)}, bf16[2,4,4,256,256]{4,3,2,1,0:T(8,128)(2,1)}, u32[]{:S(2)}) copy-start(bf16[2,4,4,256,256]{4,3,2,1,0:T(8,128)(2,1)} %param.12) | copy-start | bytes 12582916
  1.9 19.9 %collective-permute-start.2 = (bf16[512,256]{1,0:T(8,128)(2,1)S(1)}, bf16[512,256]{1,0:T(8,128)(2,1)S(1)}, u32[]{:S(2)}, u32[]{:S(2)}) collective-permute-start(bf16[512,256]{1,0:T(8,128)(2,1)S(1)} %get-tuple-element.43.outer_ref.probe_outer), channel_id=1, source_target_pairs={{0,504},{8,16},{16,8},{24,32},{32,24},{40,48},{48,40},{56,64},{64,... | collective-permute-start | bytes 786440 | tf_op jit(solution)/shard_map/ppermute | solution.py:438
  7.9 17.1 %collective-permute-start = (bf16[512,256]{1,0:T(8,128)(2,1)S(1)}, bf16[512,256]{1,0:T(8,128)(2,1)S(1)}, u32[]{:S(2)}, u32[]{:S(2)}) collective-permute-start(bf16[512,256]{1,0:T(8,128)(2,1)S(1)} %get-tuple-element.49), channel_id=1, source_target_pairs={{0,504},{8,16},{16,8},{24,32},{32,24},{40,48},{48,40},{56,64},{64,... | collective-permute-start | bytes 786440 | tf_op jit(solution)/shard_map/ppermute | solution.py:438
  9.8 13.5 %collective-permute-start.1 = (bf16[1024,256]{1,0:T(8,128)(2,1)S(1)}, bf16[1024,256]{1,0:T(8,128)(2,1)S(1)}, u32[]{:S(2)}, u32[]{:S(2)}) collective-permute-start(bf16[1024,256]{1,0:T(8,128)(2,1)S(1)} %get-tuple-element.50), channel_id=1, source_target_pairs={{0,8},{8,0},{16,24},{24,16},{32,40},{40,32},{48,56},{56,48},{64,72... | collective-permute-start | bytes 1572872 | tf_op jit(solution)/shard_map/ppermute | solution.py:442
  25.8 14.9 %collective-permute-start.3 = (bf16[528,256]{1,0:T(8,128)(2,1)S(1)}, bf16[528,256]{1,0:T(8,128)(2,1)S(1)}, u32[]{:S(2)}, u32[]{:S(2)}) collective-permute-start(bf16[528,256]{1,0:T(8,128)(2,1)S(1)} %get-tuple-element.65), channel_id=1, source_target_pairs={{0,504},{8,16},{16,8},{24,32},{32,24},{40,48},{48,40},{56,64},{64,... | collective-permute-start | bytes 811016 | tf_op jit(solution)/shard_map/ppermute | solution.py:438
  27.7 10.2 %collective-permute-start.4 = (bf16[512,256]{1,0:T(8,128)(2,1)S(1)}, bf16[512,256]{1,0:T(8,128)(2,1)S(1)}, u32[]{:S(2)}, u32[]{:S(2)}) collective-permute-start(bf16[512,256]{1,0:T(8,128)(2,1)S(1)} %get-tuple-element.66), channel_id=1, source_target_pairs={{0,8},{8,0},{16,24},{24,16},{32,40},{40,32},{48,56},{56,48},{64,72... | collective-permute-start | bytes 786440 | tf_op jit(solution)/shard_map/ppermute | solution.py:442
  35.9 3.4 %collective-permute-start.5 = (bf16[512,256]{1,0:T(8,128)(2,1)S(1)}, bf16[512,256]{1,0:T(8,128)(2,1)S(1)}, u32[]{:S(2)}, u32[]{:S(2)}) collective-permute-start(bf16[512,256]{1,0:T(8,128)(2,1)S(1)} %get-tuple-element.73), channel_id=1, source_target_pairs={{0,8},{8,0},{16,24},{24,16},{32,40},{40,32},{48,56},{56,48},{64,72... | collective-permute-start | bytes 786440 | tf_op jit(solution)/shard_map/ppermute | solution.py:442
  40.6 31.3 %copy-start.1 = (f32[2,4,256]{2,1,0:T(4,128)S(1)}, f32[2,4,256]{2,1,0:T(4,128)}, u32[]{:S(2)}) copy-start(f32[2,4,256]{2,1,0:T(4,128)} %angles_ref.1) | copy-start | bytes 24580
  40.6 31.3 %copy-start.2 = (f32[2,4,256]{2,1,0:T(4,128)S(1)}, f32[2,4,256]{2,1,0:T(4,128)}, u32[]{:S(2)}) copy-start(f32[2,4,256]{2,1,0:T(4,128)} %noise_ref.1) | copy-start | bytes 24580
  42.1 11.5 %all-to-all-start = ((f32[16,8,256]{2,1,0:T(8,128)}), f32[16,8,256]{2,1,0:T(8,128)S(1)}, u32[]{:S(2)}, u32[]{:S(2)}) async-start(f32[16,8,256]{2,1,0:T(8,128)} %shard_map.94), calls=%async_computation | async-start | bytes 262144 | tf_op jit(solution)/shard_map/all_to_all | solution.py:546

commit v7 on v6

--- a/solution.py
+++ b/solution.py
@@ -539,16 +539,17 @@
          weights, *trig, same_factor, cross_factor],
         scratch=[pltpu.VMEM(*side)], flops=local_flops,
     )[0]
+    half = sites // 2
     pairs = [
-        [half * peers + peer for half in (i, i + sites // 2) for peer in range(peers)]
-        for i in range(sites // 2)
+        [strip * peers + peer for strip in (i, half + (i ^ 1)) for peer in range(peers)]
+        for i in range(half)
     ]
     shares = lax.all_to_all(shares, ("site", "probe"), 0, 0, axis_index_groups=pairs)
     force, largest = call(
         force_body, [row_like, ((sites // 2, 1, 128), f32)],
         [IN_SMEM, IN_VMEM], (upper, held(shares)),
     )
-    halves = [list(range(sites // 2)), list(range(sites // 2, sites))]
+    halves = [list(range(half)), list(range(half, sites))]
     largest = lax.all_to_all(largest, "site", 0, 0, axis_index_groups=halves)
     return pl.pallas_call(
         move_body,

time: 73 us -> 72.6 us (level)
  blocking collectives: 18.2 us -> 16.6 us
    all_to_all x1, blocking collectives: 18.2 us -> 16.6 us  [local(): largest = lax.all_to_all(largest, 'site', 0, 0, axis_index_groups=halves)]
where the time goes in v7:
time: 72.6 us; the launch traced here: 72.2 us
  starting transfers between devices  35.6 us (49%)
  blocking collectives  16.6 us (23%)
  waiting for transfers between devices  10.1 us (14%)
  Pallas kernels  9.14 us (13%)
  between operations  0.84 us (1%)
    ppermute x3, starting transfers between devices, exchange_inner(): lax.ppermute(inner, 'site', [(i, i ^ 1) for i in range(lax.axis_size('sit...  21.5 us
    all_to_all x1, blocking collectives, local(): largest = lax.all_to_all(largest, 'site', 0, 0, axis_index_groups=halves)  16.6 us
    ppermute x3, starting transfers between devices, exchange_outer(): return lax.ppermute(outer, 'site', pairs)  8.91 us
    all_to_all x1, waiting for transfers between devices, local(): lax.all_to_all(shares, ('site', 'probe'), 0, 0, axis_index_groups=pairs)  7.43 us
    pallas_call x9, Pallas kernels, call(): pl.pallas_call(body, out_shape=[pltpu.VMEM(shape, dtype) for shape, dtype...  7.13 us
    all_to_all x1, starting transfers between devices, local(): lax.all_to_all(shares, ('site', 'probe'), 0, 0, axis_index_groups=pairs)  5.18 us
    ppermute x3, waiting for transfers between devices, exchange_inner(): lax.ppermute(inner, 'site', [(i, i ^ 1) for i in range(lax.axis_size('sit...  2.62 us
  transfers between devices with their start and end apart: 7, of which 3 were waited for; matrix products, arithmetic and copies ran while one was open for 0% of the time, Pallas kernels for 7%

profile of v7, /device:TPU:1, one launch (start us, length us, event | category | flops | bytes accessed | tf_op | source)
XLA Modules:
  0.0 72.2 jit_solution(7756954095959273537)
XLA Ops:
  0.6 0.0 copy-start
  0.7 1.3 %shard_map.86 = (bf16[512,256]{1,0:T(8,128)(2,1)S(1)}, bf16[512,256]{1,0:T(8,128)(2,1)S(1)}, s32[2,4,4]{2,1,0:T(4,128)S(4)}, f32[5]{0:T(128)S(4)}, f32[2,4,256]{2,1,0:T(4,128)S(1)}, /*index=5*/f32[2,4,256]{2,1,0:T(4,128)S(1)}) custom-call(s32[1]{0:T(128)} %bitcast.parity_ref, bf16[2,512,256]{2,1,0:T(8,128)(2,1)} %bitcast.5, s32[2,4,4]{2,1,0:T(4,128)} %offsets_hbm.1, ...), custom_call_target="tpu_custom_call" | custom-call | flops 8053063680 | tf_op jit(solution)/shard_map/pallas_call | solution.py:469
  1.9 5.1 %collective-permute-start.2 = (bf16[512,256]{1,0:T(8,128)(2,1)S(1)}, bf16[512,256]{1,0:T(8,128)(2,1)S(1)}, u32[]{:S(2)}, u32[]{:S(2)}) collective-permute-start(bf16[512,256]{1,0:T(8,128)(2,1)S(1)} %get-tuple-element.43.outer_ref.probe_outer), channel_id=1, source_target_pairs={{0,504},{8,16},{16,8},{24,32},{32,24},{40,48},{48,40},{56,64},{64,... | collective-permute-start | bytes 786440 | tf_op jit(solution)/shard_map/ppermute | solution.py:438
  7.0 0.0 copy-done
  7.0 0.9 %shard_map.87 = (bf16[32,256,256]{2,1,0:T(8,128)(2,1)S(1)}, f32[4,128,256]{2,1,0:T(8,128)S(1)}, f32[4,128,256]{2,1,0:T(8,128)S(1)}, bf16[512,256]{1,0:T(8,128)(2...) custom-call(s32[1]{0:T(128)} %bitcast.parity_ref, ...), custom_call_target="tpu_custom_call" | custom-call | flops 402653184 | bytes 4194304 | tf_op jit(solution)/shard_map/pallas_call | solution.py:24
  7.9 1.9 %collective-permute-start = (bf16[512,256]{1,0:T(8,128)(2,1)S(1)}, bf16[512,256]{1,0:T(8,128)(2,1)S(1)}, u32[]{:S(2)}, u32[]{:S(2)}) collective-permute-start(bf16[512,256]{1,0:T(8,128)(2,1)S(1)} %get-tuple-element.49), channel_id=1, source_target_pairs={{0,504},{8,16},{16,8},{24,32},{32,24},{40,48},{48,40},{56,64},{64,... | collective-permute-start | bytes 786440 | tf_op jit(solution)/shard_map/ppermute | solution.py:438
  9.8 11.9 %collective-permute-start.1 = (bf16[1024,256]{1,0:T(8,128)(2,1)S(1)}, bf16[1024,256]{1,0:T(8,128)(2,1)S(1)}, u32[]{:S(2)}, u32[]{:S(2)}) collective-permute-start(bf16[1024,256]{1,0:T(8,128)(2,1)S(1)} %get-tuple-element.50), channel_id=1, source_target_pairs={{0,8},{8,0},{16,24},{24,16},{32,40},{40,32},{48,56},{56,48},{64,72... | collective-permute-start | bytes 1572872 | tf_op jit(solution)/shard_map/ppermute | solution.py:442
  21.8 0.0 collective-permute-done.2.got_ref.rim_probe
  21.8 0.4 shard_map.88
  22.2 1.1 %collective-permute-done.1.got_ref = bf16[1024,256]{1,0:T(8,128)(2,1)S(1)} collective-permute-done((bf16[1024,256]{1,0:T(8,128)(2,1)S(1)}, bf16[1024,256]{1,0:T(8,128)(2,1)S(1)}, u32[]{:S(2)}, u32[]{:S(2)}) %collective-permute-start.1) | collective-permute-done | bytes 524320 | tf_op jit(solution)/shard_map/ppermute | solution.py:442
  23.3 1.2 %shard_map.89 = (f32[4,128,256]{2,1,0:T(8,128)S(1)}, bf16[512,256]{1,0:T(8,128)(2,1)S(1)}, f32[4,128,256]{2,1,0:T(8,128)S(1)}, f32[4,128,256]{2,1,0:T(8,128)S(1)...) custom-call(bf16[512,256]{1,0:T(8,128)(2,1)S(1)} %get-tuple-element.43.outer_ref.probe_o, ...), custom_call_target="tpu_custom_call" | custom-call | flops 402653184 | tf_op jit(solution)/shard_map/pallas_call | solution.py:24
  24.5 0.5 shard_map.90
  25.0 0.0 collective-permute-done.got_ref
  25.0 0.7 shard_map.91
  25.8 1.9 %collective-permute-start.3 = (bf16[528,256]{1,0:T(8,128)(2,1)S(1)}, bf16[528,256]{1,0:T(8,128)(2,1)S(1)}, u32[]{:S(2)}, u32[]{:S(2)}) collective-permute-start(bf16[528,256]{1,0:T(8,128)(2,1)S(1)} %get-tuple-element.65), channel_id=1, source_target_pairs={{0,504},{8,16},{16,8},{24,32},{32,24},{40,48},{48,40},{56,64},{64,... | collective-permute-start | bytes 811016 | tf_op jit(solution)/shard_map/ppermute | solution.py:438
  27.7 7.6 %collective-permute-start.4 = (bf16[512,256]{1,0:T(8,128)(2,1)S(1)}, bf16[512,256]{1,0:T(8,128)(2,1)S(1)}, u32[]{:S(2)}, u32[]{:S(2)}) collective-permute-start(bf16[512,256]{1,0:T(8,128)(2,1)S(1)} %get-tuple-element.66), channel_id=1, source_target_pairs={{0,8},{8,0},{16,24},{24,16},{32,40},{40,32},{48,56},{56,48},{64,72... | collective-permute-start | bytes 786440 | tf_op jit(solution)/shard_map/ppermute | solution.py:442
  35.3 0.6 shard_map.92
  35.9 1.9 %collective-permute-start.5 = (bf16[512,256]{1,0:T(8,128)(2,1)S(1)}, bf16[512,256]{1,0:T(8,128)(2,1)S(1)}, u32[]{:S(2)}, u32[]{:S(2)}) collective-permute-start(bf16[512,256]{1,0:T(8,128)(2,1)S(1)} %get-tuple-element.73), channel_id=1, source_target_pairs={{0,8},{8,0},{16,24},{24,16},{32,40},{40,32},{48,56},{56,48},{64,72... | collective-permute-start | bytes 786440 | tf_op jit(solution)/shard_map/ppermute | solution.py:442
  37.9 0.0 collective-permute-done.4.got_2
  37.9 1.5 %collective-permute-done.5.got_3 = bf16[512,256]{1,0:T(8,128)(2,1)S(1)} collective-permute-done((bf16[512,256]{1,0:T(8,128)(2,1)S(1)}, bf16[512,256]{1,0:T(8,128)(2,1)S(1)}, u32[]{:S(2)}, u32[]{:S(2)}) %collective-permute-start.5) | collective-permute-done | bytes 262176 | tf_op jit(solution)/shard_map/ppermute | solution.py:442
  39.4 1.2 %shard_map.93 = (f32[16,8,256]{2,1,0:T(8,128)S(1)}, f32[4,128,256]{2,1,0:T(8,128)S(1)}) custom-call(bf16[512,256]{1,0:T(8,128)(2,1)S(1)} %get-tuple-element.43.outer_ref.probe_outer, bf16[512,256]{1,0:T(8,128)(2,1)S(1)} %get-tuple-element.44.inner_ref.probe_inner, bf16[512,256]{1,0:T(8,128)(2,1)S(1)} %collective-permute-done.4.got_2, ...), custom_call_target="tpu_custom_call" | custom-call | tf_op jit(solution)/shard_map/pallas_call | solution.py:24
  40.6 0.0 copy-start.1
  40.6 0.0 copy-start.2
  40.6 0.0 collective-permute-done.3.got_ref
  40.7 1.4 %shard_map.94 = f32[16,8,256]{2,1,0:T(8,128)} custom-call(bf16[512,256]{1,0:T(8,128)(2,1)S(1)} %get-tuple-element.43.outer_ref.probe_outer, bf16[512,256]{1,0:T(8,128)(2,1)S(1)} %get-tuple-element.44.inner_ref.probe_inner, bf16[528,256]{1,0:T(8,128)(2,1)S(1)} %collective-permute-done.3.got_ref, f32[4,128,256]{2,1,0:T(8,128)S(1)} %get-tuple-element.77.halo_2_ref, ...), custom_call_target="tpu_custom_call" | custom-call | flops 402653184 | tf_op jit(solution)/shard_map/pallas_call | solution.py:24
  42.1 5.2 %all-to-all-start = ((f32[16,8,256]{2,1,0:T(8,128)}), f32[16,8,256]{2,1,0:T(8,128)S(1)}, u32[]{:S(2)}, u32[]{:S(2)}) async-start(f32[16,8,256]{2,1,0:T(8,128)} %shard_map.94), calls=%async_computation | async-start | bytes 262144 | tf_op jit(solution)/shard_map/all_to_all | solution.py:547
  47.3 7.4 %all-to-all-done.shares_ref = f32[16,8,256]{2,1,0:T(8,128)S(1)} async-done(((f32[16,8,256]{2,1,0:T(8,128)}), f32[16,8,256]{2,1,0:T(8,128)S(1)}, u32[]{:S(2)}, u32[]{:S(2)}) %all-to-all-start) | async-done | bytes 131104 | tf_op jit(solution)/shard_map/all_to_all | solution.py:547
  54.7 0.1 shard_map.95
  54.9 16.6 %all_to_all.10.largest_ref = f32[32,1,128]{2,1,0:T(1,128)S(1)} all-to-all(f32[32,1,128]{2,1,0:T(1,128)S(1)} %get-tuple-element.82), channel_id=1, replica_groups={{0,8,16,24,32,40,48,56,64,72,80,88,96,104,112,120,128,136,144,152,160,1..., dimensions={0} | all-to-all | bytes 32768 | tf_op jit(solution)/shard_map/all_to_all | solution.py:553
  71.5 0.0 copy-done.1
  71.5 0.0 copy-done.2
  71.5 0.7 %shard_map.96 = (f32[2,4,256]{2,1,0:T(4,128)}, f32[2,4,256]{2,1,0:T(4,128)}) custom-call(s32[1]{0:T(128)} %bitcast.parity_ref, f32[32,1,128]{2,1,0:T(1,128)S(1)} %all_to_all.10.largest_ref, f32[8,256]{1,0:T(8,128)S(1)} %get-tuple-element.83.force_ref, f32[2,4,256]{2,1,0:T(4,128)S(1)} %copy-done.1, f32[2,4,256]{2,1,0:T(4,128)S(1)} %copy-done.2), custom_call_target="tpu_custom_call" | custom-call | tf_op jit(solution)/shard_map/pallas_call | solution.py:554
Async XLA Ops:
  0.6 6.4 %copy-start = (bf16[2,4,4,256,256]{4,3,2,1,0:T(8,128)(2,1)S(1)}, bf16[2,4,4,256,256]{4,3,2,1,0:T(8,128)(2,1)}, u32[]{:S(2)}) copy-start(bf16[2,4,4,256,256]{4,3,2,1,0:T(8,128)(2,1)} %param.12) | copy-start | bytes 12582916
  1.9 19.9 %collective-permute-start.2 = (bf16[512,256]{1,0:T(8,128)(2,1)S(1)}, bf16[512,256]{1,0:T(8,128)(2,1)S(1)}, u32[]{:S(2)}, u32[]{:S(2)}) collective-permute-start(bf16[512,256]{1,0:T(8,128)(2,1)S(1)} %get-tuple-element.43.outer_ref.probe_outer), channel_id=1, source_target_pairs={{0,504},{8,16},{16,8},{24,32},{32,24},{40,48},{48,40},{56,64},{64,... | collective-permute-start | bytes 786440 | tf_op jit(solution)/shard_map/ppermute | solution.py:438
  7.9 17.1 %collective-permute-start = (bf16[512,256]{1,0:T(8,128)(2,1)S(1)}, bf16[512,256]{1,0:T(8,128)(2,1)S(1)}, u32[]{:S(2)}, u32[]{:S(2)}) collective-permute-start(bf16[512,256]{1,0:T(8,128)(2,1)S(1)} %get-tuple-element.49), channel_id=1, source_target_pairs={{0,504},{8,16},{16,8},{24,32},{32,24},{40,48},{48,40},{56,64},{64,... | collective-permute-start | bytes 786440 | tf_op jit(solution)/shard_map/ppermute | solution.py:438
  9.8 13.5 %collective-permute-start.1 = (bf16[1024,256]{1,0:T(8,128)(2,1)S(1)}, bf16[1024,256]{1,0:T(8,128)(2,1)S(1)}, u32[]{:S(2)}, u32[]{:S(2)}) collective-permute-start(bf16[1024,256]{1,0:T(8,128)(2,1)S(1)} %get-tuple-element.50), channel_id=1, source_target_pairs={{0,8},{8,0},{16,24},{24,16},{32,40},{40,32},{48,56},{56,48},{64,72... | collective-permute-start | bytes 1572872 | tf_op jit(solution)/shard_map/ppermute | solution.py:442
  25.8 14.9 %collective-permute-start.3 = (bf16[528,256]{1,0:T(8,128)(2,1)S(1)}, bf16[528,256]{1,0:T(8,128)(2,1)S(1)}, u32[]{:S(2)}, u32[]{:S(2)}) collective-permute-start(bf16[528,256]{1,0:T(8,128)(2,1)S(1)} %get-tuple-element.65), channel_id=1, source_target_pairs={{0,504},{8,16},{16,8},{24,32},{32,24},{40,48},{48,40},{56,64},{64,... | collective-permute-start | bytes 811016 | tf_op jit(solution)/shard_map/ppermute | solution.py:438
  27.7 10.2 %collective-permute-start.4 = (bf16[512,256]{1,0:T(8,128)(2,1)S(1)}, bf16[512,256]{1,0:T(8,128)(2,1)S(1)}, u32[]{:S(2)}, u32[]{:S(2)}) collective-permute-start(bf16[512,256]{1,0:T(8,128)(2,1)S(1)} %get-tuple-element.66), channel_id=1, source_target_pairs={{0,8},{8,0},{16,24},{24,16},{32,40},{40,32},{48,56},{56,48},{64,72... | collective-permute-start | bytes 786440 | tf_op jit(solution)/shard_map/ppermute | solution.py:442
  35.9 3.4 %collective-permute-start.5 = (bf16[512,256]{1,0:T(8,128)(2,1)S(1)}, bf16[512,256]{1,0:T(8,128)(2,1)S(1)}, u32[]{:S(2)}, u32[]{:S(2)}) collective-permute-start(bf16[512,256]{1,0:T(8,128)(2,1)S(1)} %get-tuple-element.73), channel_id=1, source_target_pairs={{0,8},{8,0},{16,24},{24,16},{32,40},{40,32},{48,56},{56,48},{64,72... | collective-permute-start | bytes 786440 | tf_op jit(solution)/shard_map/ppermute | solution.py:442
  40.6 30.9 %copy-start.1 = (f32[2,4,256]{2,1,0:T(4,128)S(1)}, f32[2,4,256]{2,1,0:T(4,128)}, u32[]{:S(2)}) copy-start(f32[2,4,256]{2,1,0:T(4,128)} %angles_ref.1) | copy-start | bytes 24580
  40.6 30.8 %copy-start.2 = (f32[2,4,256]{2,1,0:T(4,128)S(1)}, f32[2,4,256]{2,1,0:T(4,128)}, u32[]{:S(2)}) copy-start(f32[2,4,256]{2,1,0:T(4,128)} %noise_ref.1) | copy-start | bytes 24580
  42.1 12.6 %all-to-all-start = ((f32[16,8,256]{2,1,0:T(8,128)}), f32[16,8,256]{2,1,0:T(8,128)S(1)}, u32[]{:S(2)}, u32[]{:S(2)}) async-start(f32[16,8,256]{2,1,0:T(8,128)} %shard_map.94), calls=%async_computation | async-start | bytes 262144 | tf_op jit(solution)/shard_map/all_to_all | solution.py:547

commit v8 on v6

--- a/solution.py
+++ b/solution.py
@@ -406,17 +406,12 @@
         out_ref[peer] = share
 
 
-def force_body(upper_ref, shares_ref, force_ref, largest_ref):
-    peers = shares_ref.shape[0] // 2
-    strips = []
-    for strip in range(2):
-        total = shares_ref[strip * peers]
-        for peer in range(1, peers):
-            total += shares_ref[strip * peers + peer]
-        strips.append(total)
-    force_ref[...] = jnp.where(upper_ref[0] == 0, strips[0], strips[1])
-    largest = jnp.max(jnp.maximum(jnp.abs(strips[0]), jnp.abs(strips[1])))
-    largest_ref[...] = jnp.full(largest_ref.shape, largest, jnp.float32)
+def force_body(shares_ref, force_ref, largest_ref):
+    force = shares_ref[0]
+    for peer in range(1, shares_ref.shape[0]):
+        force += shares_ref[peer]
+    force_ref[...] = force
+    largest_ref[...] = jnp.full(largest_ref.shape, jnp.max(jnp.abs(force)), jnp.float32)
 
 
 def move_body(parity_ref, largest_ref, force_ref, angles_ref, noise_ref, next_ref, out_ref):
@@ -456,9 +451,7 @@
     sites, peers = lax.axis_size("site"), lax.axis_size("probe")
     probe_total = peers * share
     local_flops = 2 * 3 * tiles * rows * width * width
-    site = lax.axis_index("site")
-    parity = (site % 2).astype(jnp.int32).reshape(1)
-    upper = (site // (sites // 2)).astype(jnp.int32).reshape(1)
+    parity = (lax.axis_index("site") % 2).astype(jnp.int32).reshape(1)
 
     def run(body, outs, args, scratch=(), flops=0):
         return call(
@@ -534,22 +527,16 @@
         scratch=[pltpu.VMEM(*side)],
     )
     shares = run(
-        last_outer_body, [((2 * peers, tiles, width), f32)],
+        last_outer_body, [((peers, tiles, width), f32)],
         [*probe_rows, got_2, halo_2, sorted_hop, turned_outer, part_outer, terms,
          weights, *trig, same_factor, cross_factor],
         scratch=[pltpu.VMEM(*side)], flops=local_flops,
     )[0]
-    pairs = [
-        [half * peers + peer for half in (i, i + sites // 2) for peer in range(peers)]
-        for i in range(sites // 2)
-    ]
-    shares = lax.all_to_all(shares, ("site", "probe"), 0, 0, axis_index_groups=pairs)
+    shares = lax.all_to_all(shares, "probe", 0, 0)
     force, largest = call(
-        force_body, [row_like, ((sites // 2, 1, 128), f32)],
-        [IN_SMEM, IN_VMEM], (upper, held(shares)),
-    )
-    halves = [list(range(sites // 2)), list(range(sites // 2, sites))]
-    largest = lax.all_to_all(largest, "site", 0, 0, axis_index_groups=halves)
+        force_body, [row_like, ((sites, 1, 128), f32)], [IN_VMEM], (held(shares),)
+    )
+    largest = lax.all_to_all(largest, "site", 0, 0)
     return pl.pallas_call(
         move_body,
         out_shape=[jax.ShapeDtypeStruct(angles.shape, f32)] * 2,

time: 73 us -> 74.5 us (1.021)
  blocking collectives: 18.2 us -> 31.8 us
  waiting for transfers between devices: 9.48 us -> 2.63 us
  starting transfers between devices: 35 us -> 30.4 us
    all_to_all x1 -> x2, blocking collectives: 18.2 us -> 31.8 us  [the longest x1 22.7 us: local(): largest = lax.all_to_all(largest, 'site', 0, 0)]
    all_to_all x1 -> x0, waiting for transfers between devices: 6.85 us -> none  [local(): lax.all_to_all(shares, ('site', 'probe'), 0, 0, axis_index_groups=pairs)]
    all_to_all x1 -> x0, starting transfers between devices: 4.62 us -> none  [local(): lax.all_to_all(shares, ('site', 'probe'), 0, 0, axis_index_groups=pairs)]
  transfers between devices with their start and end apart: 7 -> 6, of which waited for: 3 -> 2; matrix products, arithmetic and copies ran while one was open for 0% -> 0% of each run, Pallas kernels for 7% -> 7%
where the time goes in v8:
time: 74.5 us; the launch traced here: 74.2 us
  blocking collectives  31.8 us (43%)
  starting transfers between devices  30.4 us (41%)
  Pallas kernels  8.51 us (11%)
  waiting for transfers between devices  2.63 us (4%)
  between operations  0.82 us (1%)
    all_to_all x1, blocking collectives, local(): largest = lax.all_to_all(largest, 'site', 0, 0)  22.7 us
    ppermute x3, starting transfers between devices, exchange_inner(): lax.ppermute(inner, 'site', [(i, i ^ 1) for i in range(lax.axis_size('sit...  21.5 us
    all_to_all x1, blocking collectives, local(): shares = lax.all_to_all(shares, 'probe', 0, 0)  9.13 us
    ppermute x3, starting transfers between devices, exchange_outer(): return lax.ppermute(outer, 'site', pairs)  8.91 us
    pallas_call x9, Pallas kernels, call(): pl.pallas_call(body, out_shape=[pltpu.VMEM(shape, dtype) for shape, dtype...  6.5 us
    ppermute x3, waiting for transfers between devices, exchange_inner(): lax.ppermute(inner, 'site', [(i, i ^ 1) for i in range(lax.axis_size('sit...  2.62 us
  transfers between devices with their start and end apart: 6, of which 2 were waited for; matrix products, arithmetic and copies ran while one was open for 0% of the time, Pallas kernels for 7%

profile of v8, /device:TPU:1, one launch (start us, length us, event | category | flops | bytes accessed | tf_op | source)
XLA Modules:
  0.0 74.2 jit_solution(15229239354392946290)
XLA Ops:
  0.6 0.0 copy-start
  0.7 1.3 %shard_map.86 = (bf16[512,256]{1,0:T(8,128)(2,1)S(1)}, bf16[512,256]{1,0:T(8,128)(2,1)S(1)}, s32[2,4,4]{2,1,0:T(4,128)S(4)}, f32[5]{0:T(128)S(4)}, f32[2,4,256]{2,1,0:T(4,128)S(1)}, /*index=5*/f32[2,4,256]{2,1,0:T(4,128)S(1)}) custom-call(s32[1]{0:T(128)} %bitcast.parity_ref, bf16[2,512,256]{2,1,0:T(8,128)(2,1)} %bitcast.4, s32[2,4,4]{2,1,0:T(4,128)} %offsets_hbm.1, ...), custom_call_target="tpu_custom_call" | custom-call | flops 8053063680 | tf_op jit(solution)/shard_map/pallas_call | solution.py:462
  1.9 5.1 %collective-permute-start.2 = (bf16[512,256]{1,0:T(8,128)(2,1)S(1)}, bf16[512,256]{1,0:T(8,128)(2,1)S(1)}, u32[]{:S(2)}, u32[]{:S(2)}) collective-permute-start(bf16[512,256]{1,0:T(8,128)(2,1)S(1)} %get-tuple-element.43.outer_ref.probe_outer), channel_id=1, source_target_pairs={{0,504},{8,16},{16,8},{24,32},{32,24},{40,48},{48,40},{56,64},{64,... | collective-permute-start | bytes 786440 | tf_op jit(solution)/shard_map/ppermute | solution.py:433
  7.0 0.0 copy-done
  7.0 0.9 %shard_map.87 = (bf16[32,256,256]{2,1,0:T(8,128)(2,1)S(1)}, f32[4,128,256]{2,1,0:T(8,128)S(1)}, f32[4,128,256]{2,1,0:T(8,128)S(1)}, bf16[512,256]{1,0:T(8,128)(2...) custom-call(s32[1]{0:T(128)} %bitcast.parity_ref, ...), custom_call_target="tpu_custom_call" | custom-call | flops 402653184 | bytes 4194304 | tf_op jit(solution)/shard_map/pallas_call | solution.py:24
  7.9 1.9 %collective-permute-start = (bf16[512,256]{1,0:T(8,128)(2,1)S(1)}, bf16[512,256]{1,0:T(8,128)(2,1)S(1)}, u32[]{:S(2)}, u32[]{:S(2)}) collective-permute-start(bf16[512,256]{1,0:T(8,128)(2,1)S(1)} %get-tuple-element.49), channel_id=1, source_target_pairs={{0,504},{8,16},{16,8},{24,32},{32,24},{40,48},{48,40},{56,64},{64,... | collective-permute-start | bytes 786440 | tf_op jit(solution)/shard_map/ppermute | solution.py:433
  9.8 11.9 %collective-permute-start.1 = (bf16[1024,256]{1,0:T(8,128)(2,1)S(1)}, bf16[1024,256]{1,0:T(8,128)(2,1)S(1)}, u32[]{:S(2)}, u32[]{:S(2)}) collective-permute-start(bf16[1024,256]{1,0:T(8,128)(2,1)S(1)} %get-tuple-element.50), channel_id=1, source_target_pairs={{0,8},{8,0},{16,24},{24,16},{32,40},{40,32},{48,56},{56,48},{64,72... | collective-permute-start | bytes 1572872 | tf_op jit(solution)/shard_map/ppermute | solution.py:437
  21.8 0.0 collective-permute-done.2.got_ref.rim_probe
  21.8 0.4 shard_map.88
  22.2 1.1 %collective-permute-done.1.got_ref = bf16[1024,256]{1,0:T(8,128)(2,1)S(1)} collective-permute-done((bf16[1024,256]{1,0:T(8,128)(2,1)S(1)}, bf16[1024,256]{1,0:T(8,128)(2,1)S(1)}, u32[]{:S(2)}, u32[]{:S(2)}) %collective-permute-start.1) | collective-permute-done | bytes 524320 | tf_op jit(solution)/shard_map/ppermute | solution.py:437
  23.3 1.2 %shard_map.89 = (f32[4,128,256]{2,1,0:T(8,128)S(1)}, bf16[512,256]{1,0:T(8,128)(2,1)S(1)}, f32[4,128,256]{2,1,0:T(8,128)S(1)}, f32[4,128,256]{2,1,0:T(8,128)S(1)...) custom-call(bf16[512,256]{1,0:T(8,128)(2,1)S(1)} %get-tuple-element.43.outer_ref.probe_o, ...), custom_call_target="tpu_custom_call" | custom-call | flops 402653184 | tf_op jit(solution)/shard_map/pallas_call | solution.py:24
  24.5 0.5 shard_map.90
  25.0 0.0 collective-permute-done.got_ref
  25.1 0.7 shard_map.91
  25.8 1.9 %collective-permute-start.3 = (bf16[528,256]{1,0:T(8,128)(2,1)S(1)}, bf16[528,256]{1,0:T(8,128)(2,1)S(1)}, u32[]{:S(2)}, u32[]{:S(2)}) collective-permute-start(bf16[528,256]{1,0:T(8,128)(2,1)S(1)} %get-tuple-element.65), channel_id=1, source_target_pairs={{0,504},{8,16},{16,8},{24,32},{32,24},{40,48},{48,40},{56,64},{64,... | collective-permute-start | bytes 811016 | tf_op jit(solution)/shard_map/ppermute | solution.py:433
  27.7 7.6 %collective-permute-start.4 = (bf16[512,256]{1,0:T(8,128)(2,1)S(1)}, bf16[512,256]{1,0:T(8,128)(2,1)S(1)}, u32[]{:S(2)}, u32[]{:S(2)}) collective-permute-start(bf16[512,256]{1,0:T(8,128)(2,1)S(1)} %get-tuple-element.66), channel_id=1, source_target_pairs={{0,8},{8,0},{16,24},{24,16},{32,40},{40,32},{48,56},{56,48},{64,72... | collective-permute-start | bytes 786440 | tf_op jit(solution)/shard_map/ppermute | solution.py:437
  35.3 0.6 shard_map.92
  35.9 1.9 %collective-permute-start.5 = (bf16[512,256]{1,0:T(8,128)(2,1)S(1)}, bf16[512,256]{1,0:T(8,128)(2,1)S(1)}, u32[]{:S(2)}, u32[]{:S(2)}) collective-permute-start(bf16[512,256]{1,0:T(8,128)(2,1)S(1)} %get-tuple-element.73), channel_id=1, source_target_pairs={{0,8},{8,0},{16,24},{24,16},{32,40},{40,32},{48,56},{56,48},{64,72... | collective-permute-start | bytes 786440 | tf_op jit(solution)/shard_map/ppermute | solution.py:437
  37.9 0.0 collective-permute-done.4.got_2
  37.9 1.5 %collective-permute-done.5.got_3 = bf16[512,256]{1,0:T(8,128)(2,1)S(1)} collective-permute-done((bf16[512,256]{1,0:T(8,128)(2,1)S(1)}, bf16[512,256]{1,0:T(8,128)(2,1)S(1)}, u32[]{:S(2)}, u32[]{:S(2)}) %collective-permute-start.5) | collective-permute-done | bytes 262176 | tf_op jit(solution)/shard_map/ppermute | solution.py:437
  39.4 1.2 %shard_map.93 = (f32[16,8,256]{2,1,0:T(8,128)S(1)}, f32[4,128,256]{2,1,0:T(8,128)S(1)}) custom-call(bf16[512,256]{1,0:T(8,128)(2,1)S(1)} %get-tuple-element.43.outer_ref.probe_outer, bf16[512,256]{1,0:T(8,128)(2,1)S(1)} %get-tuple-element.44.inner_ref.probe_inner, bf16[512,256]{1,0:T(8,128)(2,1)S(1)} %collective-permute-done.4.got_2, ...), custom_call_target="tpu_custom_call" | custom-call | tf_op jit(solution)/shard_map/pallas_call | solution.py:24
  40.6 0.0 copy-start.1
  40.6 0.0 copy-start.2
  40.6 0.0 collective-permute-done.3.got_ref
  40.7 0.8 %shard_map.94 = f32[8,8,256]{2,1,0:T(8,128)S(1)} custom-call(bf16[512,256]{1,0:T(8,128)(2,1)S(1)} %get-tuple-element.43.outer_ref.probe_outer, bf16[512,256]{1,0:T(8,128)(2,1)S(1)} %get-tuple-element.44.inner_ref.probe_inner, bf16[528,256]{1,0:T(8,128)(2,1)S(1)} %collective-permute-done.3.got_ref, f32[4,128,256]{2,1,0:T(8,128)S(1)} %get-tuple-element.77.halo_2_ref, ...), custom_call_target="tpu_custom_call" | custom-call | flops 402653184 | tf_op jit(solution)/shard_map/pallas_call | solution.py:24
  41.5 9.1 %all_to_all.10.shares_ref = f32[8,8,256]{2,1,0:T(8,128)S(1)} all-to-all(f32[8,8,256]{2,1,0:T(8,128)S(1)} %shard_map.94), channel_id=1, replica_groups=mesh['site'=64,'probe'=8] {'probe'}, dimensions={0} | all-to-all | bytes 131072 | tf_op jit(solution)/shard_map/all_to_all | solution.py:535
  50.6 0.1 shard_map.95
  50.7 22.7 %all_to_all.11.largest_ref = f32[64,1,128]{2,1,0:T(1,128)S(1)} all-to-all(f32[64,1,128]{2,1,0:T(1,128)S(1)} %get-tuple-element.82), channel_id=1, replica_groups=mesh['site'=64,'probe'=8] {'site'}, dimensions={0} | all-to-all | bytes 65536 | tf_op jit(solution)/shard_map/all_to_all | solution.py:539
  73.4 0.0 copy-done.1
  73.4 0.0 copy-done.2
  73.4 0.8 %shard_map.96 = (f32[2,4,256]{2,1,0:T(4,128)}, f32[2,4,256]{2,1,0:T(4,128)}) custom-call(s32[1]{0:T(128)} %bitcast.parity_ref, f32[64,1,128]{2,1,0:T(1,128)S(1)} %all_to_all.11.largest_ref, f32[8,256]{1,0:T(8,128)S(1)} %get-tuple-element.83.force_ref, f32[2,4,256]{2,1,0:T(4,128)S(1)} %copy-done.1, f32[2,4,256]{2,1,0:T(4,128)S(1)} %copy-done.2), custom_call_target="tpu_custom_call" | custom-call | tf_op jit(solution)/shard_map/pallas_call | solution.py:540
Async XLA Ops:
  0.6 6.3 %copy-start = (bf16[2,4,4,256,256]{4,3,2,1,0:T(8,128)(2,1)S(1)}, bf16[2,4,4,256,256]{4,3,2,1,0:T(8,128)(2,1)}, u32[]{:S(2)}) copy-start(bf16[2,4,4,256,256]{4,3,2,1,0:T(8,128)(2,1)} %param.12) | copy-start | bytes 12582916
  1.9 19.9 %collective-permute-start.2 = (bf16[512,256]{1,0:T(8,128)(2,1)S(1)}, bf16[512,256]{1,0:T(8,128)(2,1)S(1)}, u32[]{:S(2)}, u32[]{:S(2)}) collective-permute-start(bf16[512,256]{1,0:T(8,128)(2,1)S(1)} %get-tuple-element.43.outer_ref.probe_outer), channel_id=1, source_target_pairs={{0,504},{8,16},{16,8},{24,32},{32,24},{40,48},{48,40},{56,64},{64,... | collective-permute-start | bytes 786440 | tf_op jit(solution)/shard_map/ppermute | solution.py:433
  7.9 17.1 %collective-permute-start = (bf16[512,256]{1,0:T(8,128)(2,1)S(1)}, bf16[512,256]{1,0:T(8,128)(2,1)S(1)}, u32[]{:S(2)}, u32[]{:S(2)}) collective-permute-start(bf16[512,256]{1,0:T(8,128)(2,1)S(1)} %get-tuple-element.49), channel_id=1, source_target_pairs={{0,504},{8,16},{16,8},{24,32},{32,24},{40,48},{48,40},{56,64},{64,... | collective-permute-start | bytes 786440 | tf_op jit(solution)/shard_map/ppermute | solution.py:433
  9.8 13.5 %collective-permute-start.1 = (bf16[1024,256]{1,0:T(8,128)(2,1)S(1)}, bf16[1024,256]{1,0:T(8,128)(2,1)S(1)}, u32[]{:S(2)}, u32[]{:S(2)}) collective-permute-start(bf16[1024,256]{1,0:T(8,128)(2,1)S(1)} %get-tuple-element.50), channel_id=1, source_target_pairs={{0,8},{8,0},{16,24},{24,16},{32,40},{40,32},{48,56},{56,48},{64,72... | collective-permute-start | bytes 1572872 | tf_op jit(solution)/shard_map/ppermute | solution.py:437
  25.8 14.9 %collective-permute-start.3 = (bf16[528,256]{1,0:T(8,128)(2,1)S(1)}, bf16[528,256]{1,0:T(8,128)(2,1)S(1)}, u32[]{:S(2)}, u32[]{:S(2)}) collective-permute-start(bf16[528,256]{1,0:T(8,128)(2,1)S(1)} %get-tuple-element.65), channel_id=1, source_target_pairs={{0,504},{8,16},{16,8},{24,32},{32,24},{40,48},{48,40},{56,64},{64,... | collective-permute-start | bytes 811016 | tf_op jit(solution)/shard_map/ppermute | solution.py:433
  27.7 10.2 %collective-permute-start.4 = (bf16[512,256]{1,0:T(8,128)(2,1)S(1)}, bf16[512,256]{1,0:T(8,128)(2,1)S(1)}, u32[]{:S(2)}, u32[]{:S(2)}) collective-permute-start(bf16[512,256]{1,0:T(8,128)(2,1)S(1)} %get-tuple-element.66), channel_id=1, source_target_pairs={{0,8},{8,0},{16,24},{24,16},{32,40},{40,32},{48,56},{56,48},{64,72... | collective-permute-start | bytes 786440 | tf_op jit(solution)/shard_map/ppermute | solution.py:437
  35.9 3.4 %collective-permute-start.5 = (bf16[512,256]{1,0:T(8,128)(2,1)S(1)}, bf16[512,256]{1,0:T(8,128)(2,1)S(1)}, u32[]{:S(2)}, u32[]{:S(2)}) collective-permute-start(bf16[512,256]{1,0:T(8,128)(2,1)S(1)} %get-tuple-element.73), channel_id=1, source_target_pairs={{0,8},{8,0},{16,24},{24,16},{32,40},{40,32},{48,56},{56,48},{64,72... | collective-permute-start | bytes 786440 | tf_op jit(solution)/shard_map/ppermute | solution.py:437
  40.6 32.8 %copy-start.1 = (f32[2,4,256]{2,1,0:T(4,128)S(1)}, f32[2,4,256]{2,1,0:T(4,128)}, u32[]{:S(2)}) copy-start(f32[2,4,256]{2,1,0:T(4,128)} %angles_ref.1) | copy-start | bytes 24580
  40.6 32.8 %copy-start.2 = (f32[2,4,256]{2,1,0:T(4,128)S(1)}, f32[2,4,256]{2,1,0:T(4,128)}, u32[]{:S(2)}) copy-start(f32[2,4,256]{2,1,0:T(4,128)} %noise_ref.1) | copy-start | bytes 24580

commit v9 on v8

--- a/solution.py
+++ b/solution.py
@@ -536,7 +536,12 @@
     force, largest = call(
         force_body, [row_like, ((sites, 1, 128), f32)], [IN_VMEM], (held(shares),)
     )
-    largest = lax.all_to_all(largest, "site", 0, 0)
+    near = [
+        [strip * peers + (peer + strip // (sites // 2) * (peers // 2)) % peers
+         for strip in range(sites)]
+        for peer in range(peers)
+    ]
+    largest = lax.all_to_all(largest, ("site", "probe"), 0, 0, axis_index_groups=near)
     return pl.pallas_call(
         move_body,
         out_shape=[jax.ShapeDtypeStruct(angles.shape, f32)] * 2,

time: 74.5 us -> 73.3 us (0.984)
  blocking collectives: 31.8 us -> 30.6 us
    all_to_all x1, blocking collectives: 22.7 us -> 21.5 us  [local(): lax.all_to_all(largest, ('site', 'probe'), 0, 0, axis_index_groups=near)]
where the time goes in v9:
time: 73.3 us; the launch traced here: 73 us
  blocking collectives  30.6 us (42%)
  starting transfers between devices  30.4 us (41%)
  Pallas kernels  8.51 us (12%)
  waiting for transfers between devices  2.63 us (4%)
  between operations  0.82 us (1%)
    ppermute x3, starting transfers between devices, exchange_inner(): lax.ppermute(inner, 'site', [(i, i ^ 1) for i in range(lax.axis_size('sit...  21.5 us
    all_to_all x1, blocking collectives, local(): lax.all_to_all(largest, ('site', 'probe'), 0, 0, axis_index_groups=near)  21.5 us
    all_to_all x1, blocking collectives, local(): shares = lax.all_to_all(shares, 'probe', 0, 0)  9.13 us
    ppermute x3, starting transfers between devices, exchange_outer(): return lax.ppermute(outer, 'site', pairs)  8.91 us
    pallas_call x9, Pallas kernels, call(): pl.pallas_call(body, out_shape=[pltpu.VMEM(shape, dtype) for shape, dtype...  6.5 us
    ppermute x3, waiting for transfers between devices, exchange_inner(): lax.ppermute(inner, 'site', [(i, i ^ 1) for i in range(lax.axis_size('sit...  2.62 us
  transfers between devices with their start and end apart: 6, of which 2 were waited for; matrix products, arithmetic and copies ran while one was open for 0% of the time, Pallas kernels for 7%

profile of v9, /device:TPU:1, one launch (start us, length us, event | category | flops | bytes accessed | tf_op | source)
XLA Modules:
  0.0 73.0 jit_solution(6438664689878181004)
XLA Ops:
  0.6 0.0 copy-start
  0.7 1.3 %shard_map.86 = (bf16[512,256]{1,0:T(8,128)(2,1)S(1)}, bf16[512,256]{1,0:T(8,128)(2,1)S(1)}, s32[2,4,4]{2,1,0:T(4,128)S(4)}, f32[5]{0:T(128)S(4)}, f32[2,4,256]{2,1,0:T(4,128)S(1)}, /*index=5*/f32[2,4,256]{2,1,0:T(4,128)S(1)}) custom-call(s32[1]{0:T(128)} %bitcast.parity_ref, bf16[2,512,256]{2,1,0:T(8,128)(2,1)} %bitcast.4, s32[2,4,4]{2,1,0:T(4,128)} %offsets_hbm.1, ...), custom_call_target="tpu_custom_call" | custom-call | flops 8053063680 | tf_op jit(solution)/shard_map/pallas_call | solution.py:462
  1.9 5.1 %collective-permute-start.2 = (bf16[512,256]{1,0:T(8,128)(2,1)S(1)}, bf16[512,256]{1,0:T(8,128)(2,1)S(1)}, u32[]{:S(2)}, u32[]{:S(2)}) collective-permute-start(bf16[512,256]{1,0:T(8,128)(2,1)S(1)} %get-tuple-element.43.outer_ref.probe_outer), channel_id=1, source_target_pairs={{0,504},{8,16},{16,8},{24,32},{32,24},{40,48},{48,40},{56,64},{64,... | collective-permute-start | bytes 786440 | tf_op jit(solution)/shard_map/ppermute | solution.py:433
  7.0 0.0 copy-done
  7.0 0.9 %shard_map.87 = (bf16[32,256,256]{2,1,0:T(8,128)(2,1)S(1)}, f32[4,128,256]{2,1,0:T(8,128)S(1)}, f32[4,128,256]{2,1,0:T(8,128)S(1)}, bf16[512,256]{1,0:T(8,128)(2...) custom-call(s32[1]{0:T(128)} %bitcast.parity_ref, ...), custom_call_target="tpu_custom_call" | custom-call | flops 402653184 | bytes 4194304 | tf_op jit(solution)/shard_map/pallas_call | solution.py:24
  7.9 1.9 %collective-permute-start = (bf16[512,256]{1,0:T(8,128)(2,1)S(1)}, bf16[512,256]{1,0:T(8,128)(2,1)S(1)}, u32[]{:S(2)}, u32[]{:S(2)}) collective-permute-start(bf16[512,256]{1,0:T(8,128)(2,1)S(1)} %get-tuple-element.49), channel_id=1, source_target_pairs={{0,504},{8,16},{16,8},{24,32},{32,24},{40,48},{48,40},{56,64},{64,... | collective-permute-start | bytes 786440 | tf_op jit(solution)/shard_map/ppermute | solution.py:433
  9.8 11.9 %collective-permute-start.1 = (bf16[1024,256]{1,0:T(8,128)(2,1)S(1)}, bf16[1024,256]{1,0:T(8,128)(2,1)S(1)}, u32[]{:S(2)}, u32[]{:S(2)}) collective-permute-start(bf16[1024,256]{1,0:T(8,128)(2,1)S(1)} %get-tuple-element.50), channel_id=1, source_target_pairs={{0,8},{8,0},{16,24},{24,16},{32,40},{40,32},{48,56},{56,48},{64,72... | collective-permute-start | bytes 1572872 | tf_op jit(solution)/shard_map/ppermute | solution.py:437
  21.8 0.0 collective-permute-done.2.got_ref.rim_probe
  21.8 0.4 shard_map.88
  22.2 1.1 %collective-permute-done.1.got_ref = bf16[1024,256]{1,0:T(8,128)(2,1)S(1)} collective-permute-done((bf16[1024,256]{1,0:T(8,128)(2,1)S(1)}, bf16[1024,256]{1,0:T(8,128)(2,1)S(1)}, u32[]{:S(2)}, u32[]{:S(2)}) %collective-permute-start.1) | collective-permute-done | bytes 524320 | tf_op jit(solution)/shard_map/ppermute | solution.py:437
  23.3 1.2 %shard_map.89 = (f32[4,128,256]{2,1,0:T(8,128)S(1)}, bf16[512,256]{1,0:T(8,128)(2,1)S(1)}, f32[4,128,256]{2,1,0:T(8,128)S(1)}, f32[4,128,256]{2,1,0:T(8,128)S(1)...) custom-call(bf16[512,256]{1,0:T(8,128)(2,1)S(1)} %get-tuple-element.43.outer_ref.probe_o, ...), custom_call_target="tpu_custom_call" | custom-call | flops 402653184 | tf_op jit(solution)/shard_map/pallas_call | solution.py:24
  24.5 0.5 shard_map.90
  25.0 0.0 collective-permute-done.got_ref
  25.1 0.7 shard_map.91
  25.8 1.9 %collective-permute-start.3 = (bf16[528,256]{1,0:T(8,128)(2,1)S(1)}, bf16[528,256]{1,0:T(8,128)(2,1)S(1)}, u32[]{:S(2)}, u32[]{:S(2)}) collective-permute-start(bf16[528,256]{1,0:T(8,128)(2,1)S(1)} %get-tuple-element.65), channel_id=1, source_target_pairs={{0,504},{8,16},{16,8},{24,32},{32,24},{40,48},{48,40},{56,64},{64,... | collective-permute-start | bytes 811016 | tf_op jit(solution)/shard_map/ppermute | solution.py:433
  27.7 7.6 %collective-permute-start.4 = (bf16[512,256]{1,0:T(8,128)(2,1)S(1)}, bf16[512,256]{1,0:T(8,128)(2,1)S(1)}, u32[]{:S(2)}, u32[]{:S(2)}) collective-permute-start(bf16[512,256]{1,0:T(8,128)(2,1)S(1)} %get-tuple-element.66), channel_id=1, source_target_pairs={{0,8},{8,0},{16,24},{24,16},{32,40},{40,32},{48,56},{56,48},{64,72... | collective-permute-start | bytes 786440 | tf_op jit(solution)/shard_map/ppermute | solution.py:437
  35.3 0.6 shard_map.92
  35.9 1.9 %collective-permute-start.5 = (bf16[512,256]{1,0:T(8,128)(2,1)S(1)}, bf16[512,256]{1,0:T(8,128)(2,1)S(1)}, u32[]{:S(2)}, u32[]{:S(2)}) collective-permute-start(bf16[512,256]{1,0:T(8,128)(2,1)S(1)} %get-tuple-element.73), channel_id=1, source_target_pairs={{0,8},{8,0},{16,24},{24,16},{32,40},{40,32},{48,56},{56,48},{64,72... | collective-permute-start | bytes 786440 | tf_op jit(solution)/shard_map/ppermute | solution.py:437
  37.9 0.0 collective-permute-done.4.got_2
  37.9 1.5 %collective-permute-done.5.got_3 = bf16[512,256]{1,0:T(8,128)(2,1)S(1)} collective-permute-done((bf16[512,256]{1,0:T(8,128)(2,1)S(1)}, bf16[512,256]{1,0:T(8,128)(2,1)S(1)}, u32[]{:S(2)}, u32[]{:S(2)}) %collective-permute-start.5) | collective-permute-done | bytes 262176 | tf_op jit(solution)/shard_map/ppermute | solution.py:437
  39.4 1.2 %shard_map.93 = (f32[16,8,256]{2,1,0:T(8,128)S(1)}, f32[4,128,256]{2,1,0:T(8,128)S(1)}) custom-call(bf16[512,256]{1,0:T(8,128)(2,1)S(1)} %get-tuple-element.43.outer_ref.probe_outer, bf16[512,256]{1,0:T(8,128)(2,1)S(1)} %get-tuple-element.44.inner_ref.probe_inner, bf16[512,256]{1,0:T(8,128)(2,1)S(1)} %collective-permute-done.4.got_2, ...), custom_call_target="tpu_custom_call" | custom-call | tf_op jit(solution)/shard_map/pallas_call | solution.py:24
  40.6 0.0 copy-start.1
  40.6 0.0 copy-start.2
  40.6 0.0 collective-permute-done.3.got_ref
  40.7 0.8 %shard_map.94 = f32[8,8,256]{2,1,0:T(8,128)S(1)} custom-call(bf16[512,256]{1,0:T(8,128)(2,1)S(1)} %get-tuple-element.43.outer_ref.probe_outer, bf16[512,256]{1,0:T(8,128)(2,1)S(1)} %get-tuple-element.44.inner_ref.probe_inner, bf16[528,256]{1,0:T(8,128)(2,1)S(1)} %collective-permute-done.3.got_ref, f32[4,128,256]{2,1,0:T(8,128)S(1)} %get-tuple-element.77.halo_2_ref, ...), custom_call_target="tpu_custom_call" | custom-call | flops 402653184 | tf_op jit(solution)/shard_map/pallas_call | solution.py:24
  41.5 9.1 %all_to_all.10.shares_ref = f32[8,8,256]{2,1,0:T(8,128)S(1)} all-to-all(f32[8,8,256]{2,1,0:T(8,128)S(1)} %shard_map.94), channel_id=1, replica_groups=mesh['site'=64,'probe'=8] {'probe'}, dimensions={0} | all-to-all | bytes 131072 | tf_op jit(solution)/shard_map/all_to_all | solution.py:535
  50.6 0.1 shard_map.95
  50.7 21.5 %all_to_all.11.largest_ref = f32[64,1,128]{2,1,0:T(1,128)S(1)} all-to-all(f32[64,1,128]{2,1,0:T(1,128)S(1)} %get-tuple-element.82), channel_id=1, replica_groups={{0,8,16,24,32,40,48,56,64,72,80,88,96,104,112,120,128,136,144,152,160,1..., dimensions={0} | all-to-all | bytes 65536 | tf_op jit(solution)/shard_map/all_to_all | solution.py:544
  72.2 0.0 copy-done.1
  72.2 0.0 copy-done.2
  72.2 0.8 %shard_map.96 = (f32[2,4,256]{2,1,0:T(4,128)}, f32[2,4,256]{2,1,0:T(4,128)}) custom-call(s32[1]{0:T(128)} %bitcast.parity_ref, f32[64,1,128]{2,1,0:T(1,128)S(1)} %all_to_all.11.largest_ref, f32[8,256]{1,0:T(8,128)S(1)} %get-tuple-element.83.force_ref, f32[2,4,256]{2,1,0:T(4,128)S(1)} %copy-done.1, f32[2,4,256]{2,1,0:T(4,128)S(1)} %copy-done.2), custom_call_target="tpu_custom_call" | custom-call | tf_op jit(solution)/shard_map/pallas_call | solution.py:545
Async XLA Ops:
  0.6 6.3 %copy-start = (bf16[2,4,4,256,256]{4,3,2,1,0:T(8,128)(2,1)S(1)}, bf16[2,4,4,256,256]{4,3,2,1,0:T(8,128)(2,1)}, u32[]{:S(2)}) copy-start(bf16[2,4,4,256,256]{4,3,2,1,0:T(8,128)(2,1)} %param.12) | copy-start | bytes 12582916
  1.9 19.9 %collective-permute-start.2 = (bf16[512,256]{1,0:T(8,128)(2,1)S(1)}, bf16[512,256]{1,0:T(8,128)(2,1)S(1)}, u32[]{:S(2)}, u32[]{:S(2)}) collective-permute-start(bf16[512,256]{1,0:T(8,128)(2,1)S(1)} %get-tuple-element.43.outer_ref.probe_outer), channel_id=1, source_target_pairs={{0,504},{8,16},{16,8},{24,32},{32,24},{40,48},{48,40},{56,64},{64,... | collective-permute-start | bytes 786440 | tf_op jit(solution)/shard_map/ppermute | solution.py:433
  7.9 17.1 %collective-permute-start = (bf16[512,256]{1,0:T(8,128)(2,1)S(1)}, bf16[512,256]{1,0:T(8,128)(2,1)S(1)}, u32[]{:S(2)}, u32[]{:S(2)}) collective-permute-start(bf16[512,256]{1,0:T(8,128)(2,1)S(1)} %get-tuple-element.49), channel_id=1, source_target_pairs={{0,504},{8,16},{16,8},{24,32},{32,24},{40,48},{48,40},{56,64},{64,... | collective-permute-start | bytes 786440 | tf_op jit(solution)/shard_map/ppermute | solution.py:433
  9.8 13.5 %collective-permute-start.1 = (bf16[1024,256]{1,0:T(8,128)(2,1)S(1)}, bf16[1024,256]{1,0:T(8,128)(2,1)S(1)}, u32[]{:S(2)}, u32[]{:S(2)}) collective-permute-start(bf16[1024,256]{1,0:T(8,128)(2,1)S(1)} %get-tuple-element.50), channel_id=1, source_target_pairs={{0,8},{8,0},{16,24},{24,16},{32,40},{40,32},{48,56},{56,48},{64,72... | collective-permute-start | bytes 1572872 | tf_op jit(solution)/shard_map/ppermute | solution.py:437
  25.8 14.9 %collective-permute-start.3 = (bf16[528,256]{1,0:T(8,128)(2,1)S(1)}, bf16[528,256]{1,0:T(8,128)(2,1)S(1)}, u32[]{:S(2)}, u32[]{:S(2)}) collective-permute-start(bf16[528,256]{1,0:T(8,128)(2,1)S(1)} %get-tuple-element.65), channel_id=1, source_target_pairs={{0,504},{8,16},{16,8},{24,32},{32,24},{40,48},{48,40},{56,64},{64,... | collective-permute-start | bytes 811016 | tf_op jit(solution)/shard_map/ppermute | solution.py:433
  27.7 10.2 %collective-permute-start.4 = (bf16[512,256]{1,0:T(8,128)(2,1)S(1)}, bf16[512,256]{1,0:T(8,128)(2,1)S(1)}, u32[]{:S(2)}, u32[]{:S(2)}) collective-permute-start(bf16[512,256]{1,0:T(8,128)(2,1)S(1)} %get-tuple-element.66), channel_id=1, source_target_pairs={{0,8},{8,0},{16,24},{24,16},{32,40},{40,32},{48,56},{56,48},{64,72... | collective-permute-start | bytes 786440 | tf_op jit(solution)/shard_map/ppermute | solution.py:437
  35.9 3.4 %collective-permute-start.5 = (bf16[512,256]{1,0:T(8,128)(2,1)S(1)}, bf16[512,256]{1,0:T(8,128)(2,1)S(1)}, u32[]{:S(2)}, u32[]{:S(2)}) collective-permute-start(bf16[512,256]{1,0:T(8,128)(2,1)S(1)} %get-tuple-element.73), channel_id=1, source_target_pairs={{0,8},{8,0},{16,24},{24,16},{32,40},{40,32},{48,56},{56,48},{64,72... | collective-permute-start | bytes 786440 | tf_op jit(solution)/shard_map/ppermute | solution.py:437
  40.6 31.6 %copy-start.1 = (f32[2,4,256]{2,1,0:T(4,128)S(1)}, f32[2,4,256]{2,1,0:T(4,128)}, u32[]{:S(2)}) copy-start(f32[2,4,256]{2,1,0:T(4,128)} %angles_ref.1) | copy-start | bytes 24580
  40.6 31.6 %copy-start.2 = (f32[2,4,256]{2,1,0:T(4,128)S(1)}, f32[2,4,256]{2,1,0:T(4,128)}, u32[]{:S(2)}) copy-start(f32[2,4,256]{2,1,0:T(4,128)} %noise_ref.1) | copy-start | bytes 24580

commit v10 on v9

--- a/solution.py
+++ b/solution.py
@@ -406,12 +406,17 @@
         out_ref[peer] = share
 
 
-def force_body(shares_ref, force_ref, largest_ref):
-    force = shares_ref[0]
-    for peer in range(1, shares_ref.shape[0]):
-        force += shares_ref[peer]
-    force_ref[...] = force
-    largest_ref[...] = jnp.full(largest_ref.shape, jnp.max(jnp.abs(force)), jnp.float32)
+def force_body(parity_ref, shares_ref, force_ref, largest_ref):
+    peers = shares_ref.shape[0] // 2
+    strips = []
+    for strip in range(2):
+        total = shares_ref[strip * peers]
+        for peer in range(1, peers):
+            total += shares_ref[strip * peers + peer]
+        strips.append(total)
+    force_ref[...] = jnp.where(parity_ref[0] == 0, strips[0], strips[1])
+    largest = jnp.max(jnp.maximum(jnp.abs(strips[0]), jnp.abs(strips[1])))
+    largest_ref[...] = jnp.full(largest_ref.shape, largest, jnp.float32)
 
 
 def move_body(parity_ref, largest_ref, force_ref, angles_ref, noise_ref, next_ref, out_ref):
@@ -527,19 +532,21 @@
         scratch=[pltpu.VMEM(*side)],
     )
     shares = run(
-        last_outer_body, [((peers, tiles, width), f32)],
+        last_outer_body, [((2 * peers, tiles, width), f32)],
         [*probe_rows, got_2, halo_2, sorted_hop, turned_outer, part_outer, terms,
          weights, *trig, same_factor, cross_factor],
         scratch=[pltpu.VMEM(*side)], flops=local_flops,
     )[0]
-    shares = lax.all_to_all(shares, "probe", 0, 0)
+    chips = [list(range(i * 2 * peers, (i + 1) * 2 * peers)) for i in range(sites // 2)]
+    shares = lax.all_to_all(shares, ("site", "probe"), 0, 0, axis_index_groups=chips)
     force, largest = call(
-        force_body, [row_like, ((sites, 1, 128), f32)], [IN_VMEM], (held(shares),)
+        force_body, [row_like, ((sites // 2, 1, 128), f32)], [IN_SMEM, IN_VMEM],
+        (parity, held(shares)),
     )
     near = [
         [strip * peers + (peer + strip // (sites // 2) * (peers // 2)) % peers
-         for strip in range(sites)]
-        for peer in range(peers)
+         for strip in range(core, sites, 2)]
+        for core in range(2) for peer in range(peers)
     ]
     largest = lax.all_to_all(largest, ("site", "probe"), 0, 0, axis_index_groups=near)
     return pl.pallas_call(

time: 73.3 us -> 71.5 us (0.975)
  blocking collectives: 30.6 us -> 28.6 us
    all_to_all x1, blocking collectives: 21.5 us -> 17.4 us  [local(): lax.all_to_all(largest, ('site', 'probe'), 0, 0, axis_index_groups=near)]
    all_to_all x1, blocking collectives: 9.13 us -> 11.2 us  [local(): lax.all_to_all(shares, ('site', 'probe'), 0, 0, axis_index_groups=chips)]
where the time goes in v10:
time: 71.5 us; the launch traced here: 71 us
  starting transfers between devices  30.4 us (43%)
  blocking collectives  28.6 us (40%)
  Pallas kernels  8.5 us (12%)
  waiting for transfers between devices  2.63 us (4%)
  between operations  0.82 us (1%)
    ppermute x3, starting transfers between devices, exchange_inner(): lax.ppermute(inner, 'site', [(i, i ^ 1) for i in range(lax.axis_size('sit...  21.5 us
    all_to_all x1, blocking collectives, local(): lax.all_to_all(largest, ('site', 'probe'), 0, 0, axis_index_groups=near)  17.4 us
    all_to_all x1, blocking collectives, local(): lax.all_to_all(shares, ('site', 'probe'), 0, 0, axis_index_groups=chips)  11.2 us
    ppermute x3, starting transfers between devices, exchange_outer(): return lax.ppermute(outer, 'site', pairs)  8.91 us
    pallas_call x9, Pallas kernels, call(): pl.pallas_call(body, out_shape=[pltpu.VMEM(shape, dtype) for shape, dtype...  6.5 us
    ppermute x3, waiting for transfers between devices, exchange_inner(): lax.ppermute(inner, 'site', [(i, i ^ 1) for i in range(lax.axis_size('sit...  2.62 us
  transfers between devices with their start and end apart: 6, of which 2 were waited for; matrix products, arithmetic and copies ran while one was open for 0% of the time, Pallas kernels for 7%

profile of v10, /device:TPU:1, one launch (start us, length us, event | category | flops | bytes accessed | tf_op | source)
XLA Modules:
  0.0 71.0 jit_solution(13009275244394296437)
XLA Ops:
  0.6 0.0 copy-start
  0.7 1.3 %shard_map.86 = (bf16[512,256]{1,0:T(8,128)(2,1)S(1)}, bf16[512,256]{1,0:T(8,128)(2,1)S(1)}, s32[2,4,4]{2,1,0:T(4,128)S(4)}, f32[5]{0:T(128)S(4)}, f32[2,4,256]{2,1,0:T(4,128)S(1)}, /*index=5*/f32[2,4,256]{2,1,0:T(4,128)S(1)}) custom-call(s32[1]{0:T(128)} %bitcast.parity_ref, bf16[2,512,256]{2,1,0:T(8,128)(2,1)} %bitcast.4, s32[2,4,4]{2,1,0:T(4,128)} %offsets_hbm.1, ...), custom_call_target="tpu_custom_call" | custom-call | flops 8053063680 | tf_op jit(solution)/shard_map/pallas_call | solution.py:467
  1.9 5.1 %collective-permute-start.2 = (bf16[512,256]{1,0:T(8,128)(2,1)S(1)}, bf16[512,256]{1,0:T(8,128)(2,1)S(1)}, u32[]{:S(2)}, u32[]{:S(2)}) collective-permute-start(bf16[512,256]{1,0:T(8,128)(2,1)S(1)} %get-tuple-element.43.outer_ref.probe_outer), channel_id=1, source_target_pairs={{0,504},{8,16},{16,8},{24,32},{32,24},{40,48},{48,40},{56,64},{64,... | collective-permute-start | bytes 786440 | tf_op jit(solution)/shard_map/ppermute | solution.py:438
  7.0 0.0 copy-done
  7.0 0.9 %shard_map.87 = (bf16[32,256,256]{2,1,0:T(8,128)(2,1)S(1)}, f32[4,128,256]{2,1,0:T(8,128)S(1)}, f32[4,128,256]{2,1,0:T(8,128)S(1)}, bf16[512,256]{1,0:T(8,128)(2...) custom-call(s32[1]{0:T(128)} %bitcast.parity_ref, ...), custom_call_target="tpu_custom_call" | custom-call | flops 402653184 | bytes 4194304 | tf_op jit(solution)/shard_map/pallas_call | solution.py:24
  7.9 1.9 %collective-permute-start = (bf16[512,256]{1,0:T(8,128)(2,1)S(1)}, bf16[512,256]{1,0:T(8,128)(2,1)S(1)}, u32[]{:S(2)}, u32[]{:S(2)}) collective-permute-start(bf16[512,256]{1,0:T(8,128)(2,1)S(1)} %get-tuple-element.49), channel_id=1, source_target_pairs={{0,504},{8,16},{16,8},{24,32},{32,24},{40,48},{48,40},{56,64},{64,... | collective-permute-start | bytes 786440 | tf_op jit(solution)/shard_map/ppermute | solution.py:438
  9.8 11.9 %collective-permute-start.1 = (bf16[1024,256]{1,0:T(8,128)(2,1)S(1)}, bf16[1024,256]{1,0:T(8,128)(2,1)S(1)}, u32[]{:S(2)}, u32[]{:S(2)}) collective-permute-start(bf16[1024,256]{1,0:T(8,128)(2,1)S(1)} %get-tuple-element.50), channel_id=1, source_target_pairs={{0,8},{8,0},{16,24},{24,16},{32,40},{40,32},{48,56},{56,48},{64,72... | collective-permute-start | bytes 1572872 | tf_op jit(solution)/shard_map/ppermute | solution.py:442
  21.8 0.0 collective-permute-done.2.got_ref.rim_probe
  21.8 0.4 shard_map.88
  22.2 1.1 %collective-permute-done.1.got_ref = bf16[1024,256]{1,0:T(8,128)(2,1)S(1)} collective-permute-done((bf16[1024,256]{1,0:T(8,128)(2,1)S(1)}, bf16[1024,256]{1,0:T(8,128)(2,1)S(1)}, u32[]{:S(2)}, u32[]{:S(2)}) %collective-permute-start.1) | collective-permute-done | bytes 524320 | tf_op jit(solution)/shard_map/ppermute | solution.py:442
  23.3 1.2 %shard_map.89 = (f32[4,128,256]{2,1,0:T(8,128)S(1)}, bf16[512,256]{1,0:T(8,128)(2,1)S(1)}, f32[4,128,256]{2,1,0:T(8,128)S(1)}, f32[4,128,256]{2,1,0:T(8,128)S(1)...) custom-call(bf16[512,256]{1,0:T(8,128)(2,1)S(1)} %get-tuple-element.43.outer_ref.probe_o, ...), custom_call_target="tpu_custom_call" | custom-call | flops 402653184 | tf_op jit(solution)/shard_map/pallas_call | solution.py:24
  24.5 0.5 shard_map.90
  25.0 0.0 collective-permute-done.got_ref
  25.1 0.7 shard_map.91
  25.8 1.9 %collective-permute-start.3 = (bf16[528,256]{1,0:T(8,128)(2,1)S(1)}, bf16[528,256]{1,0:T(8,128)(2,1)S(1)}, u32[]{:S(2)}, u32[]{:S(2)}) collective-permute-start(bf16[528,256]{1,0:T(8,128)(2,1)S(1)} %get-tuple-element.65), channel_id=1, source_target_pairs={{0,504},{8,16},{16,8},{24,32},{32,24},{40,48},{48,40},{56,64},{64,... | collective-permute-start | bytes 811016 | tf_op jit(solution)/shard_map/ppermute | solution.py:438
  27.7 7.6 %collective-permute-start.4 = (bf16[512,256]{1,0:T(8,128)(2,1)S(1)}, bf16[512,256]{1,0:T(8,128)(2,1)S(1)}, u32[]{:S(2)}, u32[]{:S(2)}) collective-permute-start(bf16[512,256]{1,0:T(8,128)(2,1)S(1)} %get-tuple-element.66), channel_id=1, source_target_pairs={{0,8},{8,0},{16,24},{24,16},{32,40},{40,32},{48,56},{56,48},{64,72... | collective-permute-start | bytes 786440 | tf_op jit(solution)/shard_map/ppermute | solution.py:442
  35.3 0.6 shard_map.92
  35.9 1.9 %collective-permute-start.5 = (bf16[512,256]{1,0:T(8,128)(2,1)S(1)}, bf16[512,256]{1,0:T(8,128)(2,1)S(1)}, u32[]{:S(2)}, u32[]{:S(2)}) collective-permute-start(bf16[512,256]{1,0:T(8,128)(2,1)S(1)} %get-tuple-element.73), channel_id=1, source_target_pairs={{0,8},{8,0},{16,24},{24,16},{32,40},{40,32},{48,56},{56,48},{64,72... | collective-permute-start | bytes 786440 | tf_op jit(solution)/shard_map/ppermute | solution.py:442
  37.9 0.0 collective-permute-done.4.got_2
  37.9 1.5 %collective-permute-done.5.got_3 = bf16[512,256]{1,0:T(8,128)(2,1)S(1)} collective-permute-done((bf16[512,256]{1,0:T(8,128)(2,1)S(1)}, bf16[512,256]{1,0:T(8,128)(2,1)S(1)}, u32[]{:S(2)}, u32[]{:S(2)}) %collective-permute-start.5) | collective-permute-done | bytes 262176 | tf_op jit(solution)/shard_map/ppermute | solution.py:442
  39.4 1.2 %shard_map.93 = (f32[16,8,256]{2,1,0:T(8,128)S(1)}, f32[4,128,256]{2,1,0:T(8,128)S(1)}) custom-call(bf16[512,256]{1,0:T(8,128)(2,1)S(1)} %get-tuple-element.43.outer_ref.probe_outer, bf16[512,256]{1,0:T(8,128)(2,1)S(1)} %get-tuple-element.44.inner_ref.probe_inner, bf16[512,256]{1,0:T(8,128)(2,1)S(1)} %collective-permute-done.4.got_2, ...), custom_call_target="tpu_custom_call" | custom-call | tf_op jit(solution)/shard_map/pallas_call | solution.py:24
  40.6 0.0 copy-start.1
  40.6 0.0 copy-start.2
  40.6 0.0 collective-permute-done.3.got_ref
  40.7 0.8 %shard_map.94 = f32[16,8,256]{2,1,0:T(8,128)S(1)} custom-call(bf16[512,256]{1,0:T(8,128)(2,1)S(1)} %get-tuple-element.43.outer_ref.probe_outer, bf16[512,256]{1,0:T(8,128)(2,1)S(1)} %get-tuple-element.44.inner_ref.probe_inner, bf16[528,256]{1,0:T(8,128)(2,1)S(1)} %collective-permute-done.3.got_ref, f32[4,128,256]{2,1,0:T(8,128)S(1)} %get-tuple-element.77.halo_2_ref, ...), custom_call_target="tpu_custom_call" | custom-call | flops 402653184 | tf_op jit(solution)/shard_map/pallas_call | solution.py:24
  41.5 11.2 %all_to_all.10.shares_ref = f32[16,8,256]{2,1,0:T(8,128)S(1)} all-to-all(f32[16,8,256]{2,1,0:T(8,128)S(1)} %shard_map.94), channel_id=1, replica_groups={{0,1,2,3,4,5,6,7,8,9,10,11,12,13,14,15},{16,17,18,19,20,21,22,23,24,25,..., dimensions={0} | all-to-all | bytes 262144 | tf_op jit(solution)/shard_map/all_to_all | solution.py:541
  52.7 0.1 shard_map.95
  52.9 17.4 %all_to_all.11.largest_ref = f32[32,1,128]{2,1,0:T(1,128)S(1)} all-to-all(f32[32,1,128]{2,1,0:T(1,128)S(1)} %get-tuple-element.82), channel_id=1, replica_groups={{0,16,32,48,64,80,96,112,128,144,160,176,192,208,224,240,260,276,292,30..., dimensions={0} | all-to-all | bytes 32768 | tf_op jit(solution)/shard_map/all_to_all | solution.py:551
  70.2 0.0 copy-done.1
  70.2 0.0 copy-done.2
  70.2 0.7 %shard_map.96 = (f32[2,4,256]{2,1,0:T(4,128)}, f32[2,4,256]{2,1,0:T(4,128)}) custom-call(s32[1]{0:T(128)} %bitcast.parity_ref, f32[32,1,128]{2,1,0:T(1,128)S(1)} %all_to_all.11.largest_ref, f32[8,256]{1,0:T(8,128)S(1)} %get-tuple-element.83.force_ref, f32[2,4,256]{2,1,0:T(4,128)S(1)} %copy-done.1, f32[2,4,256]{2,1,0:T(4,128)S(1)} %copy-done.2), custom_call_target="tpu_custom_call" | custom-call | tf_op jit(solution)/shard_map/pallas_call | solution.py:552
Async XLA Ops:
  0.6 6.3 %copy-start = (bf16[2,4,4,256,256]{4,3,2,1,0:T(8,128)(2,1)S(1)}, bf16[2,4,4,256,256]{4,3,2,1,0:T(8,128)(2,1)}, u32[]{:S(2)}) copy-start(bf16[2,4,4,256,256]{4,3,2,1,0:T(8,128)(2,1)} %param.12) | copy-start | bytes 12582916
  1.9 19.9 %collective-permute-start.2 = (bf16[512,256]{1,0:T(8,128)(2,1)S(1)}, bf16[512,256]{1,0:T(8,128)(2,1)S(1)}, u32[]{:S(2)}, u32[]{:S(2)}) collective-permute-start(bf16[512,256]{1,0:T(8,128)(2,1)S(1)} %get-tuple-element.43.outer_ref.probe_outer), channel_id=1, source_target_pairs={{0,504},{8,16},{16,8},{24,32},{32,24},{40,48},{48,40},{56,64},{64,... | collective-permute-start | bytes 786440 | tf_op jit(solution)/shard_map/ppermute | solution.py:438
  7.9 17.1 %collective-permute-start = (bf16[512,256]{1,0:T(8,128)(2,1)S(1)}, bf16[512,256]{1,0:T(8,128)(2,1)S(1)}, u32[]{:S(2)}, u32[]{:S(2)}) collective-permute-start(bf16[512,256]{1,0:T(8,128)(2,1)S(1)} %get-tuple-element.49), channel_id=1, source_target_pairs={{0,504},{8,16},{16,8},{24,32},{32,24},{40,48},{48,40},{56,64},{64,... | collective-permute-start | bytes 786440 | tf_op jit(solution)/shard_map/ppermute | solution.py:438
  9.8 13.5 %collective-permute-start.1 = (bf16[1024,256]{1,0:T(8,128)(2,1)S(1)}, bf16[1024,256]{1,0:T(8,128)(2,1)S(1)}, u32[]{:S(2)}, u32[]{:S(2)}) collective-permute-start(bf16[1024,256]{1,0:T(8,128)(2,1)S(1)} %get-tuple-element.50), channel_id=1, source_target_pairs={{0,8},{8,0},{16,24},{24,16},{32,40},{40,32},{48,56},{56,48},{64,72... | collective-permute-start | bytes 1572872 | tf_op jit(solution)/shard_map/ppermute | solution.py:442
  25.8 14.9 %collective-permute-start.3 = (bf16[528,256]{1,0:T(8,128)(2,1)S(1)}, bf16[528,256]{1,0:T(8,128)(2,1)S(1)}, u32[]{:S(2)}, u32[]{:S(2)}) collective-permute-start(bf16[528,256]{1,0:T(8,128)(2,1)S(1)} %get-tuple-element.65), channel_id=1, source_target_pairs={{0,504},{8,16},{16,8},{24,32},{32,24},{40,48},{48,40},{56,64},{64,... | collective-permute-start | bytes 811016 | tf_op jit(solution)/shard_map/ppermute | solution.py:438
  27.7 10.2 %collective-permute-start.4 = (bf16[512,256]{1,0:T(8,128)(2,1)S(1)}, bf16[512,256]{1,0:T(8,128)(2,1)S(1)}, u32[]{:S(2)}, u32[]{:S(2)}) collective-permute-start(bf16[512,256]{1,0:T(8,128)(2,1)S(1)} %get-tuple-element.66), channel_id=1, source_target_pairs={{0,8},{8,0},{16,24},{24,16},{32,40},{40,32},{48,56},{56,48},{64,72... | collective-permute-start | bytes 786440 | tf_op jit(solution)/shard_map/ppermute | solution.py:442
  35.9 3.4 %collective-permute-start.5 = (bf16[512,256]{1,0:T(8,128)(2,1)S(1)}, bf16[512,256]{1,0:T(8,128)(2,1)S(1)}, u32[]{:S(2)}, u32[]{:S(2)}) collective-permute-start(bf16[512,256]{1,0:T(8,128)(2,1)S(1)} %get-tuple-element.73), channel_id=1, source_target_pairs={{0,8},{8,0},{16,24},{24,16},{32,40},{40,32},{48,56},{56,48},{64,72... | collective-permute-start | bytes 786440 | tf_op jit(solution)/shard_map/ppermute | solution.py:442
  40.6 29.6 %copy-start.1 = (f32[2,4,256]{2,1,0:T(4,128)S(1)}, f32[2,4,256]{2,1,0:T(4,128)}, u32[]{:S(2)}) copy-start(f32[2,4,256]{2,1,0:T(4,128)} %angles_ref.1) | copy-start | bytes 24580
  40.6 29.6 %copy-start.2 = (f32[2,4,256]{2,1,0:T(4,128)S(1)}, f32[2,4,256]{2,1,0:T(4,128)}, u32[]{:S(2)}) copy-start(f32[2,4,256]{2,1,0:T(4,128)} %noise_ref.1) | copy-start | bytes 24580

commit v11 on v10

--- a/solution.py
+++ b/solution.py
@@ -95,12 +95,9 @@
     )
 
 
-def first_body(cols, rows, probe_total, parity_ref, offsets_ref, coef_ref, raw_ref, angles_ref,
-               coupling_ref, outer_ref, inner_ref, sorted_ref, part_outer, part_inner, send_ref,
-               pair_ref, weights_ref, cos_ref, sin_ref, same_ref, cross_ref):
+def sorter(cols, parity, offsets_ref, raw_ref, sorted_ref):
     tiles = 2 * cols
     slots = offsets_ref.shape[2]
-    parity = parity_ref[0]
 
     def tile_of(kind, tile):
         row, col = divmod(tile, cols)
@@ -122,6 +119,14 @@
         sorted_ref[kind * tiles + tile] = found
         return found
 
+    return matrix
+
+
+def first_body(cols, rows, probe_total, parity_ref, offsets_ref, coef_ref, raw_ref, angles_ref,
+               coupling_ref, outer_ref, inner_ref, sorted_ref, part_ref, send_ref,
+               weights_ref, cos_ref, sin_ref, same_ref, cross_ref):
+    parity = parity_ref[0]
+    matrix = sorter(cols, parity, offsets_ref, raw_ref, sorted_ref)
     for row in range(2):
         origin = row + parity - 2 * row * parity
         place = pl.ds(row * cols, cols)
@@ -136,21 +141,37 @@
         weights_ref[pl.ds(level, 1), :] = jnp.full(
             (1, weights_ref.shape[1]), (level + 1) * coef_ref[level], jnp.float32
         )
-    for tile in range(tiles):
-        row, col = divmod(tile, cols)
+    for col in range(cols):
         place = pl.ds(col * rows, rows)
-        probe = (outer_ref, inner_ref)[row][place, :]
+        total = local_hop(cols, rows, outer_ref, inner_ref, col, matrix)
+        part = 2.0 * total + kondo(
+            outer_ref[place, :].astype(jnp.float32), cos_ref[pl.ds(col, 1), :],
+            sin_ref[pl.ds(col, 1), :]
+        )
+        part_ref[col] = part
+        send_ref[place, :] = part.astype(jnp.bfloat16)
+
+
+def first_rest_body(cols, rows, parity_ref, offsets_ref, raw_ref, outer_ref, inner_ref, cos_ref,
+                    sin_ref, before_ref, sorted_ref, part_ref, pair_ref):
+    tiles = 2 * cols
+    for kind in (VERT, LEFT, RIGHT):
+        for col in range(cols):
+            place = kind * tiles + col + (cols if kind == VERT else 0)
+            sorted_ref[place] = before_ref[place]
+    matrix = sorter(cols, parity_ref[0], offsets_ref, raw_ref, sorted_ref)
+    for col in range(cols):
+        place = pl.ds(col * rows, rows)
+        tile = cols + col
+        probe = inner_ref[place, :]
         total = local_hop(cols, rows, outer_ref, inner_ref, tile, matrix)
         part = 2.0 * total + kondo(
             probe.astype(jnp.float32), cos_ref[pl.ds(tile, 1), :], sin_ref[pl.ds(tile, 1), :]
         )
-        (part_outer, part_inner)[row][col] = part
-        if row == 0:
-            send_ref[place, :] = part.astype(jnp.bfloat16)
-        else:
-            pair_ref[place, :] = probe
-            pair_ref[pl.ds((cols + col) * rows, rows), :] = part.astype(jnp.bfloat16)
-    for tile in range(tiles):
+        part_ref[col] = part
+        pair_ref[place, :] = probe
+        pair_ref[pl.ds(tile * rows, rows), :] = part.astype(jnp.bfloat16)
+    for tile in range(2 * cols):
         matrix(RIM, tile)
 
 
@@ -482,18 +503,24 @@
     probe_rows = [outer, inner]
     got_0 = exchange_outer(outer)
 
-    (sorted_hop, part_outer, part_inner, send, send_pair, weights, twice_cos, twice_sin,
-     same_factor, cross_factor) = call(
+    raw = hopping.reshape(-1, width, width)
+    sorted_like = ((4 * tiles, width, width), bf16)
+    sorted_hop, part_outer, send, weights, twice_cos, twice_sin, same_factor, cross_factor = call(
         functools.partial(first_body, cols, rows, probe_total),
-        [((4 * tiles, width, width), bf16), row, row, side, pair, ((8, 128), f32)]
-        + [row_like] * 4,
+        [sorted_like, row, side, ((8, 128), f32)] + [row_like] * 4,
         [IN_SMEM] * 3 + [IN_VMEM] * 5,
         (parity, held(offsets_held, pltpu.SMEM), held(coef_held, pltpu.SMEM),
-         *(held(x) for x in (hopping.reshape(-1, width, width), angles_held, coupling_held,
-                             outer, inner))),
+         *(held(x) for x in (raw, angles_held, coupling_held, outer, inner))),
         flops=local_flops, moved=hopping.size * 2,
     )
     got_1 = exchange_outer(send)
+    sorted_hop, part_inner, send_pair = call(
+        functools.partial(first_rest_body, cols, rows), [sorted_like, row, pair],
+        [IN_SMEM] * 2 + [IN_VMEM] * 6,
+        (parity, held(offsets_held, pltpu.SMEM),
+         *(held(x) for x in (raw, outer, inner, twice_cos, twice_sin, sorted_hop))),
+        flops=local_flops,
+    )
     from_inner = exchange_inner(send_pair)
     trig = [twice_cos, twice_sin]
 

time: 71.5 us -> 70.9 us (level)
    pallas_call x9 -> x10, Pallas kernels: 6.5 us -> 6.49 us  [call(): pl.pallas_call(body, out_shape=[pltpu.VMEM(shape, dtype) for shape, dtype...]
where the time goes in v11:
time: 70.9 us; the launch traced here: 70.4 us
  starting transfers between devices  30.4 us (43%)
  blocking collectives  28.1 us (40%)
  Pallas kernels  8.49 us (12%)
  waiting for transfers between devices  2.63 us (4%)
  between operations  0.83 us (1%)
    ppermute x3, starting transfers between devices, exchange_inner(): lax.ppermute(inner, 'site', [(i, i ^ 1) for i in range(lax.axis_size('sit...  21.5 us
    all_to_all x1, blocking collectives, local(): lax.all_to_all(largest, ('site', 'probe'), 0, 0, axis_index_groups=near)  17.3 us
    all_to_all x1, blocking collectives, local(): lax.all_to_all(shares, ('site', 'probe'), 0, 0, axis_index_groups=chips)  10.8 us
    ppermute x3, starting transfers between devices, exchange_outer(): return lax.ppermute(outer, 'site', pairs)  8.91 us
    pallas_call x10, Pallas kernels, call(): pl.pallas_call(body, out_shape=[pltpu.VMEM(shape, dtype) for shape, dtype...  6.49 us
    ppermute x3, waiting for transfers between devices, exchange_inner(): lax.ppermute(inner, 'site', [(i, i ^ 1) for i in range(lax.axis_size('sit...  2.62 us
  transfers between devices with their start and end apart: 6, of which 2 were waited for; matrix products, arithmetic and copies ran while one was open for 0% of the time, Pallas kernels for 7%

profile of v11, /device:TPU:1, one launch (start us, length us, event | category | flops | bytes accessed | tf_op | source)
XLA Modules:
  0.0 70.4 jit_solution(11733018645658515015)
XLA Ops:
  0.6 0.0 copy-start
  0.7 1.3 %shard_map.86 = (bf16[512,256]{1,0:T(8,128)(2,1)S(1)}, bf16[512,256]{1,0:T(8,128)(2,1)S(1)}, s32[2,4,4]{2,1,0:T(4,128)S(4)}, f32[5]{0:T(128)S(4)}, f32[2,4,256]{2,1,0:T(4,128)S(1)}, /*index=5*/f32[2,4,256]{2,1,0:T(4,128)S(1)}) custom-call(s32[1]{0:T(128)} %bitcast.parity_ref, bf16[2,512,256]{2,1,0:T(8,128)(2,1)} %bitcast.5, s32[2,4,4]{2,1,0:T(4,128)} %offsets_hbm.1, ...), custom_call_target="tpu_custom_call" | custom-call | flops 8053063680 | tf_op jit(solution)/shard_map/pallas_call | solution.py:488
  1.9 5.1 %collective-permute-start.2 = (bf16[512,256]{1,0:T(8,128)(2,1)S(1)}, bf16[512,256]{1,0:T(8,128)(2,1)S(1)}, u32[]{:S(2)}, u32[]{:S(2)}) collective-permute-start(bf16[512,256]{1,0:T(8,128)(2,1)S(1)} %get-tuple-element.44.outer_ref.probe_outer), channel_id=1, source_target_pairs={{0,504},{8,16},{16,8},{24,32},{32,24},{40,48},{48,40},{56,64},{64,... | collective-permute-start | bytes 786440 | tf_op jit(solution)/shard_map/ppermute | solution.py:459
  7.0 0.0 copy-done
  7.0 0.5 shard_map.87
  7.5 1.9 %collective-permute-start = (bf16[512,256]{1,0:T(8,128)(2,1)S(1)}, bf16[512,256]{1,0:T(8,128)(2,1)S(1)}, u32[]{:S(2)}, u32[]{:S(2)}) collective-permute-start(bf16[512,256]{1,0:T(8,128)(2,1)S(1)} %get-tuple-element.50), channel_id=1, source_target_pairs={{0,504},{8,16},{16,8},{24,32},{32,24},{40,48},{48,40},{56,64},{64,... | collective-permute-start | bytes 786440 | tf_op jit(solution)/shard_map/ppermute | solution.py:459
  9.4 0.6 shard_map.88
  10.0 11.9 %collective-permute-start.1 = (bf16[1024,256]{1,0:T(8,128)(2,1)S(1)}, bf16[1024,256]{1,0:T(8,128)(2,1)S(1)}, u32[]{:S(2)}, u32[]{:S(2)}) collective-permute-start(bf16[1024,256]{1,0:T(8,128)(2,1)S(1)} %get-tuple-element.54), channel_id=1, source_target_pairs={{0,8},{8,0},{16,24},{24,16},{32,40},{40,32},{48,56},{56,48},{64,72... | collective-permute-start | bytes 1572872 | tf_op jit(solution)/shard_map/ppermute | solution.py:463
  21.9 0.0 collective-permute-done.2.got_ref.rim_probe
  21.9 0.4 shard_map.89
  22.3 1.1 %collective-permute-done.1.got_ref = bf16[1024,256]{1,0:T(8,128)(2,1)S(1)} collective-permute-done((bf16[1024,256]{1,0:T(8,128)(2,1)S(1)}, bf16[1024,256]{1,0:T(8,128)(2,1)S(1)}, u32[]{:S(2)}, u32[]{:S(2)}) %collective-permute-start.1) | collective-permute-done | bytes 524320 | tf_op jit(solution)/shard_map/ppermute | solution.py:463
  23.4 1.1 %shard_map.90 = (f32[4,128,256]{2,1,0:T(8,128)S(1)}, bf16[512,256]{1,0:T(8,128)(2,1)S(1)}, f32[4,128,256]{2,1,0:T(8,128)S(1)}, f32[4,128,256]{2,1,0:T(8,128)S(1)...) custom-call(bf16[512,256]{1,0:T(8,128)(2,1)S(1)} %get-tuple-element.44.outer_ref.probe_o, ...), custom_call_target="tpu_custom_call" | custom-call | flops 402653184 | tf_op jit(solution)/shard_map/pallas_call | solution.py:24
  24.6 0.5 shard_map.91
  25.1 0.0 collective-permute-done.got_ref
  25.2 0.7 shard_map.92
  25.8 1.9 %collective-permute-start.3 = (bf16[528,256]{1,0:T(8,128)(2,1)S(1)}, bf16[528,256]{1,0:T(8,128)(2,1)S(1)}, u32[]{:S(2)}, u32[]{:S(2)}) collective-permute-start(bf16[528,256]{1,0:T(8,128)(2,1)S(1)} %get-tuple-element.67), channel_id=1, source_target_pairs={{0,504},{8,16},{16,8},{24,32},{32,24},{40,48},{48,40},{56,64},{64,... | collective-permute-start | bytes 811016 | tf_op jit(solution)/shard_map/ppermute | solution.py:459
  27.8 7.6 %collective-permute-start.4 = (bf16[512,256]{1,0:T(8,128)(2,1)S(1)}, bf16[512,256]{1,0:T(8,128)(2,1)S(1)}, u32[]{:S(2)}, u32[]{:S(2)}) collective-permute-start(bf16[512,256]{1,0:T(8,128)(2,1)S(1)} %get-tuple-element.68), channel_id=1, source_target_pairs={{0,8},{8,0},{16,24},{24,16},{32,40},{40,32},{48,56},{56,48},{64,72... | collective-permute-start | bytes 786440 | tf_op jit(solution)/shard_map/ppermute | solution.py:463
  35.4 0.6 shard_map.93
  36.0 1.9 %collective-permute-start.5 = (bf16[512,256]{1,0:T(8,128)(2,1)S(1)}, bf16[512,256]{1,0:T(8,128)(2,1)S(1)}, u32[]{:S(2)}, u32[]{:S(2)}) collective-permute-start(bf16[512,256]{1,0:T(8,128)(2,1)S(1)} %get-tuple-element.75), channel_id=1, source_target_pairs={{0,8},{8,0},{16,24},{24,16},{32,40},{40,32},{48,56},{56,48},{64,72... | collective-permute-start | bytes 786440 | tf_op jit(solution)/shard_map/ppermute | solution.py:463
  38.0 0.0 collective-permute-done.4.got_2
  38.0 1.5 %collective-permute-done.5.got_3 = bf16[512,256]{1,0:T(8,128)(2,1)S(1)} collective-permute-done((bf16[512,256]{1,0:T(8,128)(2,1)S(1)}, bf16[512,256]{1,0:T(8,128)(2,1)S(1)}, u32[]{:S(2)}, u32[]{:S(2)}) %collective-permute-start.5) | collective-permute-done | bytes 262176 | tf_op jit(solution)/shard_map/ppermute | solution.py:463
  39.5 1.2 %shard_map.94 = (f32[16,8,256]{2,1,0:T(8,128)S(1)}, f32[4,128,256]{2,1,0:T(8,128)S(1)}) custom-call(bf16[512,256]{1,0:T(8,128)(2,1)S(1)} %get-tuple-element.44.outer_ref.probe_outer, bf16[512,256]{1,0:T(8,128)(2,1)S(1)} %get-tuple-element.45.inner_ref.probe_inner, bf16[512,256]{1,0:T(8,128)(2,1)S(1)} %collective-permute-done.4.got_2, ...), custom_call_target="tpu_custom_call" | custom-call | tf_op jit(solution)/shard_map/pallas_call | solution.py:24
  40.7 0.0 copy-start.1
  40.7 0.0 copy-start.2
  40.7 0.0 collective-permute-done.3.got_ref
  40.7 0.8 %shard_map.95 = f32[16,8,256]{2,1,0:T(8,128)S(1)} custom-call(bf16[512,256]{1,0:T(8,128)(2,1)S(1)} %get-tuple-element.44.outer_ref.probe_outer, bf16[512,256]{1,0:T(8,128)(2,1)S(1)} %get-tuple-element.45.inner_ref.probe_inner, bf16[528,256]{1,0:T(8,128)(2,1)S(1)} %collective-permute-done.3.got_ref, f32[4,128,256]{2,1,0:T(8,128)S(1)} %get-tuple-element.79.halo_2_ref, ...), custom_call_target="tpu_custom_call" | custom-call | flops 402653184 | tf_op jit(solution)/shard_map/pallas_call | solution.py:24
  41.5 10.8 %all_to_all.10.shares_ref = f32[16,8,256]{2,1,0:T(8,128)S(1)} all-to-all(f32[16,8,256]{2,1,0:T(8,128)S(1)} %shard_map.95), channel_id=1, replica_groups={{0,1,2,3,4,5,6,7,8,9,10,11,12,13,14,15},{16,17,18,19,20,21,22,23,24,25,..., dimensions={0} | all-to-all | bytes 262144 | tf_op jit(solution)/shard_map/all_to_all | solution.py:568
  52.2 0.1 shard_map.96
  52.4 17.3 %all_to_all.11.largest_ref = f32[32,1,128]{2,1,0:T(1,128)S(1)} all-to-all(f32[32,1,128]{2,1,0:T(1,128)S(1)} %get-tuple-element.84), channel_id=1, replica_groups={{0,16,32,48,64,80,96,112,128,144,160,176,192,208,224,240,260,276,292,30..., dimensions={0} | all-to-all | bytes 32768 | tf_op jit(solution)/shard_map/all_to_all | solution.py:578
  69.7 0.0 copy-done.1
  69.7 0.0 copy-done.2
  69.7 0.7 %shard_map.97 = (f32[2,4,256]{2,1,0:T(4,128)}, f32[2,4,256]{2,1,0:T(4,128)}) custom-call(s32[1]{0:T(128)} %bitcast.parity_ref, f32[32,1,128]{2,1,0:T(1,128)S(1)} %all_to_all.11.largest_ref, f32[8,256]{1,0:T(8,128)S(1)} %get-tuple-element.85.force_ref, f32[2,4,256]{2,1,0:T(4,128)S(1)} %copy-done.1, f32[2,4,256]{2,1,0:T(4,128)S(1)} %copy-done.2), custom_call_target="tpu_custom_call" | custom-call | tf_op jit(solution)/shard_map/pallas_call | solution.py:579
Async XLA Ops:
  0.6 6.3 %copy-start = (bf16[2,4,4,256,256]{4,3,2,1,0:T(8,128)(2,1)S(1)}, bf16[2,4,4,256,256]{4,3,2,1,0:T(8,128)(2,1)}, u32[]{:S(2)}) copy-start(bf16[2,4,4,256,256]{4,3,2,1,0:T(8,128)(2,1)} %param.12) | copy-start | bytes 12582916
  1.9 20.0 %collective-permute-start.2 = (bf16[512,256]{1,0:T(8,128)(2,1)S(1)}, bf16[512,256]{1,0:T(8,128)(2,1)S(1)}, u32[]{:S(2)}, u32[]{:S(2)}) collective-permute-start(bf16[512,256]{1,0:T(8,128)(2,1)S(1)} %get-tuple-element.44.outer_ref.probe_outer), channel_id=1, source_target_pairs={{0,504},{8,16},{16,8},{24,32},{32,24},{40,48},{48,40},{56,64},{64,... | collective-permute-start | bytes 786440 | tf_op jit(solution)/shard_map/ppermute | solution.py:459
  7.5 17.7 %collective-permute-start = (bf16[512,256]{1,0:T(8,128)(2,1)S(1)}, bf16[512,256]{1,0:T(8,128)(2,1)S(1)}, u32[]{:S(2)}, u32[]{:S(2)}) collective-permute-start(bf16[512,256]{1,0:T(8,128)(2,1)S(1)} %get-tuple-element.50), channel_id=1, source_target_pairs={{0,504},{8,16},{16,8},{24,32},{32,24},{40,48},{48,40},{56,64},{64,... | collective-permute-start | bytes 786440 | tf_op jit(solution)/shard_map/ppermute | solution.py:459
  10.0 13.5 %collective-permute-start.1 = (bf16[1024,256]{1,0:T(8,128)(2,1)S(1)}, bf16[1024,256]{1,0:T(8,128)(2,1)S(1)}, u32[]{:S(2)}, u32[]{:S(2)}) collective-permute-start(bf16[1024,256]{1,0:T(8,128)(2,1)S(1)} %get-tuple-element.54), channel_id=1, source_target_pairs={{0,8},{8,0},{16,24},{24,16},{32,40},{40,32},{48,56},{56,48},{64,72... | collective-permute-start | bytes 1572872 | tf_op jit(solution)/shard_map/ppermute | solution.py:463
  25.8 14.9 %collective-permute-start.3 = (bf16[528,256]{1,0:T(8,128)(2,1)S(1)}, bf16[528,256]{1,0:T(8,128)(2,1)S(1)}, u32[]{:S(2)}, u32[]{:S(2)}) collective-permute-start(bf16[528,256]{1,0:T(8,128)(2,1)S(1)} %get-tuple-element.67), channel_id=1, source_target_pairs={{0,504},{8,16},{16,8},{24,32},{32,24},{40,48},{48,40},{56,64},{64,... | collective-permute-start | bytes 811016 | tf_op jit(solution)/shard_map/ppermute | solution.py:459
  27.8 10.2 %collective-permute-start.4 = (bf16[512,256]{1,0:T(8,128)(2,1)S(1)}, bf16[512,256]{1,0:T(8,128)(2,1)S(1)}, u32[]{:S(2)}, u32[]{:S(2)}) collective-permute-start(bf16[512,256]{1,0:T(8,128)(2,1)S(1)} %get-tuple-element.68), channel_id=1, source_target_pairs={{0,8},{8,0},{16,24},{24,16},{32,40},{40,32},{48,56},{56,48},{64,72... | collective-permute-start | bytes 786440 | tf_op jit(solution)/shard_map/ppermute | solution.py:463
  36.0 3.4 %collective-permute-start.5 = (bf16[512,256]{1,0:T(8,128)(2,1)S(1)}, bf16[512,256]{1,0:T(8,128)(2,1)S(1)}, u32[]{:S(2)}, u32[]{:S(2)}) collective-permute-start(bf16[512,256]{1,0:T(8,128)(2,1)S(1)} %get-tuple-element.75), channel_id=1, source_target_pairs={{0,8},{8,0},{16,24},{24,16},{32,40},{40,32},{48,56},{56,48},{64,72... | collective-permute-start | bytes 786440 | tf_op jit(solution)/shard_map/ppermute | solution.py:463
  40.7 29.0 %copy-start.1 = (f32[2,4,256]{2,1,0:T(4,128)S(1)}, f32[2,4,256]{2,1,0:T(4,128)}, u32[]{:S(2)}) copy-start(f32[2,4,256]{2,1,0:T(4,128)} %angles_ref.1) | copy-start | bytes 24580
  40.7 29.0 %copy-start.2 = (f32[2,4,256]{2,1,0:T(4,128)S(1)}, f32[2,4,256]{2,1,0:T(4,128)}, u32[]{:S(2)}) copy-start(f32[2,4,256]{2,1,0:T(4,128)} %noise_ref.1) | copy-start | bytes 24580
